TPU v7x, 32 devices: a whole 2x2x4 slice. The times are simulated.
32 devices in a mesh: level: 2 (over core), blk: 16 (over z, y, x).
Axes of the slice: x: 2, y: 2, z: 4, core: 2. Of those that a mesh axis runs over, the one named last changes fastest.
Arguments:
- fluid_state: float32 [2, 256, 5, 16, 256], P('level', 'blk'), may hold values from -0.5 to 4, as said below
- neighbours: int32 [256, 6], replicated, may hold values from 0 to 255, as said below
- parents: int32 [256, 2], replicated, may hold values from 0 to 255, as said below
Outputs:
- updated: float32 [2, 256, 5, 16, 256], P('level', 'blk')
Inputs may be any that keep to these rules, and one draw needn't show every extreme that they name: Row b lists the coarse blocks beyond block b's low and high face along x, then y, then z; the relation is symmetric (the block beyond b's high face along an axis has b beyond its low face along it); block g is held by blk index g // 16, never by the same device as its neighbours; among the (block, face) pairs of one device at most 12 have their neighbour on any one other device, and some pairs of devices reach 12; no block beside a parent is a parent. `parents`: row g gives the coarse parent of refined block g and g's octant in it (4 x half + 2 y half + z half); the parent is held by the same blk index as g; every parent has one child of each octant, so each device's refined blocks are the children of 2 of its coarse blocks. `fluid_state`: components are density, x, y, z momentum and total energy of states with density 0.6 to 1.6, velocity components -0.3 to 0.3 and pressure 0.7 to 1.4, gamma 1.4.
All inputs are finite; a program needn't handle non-finite values.
Results may differ from a plain program's by a relative error of at most 0.0003.
Values sent between devices are 32-bit elements; how exact they have to be, the bound alone decides.
No kernel may reach another device: no remote copies, remote signals or barrier semaphores. Data moves between devices by JAX's collectives and lax.ppermute only.
A program may use at most 192 MiB of HBM per device.

v0:
```python
import math

import jax
import jax.numpy as jnp
from jax import lax
from jax.sharding import PartitionSpec as P

GAS_GAMMA = 1.4
STEP_RATIO = 0.12
OPPOSITE = (1, 0, 3, 2, 5, 4)
FACE_SIGNS = (-1.0, 1.0, -1.0, 1.0, -1.0, 1.0)
BIT_OF = (4, 2, 1)
TANGENT = ((2, 1), (4, 1), (4, 2))


def shifted(array, axis, by):
    devices = lax.axis_size(axis)
    pairs = [(i, i + by) for i in range(devices) if 0 <= i + by < devices]
    return lax.ppermute(array, axis, pairs)


def primitive(state_vec):
    density = state_vec[0]
    velocity = state_vec[1:4] / density
    pressure = (GAS_GAMMA - 1.0) * (state_vec[4] - 0.5 * jnp.sum(state_vec[1:4] * velocity, axis=0))
    return (density, velocity, pressure)


def physical_flux(state_vec, normal, density, velocity, pressure):
    normal_speed = velocity[normal]
    pieces = [state_vec[component] * normal_speed for component in range(4)]
    pieces.append((state_vec[4] + pressure) * normal_speed)
    pieces[1 + normal] = pieces[1 + normal] + pressure
    return jnp.stack(pieces)


def contact_flux(low_state, high_state, normal):
    density_low, velocity_low, pressure_low = primitive(low_state)
    density_high, velocity_high, pressure_high = primitive(high_state)
    sound_low = jnp.sqrt(GAS_GAMMA * pressure_low / density_low)
    sound_high = jnp.sqrt(GAS_GAMMA * pressure_high / density_high)
    speed_low = velocity_low[normal]
    speed_high = velocity_high[normal]
    slowest = jnp.minimum(speed_low - sound_low, speed_high - sound_high)
    fastest = jnp.maximum(speed_low + sound_low, speed_high + sound_high)
    mass_low = density_low * (slowest - speed_low)
    mass_high = density_high * (fastest - speed_high)
    contact = (pressure_high - pressure_low + speed_low * mass_low - speed_high * mass_high) / (
        mass_low - mass_high
    )
    flux_low = physical_flux(low_state, normal, density_low, velocity_low, pressure_low)
    flux_high = physical_flux(high_state, normal, density_high, velocity_high, pressure_high)

    def star_flux(state_vec, density, velocity, pressure, mass_flow, wave_speed, flux_here):
        factor = mass_flow / (wave_speed - contact)
        momenta = [factor * velocity[component] for component in range(3)]
        momenta[normal] = factor * contact
        energy = factor * (
            state_vec[4] / density + (contact - velocity[normal]) * (contact + pressure / mass_flow)
        )
        star_state = jnp.stack([factor] + momenta + [energy])
        return flux_here + wave_speed * (star_state - state_vec)

    star_low = star_flux(
        low_state, density_low, velocity_low, pressure_low, mass_low, slowest, flux_low
    )
    star_high = star_flux(
        high_state, density_high, velocity_high, pressure_high, mass_high, fastest, flux_high
    )
    return jnp.where(
        slowest >= 0.0,
        flux_low,
        jnp.where(contact >= 0.0, star_low, jnp.where(fastest > 0.0, star_high, flux_high)),
    )


def face_fluxes(padded, normal):
    step_below = padded[:, :, 1:-1] - padded[:, :, :-2]
    step_above = padded[:, :, 2:] - padded[:, :, 1:-1]
    limited = jnp.where(
        step_below * step_above > 0.0,
        jnp.sign(step_below) * jnp.minimum(jnp.abs(step_below), jnp.abs(step_above)),
        0.0,
    )
    centre = padded[:, :, 1:-1]
    low_face = centre - 0.5 * limited
    high_face = centre + 0.5 * limited
    change = (
        0.5
        * STEP_RATIO
        * (
            physical_flux(low_face, normal, *primitive(low_face))
            - physical_flux(high_face, normal, *primitive(high_face))
        )
    )
    low_face = low_face + change
    high_face = high_face + change
    return contact_flux(high_face[:, :, :-1], low_face[:, :, 1:], normal)


def oriented(block_cells, direction):
    leading = block_cells.shape[:2]
    edge_cells = block_cells.shape[2]
    cube_cells = block_cells.reshape(leading + (edge_cells, edge_cells, edge_cells))
    if direction == 1:
        cube_cells = cube_cells.transpose(0, 1, 3, 2, 4)
    elif direction == 2:
        cube_cells = cube_cells.transpose(0, 1, 4, 2, 3)
    return cube_cells.reshape(leading + (edge_cells, edge_cells * edge_cells))


def restored(block_cells, direction):
    leading = block_cells.shape[:2]
    edge_cells = block_cells.shape[2]
    cube_cells = block_cells.reshape(leading + (edge_cells, edge_cells, edge_cells))
    if direction == 1:
        cube_cells = cube_cells.transpose(0, 1, 3, 2, 4)
    elif direction == 2:
        cube_cells = cube_cells.transpose(0, 1, 3, 4, 2)
    return cube_cells.reshape(leading + (edge_cells, edge_cells * edge_cells))


def advance(block_cells, ghosts):
    divergence = jnp.zeros_like(block_cells)
    boundary = []
    for direction in range(3):
        padded = jnp.concatenate(
            [ghosts[2 * direction], oriented(block_cells, direction), ghosts[2 * direction + 1]],
            axis=2,
        )
        fluxes = face_fluxes(padded, direction)
        divergence = divergence + restored(fluxes[:, :, 1:] - fluxes[:, :, :-1], direction)
        boundary.append(fluxes[:, :, 0])
        boundary.append(fluxes[:, :, -1])
    return (block_cells - STEP_RATIO * divergence, jnp.stack(boundary))


def face_slabs(block_cells, layers):
    edge_cells = block_cells.shape[2]
    pieces = []
    for direction in range(3):
        view_cells = oriented(block_cells, direction)
        pieces.append(view_cells[:, :, :layers])
        pieces.append(view_cells[:, :, edge_cells - layers :])
    return jnp.stack(pieces).transpose(2, 0, 1, 3, 4)


def inner_rim(ghost_slabs):
    return jnp.stack([ghost_slabs[:, face_id, :, 1 - face_id % 2] for face_id in range(6)], axis=1)


def flipped_octant(octants, mask_bit):
    return octants + mask_bit - 2 * mask_bit * (octants // mask_bit % 2)


def fine_ghosts(face_set, rims, octants, siblings):
    block_count = face_set.shape[0]
    edge_sq = face_set.shape[-1]
    half_edge = math.isqrt(edge_sq) // 2
    row_ids = jnp.arange(block_count)
    result = []
    for face_id in range(6):
        direction = face_id // 2
        side_id = face_id % 2
        outward = octants // BIT_OF[direction] % 2 == side_id
        first_bit = octants // TANGENT[direction][0] % 2
        second_bit = octants // TANGENT[direction][1] % 2
        coarse_rim = rims[:, face_id].reshape(block_count, 5, 2, half_edge, 2, half_edge)
        quarter = coarse_rim[row_ids, :, first_bit, :, second_bit, :]
        widened = jnp.repeat(jnp.repeat(quarter, 2, axis=2), 2, axis=3).reshape(
            block_count, 5, 1, edge_sq
        )
        from_coarse = jnp.concatenate([widened, widened], axis=2)
        from_sibling = face_set[siblings[:, direction], OPPOSITE[face_id]]
        result.append(jnp.where(outward[:, None, None, None], from_coarse, from_sibling))
    return jnp.stack(result).transpose(0, 2, 1, 3, 4)


def restricted(block_cells, flux_total, octants):
    block_count = block_cells.shape[1]
    half_edge = block_cells.shape[2] // 2
    averages = (
        block_cells.reshape(5, block_count, half_edge, 2, half_edge, 2, half_edge, 2).sum(
            axis=(3, 5, 7)
        )
        * 0.125
    )
    averages = averages.transpose(1, 0, 2, 3, 4)
    quarters = []
    for direction in range(3):
        outward_high = octants // BIT_OF[direction] % 2 == 1
        chosen = jnp.where(
            outward_high[None, :, None], flux_total[2 * direction + 1], flux_total[2 * direction]
        )
        summed = chosen.reshape(5, block_count, half_edge, 2, half_edge, 2).sum(axis=(3, 5))
        quarters.append(summed.transpose(1, 0, 2, 3) * 0.125)
    return (averages, jnp.stack(quarters, axis=1))


def assemble(averages, quarters, children, coarse_faces):
    block_count = children.shape[0]
    half_edge = averages.shape[-1]
    edge_cells = 2 * half_edge
    picked = averages[children].reshape(block_count, 2, 2, 2, 5, half_edge, half_edge, half_edge)
    new_cells = picked.transpose(4, 0, 1, 5, 2, 6, 3, 7).reshape(
        5, block_count, edge_cells, edge_cells * edge_cells
    )
    deltas = []
    for face_id in range(6):
        direction = face_id // 2
        side_id = face_id % 2
        octant_list = []
        for first_bit in (0, 1):
            for second_bit in (0, 1):
                octant_list.append(
                    side_id * BIT_OF[direction]
                    + first_bit * TANGENT[direction][0]
                    + second_bit * TANGENT[direction][1]
                )
        chosen = quarters[children[:, jnp.array(octant_list, jnp.int32)]][:, :, direction]
        fine_face = (
            chosen.reshape(block_count, 2, 2, 5, half_edge, half_edge)
            .transpose(0, 3, 1, 4, 2, 5)
            .reshape(block_count, 5, edge_cells * edge_cells)
        )
        deltas.append(coarse_faces[face_id].transpose(1, 0, 2) - fine_face)
    return (new_cells, jnp.stack(deltas, axis=1))


def apply_corrections(block_cells, corrections):
    edge_cells = block_cells.shape[2]
    for direction in range(3):
        view_cells = oriented(block_cells, direction)
        view_cells = view_cells.at[:, :, 0].add(corrections[:, 2 * direction].transpose(1, 0, 2))
        view_cells = view_cells.at[:, :, edge_cells - 1].add(
            corrections[:, 2 * direction + 1].transpose(1, 0, 2)
        )
        block_cells = restored(view_cells, direction)
    return block_cells


def local(fluid_state, neighbours, parents):
    level_id = lax.axis_index("level")
    blk_index = lax.axis_index("blk")
    device_count = lax.axis_size("blk")
    block_cells = fluid_state[0].transpose(1, 0, 2, 3)
    block_count = block_cells.shape[1]
    edge_cells = block_cells.shape[2]
    capacity = 2 * ((6 * block_count + device_count - 1) // device_count)
    own_rows = lax.dynamic_slice_in_dim(
        neighbours, blk_index * block_count, block_count, 0
    ).reshape(-1)
    item_ids = jnp.arange(6 * block_count, dtype=jnp.int32)
    targets = own_rows // block_count
    send_rank = jnp.sum(
        (targets[:, None] == targets[None, :]) & (item_ids[None, :] < item_ids[:, None]), axis=1
    )
    face_ids = item_ids % 6
    wanted = own_rows % block_count * 6 + face_ids + 1 - 2 * (face_ids % 2)
    their_rows = (
        neighbours.reshape(-1)[(targets * 6 * block_count)[:, None] + item_ids[None, :]]
        // block_count
    )
    recv_rank = jnp.sum((their_rows == blk_index) & (item_ids[None, :] < wanted[:, None]), axis=1)

    def spread(payload):
        return (
            jnp.zeros((device_count, capacity) + payload.shape[1:], payload.dtype)
            .at[targets, send_rank]
            .set(payload)
        )

    def collect(received):
        return received[targets, recv_rank]

    def route(buffer):
        return lax.all_to_all(buffer, "blk", split_axis=0, concat_axis=0, tiled=True)

    parent_rows = lax.dynamic_slice_in_dim(parents, blk_index * block_count, block_count, 0)
    parent_local = parent_rows[:, 0] - blk_index * block_count
    octants = parent_rows[:, 1]
    parents_here = block_count // 8
    refined = jnp.zeros((block_count,), jnp.int32).at[parent_local].set(1)
    packed_slot = jnp.cumsum(refined) - 1
    target_slot = jnp.where(refined > 0, packed_slot, parents_here)
    rim_source = packed_slot[parent_local]
    children = (
        jnp.zeros((block_count, 8), jnp.int32)
        .at[parent_local, octants]
        .set(jnp.arange(block_count, dtype=jnp.int32))
    )
    siblings = jnp.stack(
        [
            children[parent_local, flipped_octant(octants, BIT_OF[direction])]
            for direction in range(3)
        ],
        axis=1,
    )

    def lend_rims(all_rims):
        packed = (
            jnp.zeros((parents_here,) + all_rims.shape[1:], all_rims.dtype)
            .at[target_slot]
            .set(all_rims, mode="drop")
        )
        lent_rims = shifted(packed, "level", 1)
        return lent_rims[rim_source]

    face_set = face_slabs(block_cells, 2)
    received = route(spread(face_set.reshape(6 * block_count, 5, 2, -1)))
    early_ghosts = collect(received).reshape(block_count, 6, 5, 2, -1)
    early_rims = lend_rims(inner_rim(early_ghosts))
    fine_early = fine_ghosts(face_set, early_rims, octants, siblings)
    first_ghosts = jnp.where(level_id == 0, early_ghosts.transpose(1, 2, 0, 3, 4), fine_early)
    cells_half, first_faces = advance(block_cells, first_ghosts)
    late_slabs = face_slabs(cells_half, 2)
    outer_set = face_slabs(cells_half, 1)
    received = route(spread(outer_set.reshape(6 * block_count, 5, 1, -1)))
    late_all = collect(received).reshape(block_count, 6, 5, -1)
    late_rims = lend_rims(late_all)
    later_ghosts = fine_ghosts(late_slabs, 0.5 * (early_rims + late_rims), octants, siblings)
    cells_out, second_faces = lax.cond(
        level_id == 1,
        lambda: advance(cells_half, later_ghosts),
        lambda: (cells_half, jnp.zeros_like(first_faces)),
    )
    flux_total = first_faces + second_faces
    half_edge = edge_cells // 2
    averages, quarters = restricted(cells_out, flux_total, octants)
    bundle = jnp.concatenate(
        [averages.reshape(block_count, -1), quarters.reshape(block_count, -1)], axis=1
    )
    moved = shifted(bundle, "level", -1)
    split_at = 5 * half_edge**3
    averages = moved[:, :split_at].reshape(block_count, 5, half_edge, half_edge, half_edge)
    quarters = moved[:, split_at:].reshape(block_count, 3, 5, half_edge, half_edge)
    parent_cells, deltas = assemble(averages, quarters, children, first_faces)
    refined_mask = refined.astype(jnp.float32)
    coarse_mixed = jnp.where(refined_mask[None, :, None, None] > 0.0, parent_cells, cells_half)
    deltas = deltas * refined_mask[:, None, None, None]
    returned = collect(route(spread(deltas.reshape(6 * block_count, 5, -1))))
    corrections = (
        returned.reshape(block_count, 6, 5, -1)
        * jnp.array(FACE_SIGNS, jnp.float32)[None, :, None, None]
        * STEP_RATIO
    )
    coarse_out = apply_corrections(coarse_mixed, corrections)
    finished = jnp.where(level_id == 0, coarse_out, cells_out)
    return finished.transpose(1, 0, 2, 3)[None]


def solution(mesh):
    return jax.shard_map(
        local,
        mesh=mesh,
        in_specs=(P("level", "blk", None, None, None), P(), P()),
        out_specs=P("level", "blk", None, None, None),
        check_vma=False,
    )
```

profile of v0, /device:TPU:0, one launch (start us, length us, event | category | flops | bytes accessed | tf_op | source)
XLA Modules:
  0.0 822.1 jit_solution(16303029112712116674)
XLA Ops:
  9.9 13.8 %copy.2039 = f32[5,16,16,16,16]{4,2,1,3,0:T(8,128)} copy(f32[5,16,16,16,16]{4,3,1,0,2:T(8,128)} %reshape.1812) | data formatting | bytes 2621440 | tf_op jit(solution)/shard_map/reshape | solution.py:104
  23.8 12.7 %copy.1724 = f32[5,16,16,16,16]{3,2,1,4,0:T(8,128)} copy(f32[5,16,16,16,16]{4,3,1,0,2:T(8,128)} %reshape.1812) | data formatting | bytes 2621440 | tf_op jit(solution)/shard_map/reshape | solution.py:104
  36.9 51.2 %gather_fusion = s32[9216]{0:T(1024)S(1)} fusion(s32[1536]{0:T(1024)S(1)} %reshape.1816, s32[9216]{0:T(1024)S(1)} %broadcast_clamp_fusion), kind=kCustom, calls=%fused_computation | custom fusion | bytes 110592 | tf_op jit(solution)/shard_map/gather | solution.py:261
  98.6 8.3 %reshape.1814 = f32[5,16,16,256]{3,1,2,0:T(8,128)} reshape(f32[5,16,16,16,16]{4,3,1,2,0:T(8,128)} %bitcast.1390) | data formatting | bytes 2621440 | tf_op jit(solution)/shard_map/reshape | solution.py:109
  114.2 12.8 %scatter_fusion = f32[16,12,5,2,256]{4,3,2,1,0:T(2,128)} fusion(f32[16,12,5,2,256]{4,3,2,1,0:T(2,128)} %broadcast_in_dim.370, s32[96]{0:T(128)S(1)} %fusion.321, f32[96,5,2,256]{3,2,1,0:T(2,128)S(1)} %bitcast.1409), kind=kCustom, calls=%fused_computation.48 | custom fusion | bytes 2949888 | tf_op jit(solution)/shard_map/scatter | solution.py:270
  127.0 8.3 %all-to-all-start = ((f32[16,12,5,2,256]{4,3,2,1,0:T(2,128)}), f32[16,12,5,2,256]{4,3,2,1,0:T(2,128)}, u32[]{:S(2)}, u32[]{:S(2)}) async-start(f32[16,12,5,2,256]{4,3,2,1,0:T(2,128)} %scatter_fusion), calls=%async_computation | async-start | bytes 3932160 | tf_op jit(solution)/shard_map/all_to_all | solution.py:277
  156.6 19.6 %all-to-all-done = f32[16,12,5,2,256]{4,3,2,1,0:T(2,128)} async-done(((f32[16,12,5,2,256]{4,3,2,1,0:T(2,128)}), f32[16,12,5,2,256]{4,3,2,1,0:T(2,128)}, u32[]{:S(2)}, u32[]{:S(2)}) %all-to-all-start) | async-done | bytes 1966112 | tf_op jit(solution)/shard_map/all_to_all | solution.py:277
  258.1 12.4 %copy.1818 = f32[5,16,16,16,16]{4,3,1,0,2:T(8,128)} copy(f32[5,16,16,16,16]{3,2,1,4,0:T(8,128)} %bitcast.1394) | data formatting | bytes 2621440 | tf_op jit(solution)/shard_map/transpose | solution.py:119
  270.5 8.2 reshape.1828
  297.9 11.2 %copy.1815 = f32[5,16,16,16,16]{4,3,1,0,2:T(8,128)} copy(f32[5,16,16,16,16]{4,2,3,1,0:T(8,128)} %bitcast.1395) | data formatting | bytes 2621440 | tf_op jit(solution)/shard_map/transpose | solution.py:117
  309.1 8.2 reshape.1826
  335.4 14.1 %copy.2038 = f32[5,16,16,16,16]{4,2,1,0,3:T(8,128)} copy(f32[5,16,16,16,16]{4,3,1,0,2:T(8,128)} %reshape.1829) | data formatting | bytes 2621440 | tf_op jit(solution)/shard_map/reshape | solution.py:104
  349.5 12.7 %copy.1820 = f32[5,16,16,16,16]{3,2,1,0,4:T(8,128)} copy(f32[5,16,16,16,16]{4,3,1,0,2:T(8,128)} %reshape.1829) | data formatting | bytes 2621440 | tf_op jit(solution)/shard_map/reshape | solution.py:104
  392.1 9.6 %all-to-all-start.1 = ((f32[16,12,5,1,256]{4,3,2,1,0:T(1,128)}), f32[16,12,5,1,256]{4,3,2,1,0:T(1,128)S(1)}, u32[]{:S(2)}, u32[]{:S(2)}) async-start(f32[16,12,5,1,256]{4,3,2,1,0:T(1,128)} %copy.1823), calls=%async_computation.1 | async-start | bytes 1966080 | tf_op jit(solution)/shard_map/all_to_all | solution.py:277
  411.5 13.5 %all-to-all-done.1 = f32[16,12,5,1,256]{4,3,2,1,0:T(1,128)S(1)} async-done(((f32[16,12,5,1,256]{4,3,2,1,0:T(1,128)}), f32[16,12,5,1,256]{4,3,2,1,0:T(1,128)S(1)}, u32[]{:S(2)}, u32[]{:S(2)}) %all-to-all-start.1) | async-done | bytes 983072 | tf_op jit(solution)/shard_map/all_to_all | solution.py:277
  464.1 12.7 %conditional.1 = (f32[5,16,16,256]{3,2,1,0:T(8,128)}, f32[6,5,16,256]{3,2,1,0:T(8,128)}) conditional(s32[]{:T(128)} %convert_element_type.13, (f32[5,16,16,256]{3,1,0,2:T(8,128)S(1)}) %tuple.48, (f32[6,5,16,2,256]{4,2,3,1,0:T(8,128)S(1)}, f32[5,16,16,256]{3,1,0,2:T(8,128)S(1)}) %tuple.265), branch_computations={%region_21.22_spmd, %region_22.35_spmd} | conditional | flops 89956344 | bytes 339861696 | solution.py:322
  483.5 10.6 %reduce_sum.290 = f32[5,16,8,8,8]{1,4,3,2,0:T(8,128)S(1)} reduce(f32[5,16,8,2,8,2,8,2]{1,7,6,5,4,3,2,0:T(2,128)} %bitcast.1403, f32[]{:T(128)} %constant.552.clone.1), dimensions={3,5,7}, to_apply=%region_35.36 | reduce | flops 286720 | bytes 1474564 | tf_op jit(solution)/shard_map/reduce_sum | solution.py:183
  502.3 138.4 %collective-permute-done.2 = f32[16,3520]{1,0:T(8,128)S(1)} collective-permute-done((f32[16,3520]{1,0:T(8,128)S(1)}, f32[16,3520]{1,0:T(8,128)S(1)}, u32[]{:S(2)}, u32[]{:S(2)}) %collective-permute-start.2) | collective-permute-done | bytes 225312 | tf_op jit(solution)/shard_map/ppermute | solution.py:19
  685.5 8.4 %all-to-all-start.2 = ((f32[16,12,5,256]{3,1,2,0:T(8,128)}), f32[16,12,5,256]{3,1,2,0:T(8,128)}, u32[]{:S(2)}, u32[]{:S(2)}) async-start(f32[16,12,5,256]{3,1,2,0:T(8,128)} %copy.1922), calls=%async_computation.2 | async-start | bytes 2621440 | tf_op jit(solution)/shard_map/all_to_all | solution.py:277
  698.6 8.9 %gather_fusion.33 = f32[128,5,8,8,8]{4,3,2,1,0:T(8,128)} fusion(f32[16,5,8,8,8]{4,3,2,1,0:T(8,128)S(1)} %copy.1886, s32[1024]{0:T(1024)S(1)} %copy-done.67), kind=kCustom, calls=%fused_computation.33 | custom fusion | bytes 2621952 | tf_op jit(solution)/shard_map/gather | solution.py:204
  707.5 16.7 %copy.1887 = f32[5,16,2,8,2,8,2,8]{1,7,6,5,4,3,2,0:T(8,128)} copy(f32[5,16,2,8,2,8,2,8]{7,5,3,0,6,4,2,1:T(8,128)} %bitcast.1389) | data formatting | bytes 2621440 | tf_op jit(solution)/shard_map/transpose | solution.py:205
  745.0 13.9 %copy.1926 = f32[5,16,16,16,16]{4,3,1,0,2:T(8,128)} copy(f32[5,16,16,16,16]{4,2,1,0,3:T(8,128)} %bitcast.1399) | data formatting | bytes 2621440 | tf_op jit(solution)/shard_map/transpose | solution.py:106
  772.3 13.7 %copy.1927 = f32[5,16,16,16,16]{2,3,1,0,4:T(8,128)} copy(f32[5,16,16,16,16]{4,3,1,0,2:T(8,128)} %reshape.1859) | data formatting | bytes 2621440 | tf_op jit(solution)/shard_map/reshape | solution.py:115
  799.3 12.2 %copy.1928 = f32[5,16,16,16,16]{4,3,2,0,1:T(8,128)} copy(f32[5,16,16,16,16]{3,2,1,0,4:T(8,128)} %bitcast.1401) | data formatting | bytes 2621440 | tf_op jit(solution)/shard_map/transpose | solution.py:119
  (630 shorter events, 369.0 us)
Async XLA Ops:
  0.0 135.4 %copy-start = (s32[256,2]{0,1:T(2,128)S(1)}, s32[256,2]{0,1:T(2,128)}, u32[]{:S(2)}) copy-start(s32[256,2]{0,1:T(2,128)} %param.26) | copy-start | bytes 6148
  36.8 51.3 %copy-start.15 = (f32[1,16,5,16,256]{4,3,2,1,0:T(8,128)S(1)}, f32[1,16,5,16,256]{4,3,2,1,0:T(8,128)}, u32[]{:S(2)}) copy-start(f32[1,16,5,16,256]{4,3,2,1,0:T(8,128)} %param.24) | copy-start | bytes 3932164
  112.4 314.0 %copy-start.4 = (s32[96]{0:T(128)}, s32[96]{0:T(128)S(1)}, u32[]{:S(2)}) copy-start(s32[96]{0:T(128)S(1)} %get-tuple-element.252) | copy-start | bytes 1156
  112.4 270.2 %copy-start.6 = (s32[96]{0:T(128)}, s32[96]{0:T(128)S(1)}, u32[]{:S(2)}) copy-start(s32[96]{0:T(128)S(1)} %fusion.321) | copy-start | bytes 1156
  127.0 49.2 %all-to-all-start = ((f32[16,12,5,2,256]{4,3,2,1,0:T(2,128)}), f32[16,12,5,2,256]{4,3,2,1,0:T(2,128)}, u32[]{:S(2)}, u32[]{:S(2)}) async-start(f32[16,12,5,2,256]{4,3,2,1,0:T(2,128)} %scatter_fusion), calls=%async_computation | async-start | bytes 3932160 | tf_op jit(solution)/shard_map/all_to_all | solution.py:277
  136.5 18.9 %copy-start.84 = (s32[16]{0:T(128)}, s32[16]{0:T(128)S(1)}, u32[]{:S(2)}) copy-start(s32[16]{0:T(128)S(1)} %scatter_custom_fusion) | copy-start | bytes 196
  141.2 10.1 %copy-start.89 = (s32[4]{0:T(128)S(1)}, s32[4]{0:T(128)}, u32[]{:S(2)}) copy-start(s32[4]{0:T(128)} %constant.1158) | copy-start | bytes 52
  142.0 11.5 %copy-start.88 = (s32[4]{0:T(128)S(1)}, s32[4]{0:T(128)}, u32[]{:S(2)}) copy-start(s32[4]{0:T(128)} %constant.1159) | copy-start | bytes 52
  154.2 32.8 %copy-start.72 = (s32[1024]{0:T(1024)}, s32[1024]{0:T(1024)S(1)}, u32[]{:S(2)}) copy-start(s32[1024]{0:T(1024)S(1)} %pad_clamp_fusion.13) | copy-start | bytes 12292
  155.9 27.7 %copy-start.81 = (s32[16]{0:T(128)}, s32[16]{0:T(128)S(1)}, u32[]{:S(2)}) copy-start(s32[16]{0:T(128)S(1)} %get-tuple-element.418) | copy-start | bytes 196
  155.9 77.1 %copy-start.73 = (pred[16]{0:T(512)(128)(4,1)}, pred[16]{0:T(512)(128)(4,1)S(1)}, u32[]{:S(2)}) copy-start(pred[16]{0:T(512)(128)(4,1)S(1)} %get-tuple-element.246) | copy-start | bytes 52
  156.0 72.8 %copy-start.68 = (pred[16]{0:T(512)(128)(4,1)}, pred[16]{0:T(512)(128)(4,1)S(1)}, u32[]{:S(2)}) copy-start(pred[16]{0:T(512)(128)(4,1)S(1)} %get-tuple-element.413) | copy-start | bytes 52
  156.0 76.0 %copy-start.75 = (pred[16]{0:T(512)(128)(4,1)}, pred[16]{0:T(512)(128)(4,1)S(1)}, u32[]{:S(2)}) copy-start(pred[16]{0:T(512)(128)(4,1)S(1)} %get-tuple-element.419) | copy-start | bytes 52
  156.0 71.7 %copy-start.79 = (pred[16]{0:T(512)(128)(4,1)}, pred[16]{0:T(512)(128)(4,1)S(1)}, u32[]{:S(2)}) copy-start(pred[16]{0:T(512)(128)(4,1)S(1)} %get-tuple-element.427) | copy-start | bytes 52
  156.0 73.8 %copy-start.77 = (pred[16]{0:T(512)(128)(4,1)}, pred[16]{0:T(512)(128)(4,1)S(1)}, u32[]{:S(2)}) copy-start(pred[16]{0:T(512)(128)(4,1)S(1)} %get-tuple-element.428) | copy-start | bytes 52
  184.8 2.2 collective-permute-start
  329.1 135.0 %copy-start.2 = (f32[5,16,16,256]{3,1,0,2:T(8,128)}, f32[5,16,16,256]{3,1,0,2:T(8,128)S(1)}, u32[]{:S(2)}) copy-start(f32[5,16,16,256]{3,1,0,2:T(8,128)S(1)} %fusion.146) | copy-start | bytes 3932164
  392.1 32.9 %all-to-all-start.1 = ((f32[16,12,5,1,256]{4,3,2,1,0:T(1,128)}), f32[16,12,5,1,256]{4,3,2,1,0:T(1,128)S(1)}, u32[]{:S(2)}, u32[]{:S(2)}) async-start(f32[16,12,5,1,256]{4,3,2,1,0:T(1,128)} %copy.1823), calls=%async_computation.1 | async-start | bytes 1966080 | tf_op jit(solution)/shard_map/all_to_all | solution.py:277
  411.5 14.9 %copy-start.40 = (f32[6,5,16,2,256]{4,2,1,3,0:T(8,128)}, f32[6,5,16,2,256]{4,2,1,3,0:T(8,128)S(1)}, u32[]{:S(2)}) copy-start(f32[6,5,16,2,256]{4,2,1,3,0:T(8,128)S(1)} %constant_dynamic-update-slice_fusion.30) | copy-start | bytes 2949124
  430.2 12.5 %collective-permute-start.1 = (f32[2,6,5,256]{3,1,2,0:T(8,128)S(1)}, f32[2,6,5,256]{3,1,2,0:T(8,128)S(1)}, u32[]{:S(2)}, u32[]{:S(2)}) collective-permute-start(f32[2,6,5,256]{3,1,2,0:T(8,128)S(1)} %scatter_fusion.4), channel_id=1, source_target_pairs={{0,16},{1,17},{2,18},{3,19},{4,20},{5,21},{6,22},{7,23},{8,24},{9,... | collective-permute-start | bytes 184328 | tf_op jit(solution)/shard_map/ppermute | solution.py:19
  500.2 141.6 %copy-start.65 = (s32[1024]{0:T(1024)S(1)}, s32[1024]{0:T(1024)}, u32[]{:S(2)}) copy-start(s32[1024]{0:T(1024)} %pad_clamp_fusion.10) | copy-start | bytes 12292
  500.2 140.5 %collective-permute-start.2 = (f32[16,3520]{1,0:T(8,128)S(1)}, f32[16,3520]{1,0:T(8,128)S(1)}, u32[]{:S(2)}, u32[]{:S(2)}) collective-permute-start(f32[16,3520]{1,0:T(8,128)S(1)} %pad_maximum_fusion.13), channel_id=1, source_target_pairs={{16,0},{17,1},{18,2},{19,3},{20,4},{21,5},{22,6},{23,7},{24,8},{25... | collective-permute-start | bytes 675848 | tf_op jit(solution)/shard_map/ppermute | solution.py:19
  685.5 47.3 %all-to-all-start.2 = ((f32[16,12,5,256]{3,1,2,0:T(8,128)}), f32[16,12,5,256]{3,1,2,0:T(8,128)}, u32[]{:S(2)}, u32[]{:S(2)}) async-start(f32[16,12,5,256]{3,1,2,0:T(8,128)} %copy.1922), calls=%async_computation.2 | async-start | bytes 2621440 | tf_op jit(solution)/shard_map/all_to_all | solution.py:277
  811.5 10.0 %copy-start.1 = (s32[256,2]{0,1:T(2,128)S(1)}, s32[256,2]{0,1:T(2,128)}, u32[]{:S(2)}) copy-start(s32[256,2]{0,1:T(2,128)} %param.26) | copy-start | bytes 6148
  (69 other events, 180.5 us)
where the time goes:
time: 837 us; the launch traced here: 822 us
  local copies, waits for them, and re-layouts  538 us (64%)
  waiting for transfers between devices  172 us (21%)
  other arithmetic  68.6 us (8%)
  starting transfers between devices  30.7 us (4%)
  loops' own time  9.99 us (1%)
    ppermute x3, waiting for transfers between devices, shifted(): return lax.ppermute(array, axis, pairs)  138 us
    reshape x6, local copies, waits for them, and re-layouts, oriented(): block_cells.reshape(leading + (edge_cells, edge_cells, edge_cells))  65.6 us
    gather x2, local copies, waits for them, and re-layouts, local(): neighbours.reshape(-1)  51.2 us
    reshape x6, local copies, waits for them, and re-layouts, oriented(): return cube_cells.reshape(leading + (edge_cells, edge_cells * edge_cells))  45.8 us
    reshape x5, local copies, waits for them, and re-layouts, restored(): block_cells.reshape(leading + (edge_cells, edge_cells, edge_cells))  40 us
    all_to_all x3, waiting for transfers between devices, route(): lax.all_to_all(buffer, 'blk', split_axis=0, concat_axis=0, tiled=True)  33.1 us
    unnamed x198, local copies, waits for them, and re-layouts  28.1 us
    scatter x5, local copies, waits for them, and re-layouts, spread(): return jnp.zeros((device_count, capacity) + payload.shape[1:], payload.dt...  28.1 us
  transfers between devices with their start and end apart: 6, of which 4 were waited for; matrix products, arithmetic and copies ran while one was open for 10% of the time, Pallas kernels for 0%

commit v1 on v0

v1 whole, which is shorter than its diff:
```python
import functools

import jax
import jax.numpy as jnp
from jax import lax
from jax.experimental import pallas as pl
from jax.experimental.pallas import tpu as pltpu
from jax.sharding import PartitionSpec as P

GAS_GAMMA = 1.4
STEP_RATIO = 0.12
BIT_OF = (4, 2, 1)
TANGENT = ((2, 1), (4, 1), (4, 2))
F32 = jnp.float32
I32 = jnp.int32
VMEM_LIMIT = 48 * 1024 * 1024
LANES = 128
ROWS = 8


def iota(shape, dim):
    return lax.broadcasted_iota(I32, shape, dim)


def reciprocal(x):
    return pltpu.reciprocal(x, approx=True)


def exact_dot(a, b):
    return jnp.dot(a, b, precision=lax.Precision.HIGHEST, preferred_element_type=F32)


def exact_dot_nt(a, b):
    return lax.dot_general(
        a, b, (((1,), (1,)), ((), ())), precision=lax.Precision.HIGHEST, preferred_element_type=F32
    )


def physical_flux(s, n):
    inv = reciprocal(s[0])
    vn = s[n] * inv
    kinetic = s[1] * s[1] + s[2] * s[2] + s[3] * s[3]
    p = (GAS_GAMMA - 1.0) * (s[4] - 0.5 * (kinetic * inv))
    out = [s[n], s[1] * vn, s[2] * vn, s[3] * vn, (s[4] + p) * vn]
    out[n] = out[n] + p
    return out


def evolve(u, below, above, n):
    low = []
    high = []
    for c in range(5):
        d = jnp.maximum(jnp.minimum(below[c], above[c]), 0.0) + jnp.minimum(
            jnp.maximum(below[c], above[c]), 0.0
        )
        d = 0.5 * d
        low.append(u[c] - d)
        high.append(u[c] + d)
    fl = physical_flux(low, n)
    fh = physical_flux(high, n)
    for c in range(5):
        change = (0.5 * STEP_RATIO) * (fl[c] - fh[c])
        low[c] = low[c] + change
        high[c] = high[c] + change
    return low, high


def side_values(s, n):
    inv = reciprocal(s[0])
    vn = s[n] * inv
    kinetic = s[1] * s[1] + s[2] * s[2] + s[3] * s[3]
    p = (GAS_GAMMA - 1.0) * (s[4] - 0.5 * (kinetic * inv))
    square = GAS_GAMMA * p * inv
    sound = square * lax.rsqrt(square)
    return vn, p, sound


def hllc(a, b, n):
    va, pa, ca = side_values(a, n)
    vb, pb, cb = side_values(b, n)
    slow = jnp.minimum(va - ca, vb - cb)
    fast = jnp.maximum(va + ca, vb + cb)
    qa = a[0] * (slow - va)
    qb = b[0] * (fast - vb)
    contact = (pb - pa + va * qa - vb * qb) * reciprocal(qa - qb)
    is_low = contact >= 0.0

    def pick(x, y):
        return jnp.where(is_low, x, y)

    s = [pick(a[c], b[c]) for c in range(5)]
    v = pick(va, vb)
    p = pick(pa, pb)
    q = pick(qa, qb)
    speed = pick(slow, fast)
    clipped = pick(jnp.minimum(slow, 0.0), jnp.maximum(fast, 0.0))
    extra = clipped * (contact - v) * reciprocal(speed - contact)
    h = v + extra
    push = extra * q
    out = [s[0] * h, s[1] * h, s[2] * h, s[3] * h, (s[4] + p) * h + push * contact]
    out[n] = out[n] + p + push
    return out


def extract(u_ref, plane_ref, layers, nb, edge):
    half_blocks = nb // 2
    for side in range(2):
        for layer in range(layers):
            x = layer if side == 0 else edge - 1 - layer
            for c in range(5):
                plane_ref[side, layer, c * nb : (c + 1) * nb, :] = u_ref[:, c, x, :]
    grp = iota((ROWS, LANES), 1) // edge
    sub = iota((ROWS, LANES), 1) % edge
    zero = jnp.zeros((ROWS, LANES), F32)
    offsets = [o for layer in range(layers) for o in (layer, edge - 1 - layer)]

    def body(k, carry):
        c = k // 2
        start = pl.multiple_of((k % 2) * ROWS, ROWS)
        ylow = [[zero, zero] for _ in range(layers)]
        yhigh = [[zero, zero] for _ in range(layers)]
        zacc = {o: [zero, zero] for o in offsets}
        for b in range(nb):
            v = [u_ref[b, c, pl.ds(start, ROWS), h * LANES : (h + 1) * LANES] for h in range(2)]
            t = b // half_blocks
            low = pltpu.roll(v[0], edge * b % LANES, 1)
            high = pltpu.roll(v[1], edge * b % LANES, 1)
            for layer in range(layers):
                ylow[layer][t] = jnp.where(grp == (b + layer) % half_blocks, low, ylow[layer][t])
                yhigh[layer][t] = jnp.where(
                    grp == (b + half_blocks - 1 - layer) % half_blocks, high, yhigh[layer][t]
                )
            for h in range(2):
                r = pltpu.roll(v[h], b, 1) if b else v[h]
                for o in offsets:
                    zacc[o][h] = jnp.where(sub == (b + o) % edge, r, zacc[o][h])
        at = pl.ds(pl.multiple_of(k * ROWS, ROWS), ROWS)
        for layer in range(layers):
            for h in range(2):
                lanes = slice(h * LANES, (h + 1) * LANES)
                plane_ref[2, layer, at, lanes] = pltpu.roll(
                    ylow[layer][h], (LANES - edge * layer) % LANES, 1
                )
                plane_ref[3, layer, at, lanes] = pltpu.roll(
                    yhigh[layer][h], edge * (1 + layer) % LANES, 1
                )
                for side, o in ((0, layer), (1, edge - 1 - layer)):
                    plane_ref[4 + side, layer, at, lanes] = pltpu.roll(
                        zacc[o][h], (LANES - o) % LANES, 1
                    )
        return carry

    lax.fori_loop(0, 10, body, 0)


def expand_add(base_ref, add_ref, out_ref, layers, nb, edge):
    half_blocks = nb // 2
    lane = iota((ROWS, LANES), 1)
    row = iota((ROWS, LANES), 0)
    grp = lane // edge
    sub = lane % edge

    def body(k, carry):
        c = k // 2
        rt = k % 2
        start = pl.multiple_of(rt * ROWS, ROWS)
        at = pl.ds(pl.multiple_of(k * ROWS, ROWS), ROWS)

        def plane(face, layer, h):
            return add_ref[face, layer, at, h * LANES : (h + 1) * LANES]

        ylow = [[plane(2, layer, h) for h in range(2)] for layer in range(layers)]
        yhigh = [[plane(3, layer, h) for h in range(2)] for layer in range(layers)]
        zlow = [[plane(4, layer, h) for h in range(2)] for layer in range(layers)]
        zhigh = [[plane(5, layer, h) for h in range(2)] for layer in range(layers)]
        for h in range(2):
            zhigh[0][h] = pltpu.roll(zhigh[0][h], edge - 1, 1)
            if layers > 1:
                ylow[1][h] = pltpu.roll(ylow[1][h], edge, 1)
                yhigh[1][h] = pltpu.roll(yhigh[1][h], LANES - edge, 1)
                zlow[1][h] = pltpu.roll(zlow[1][h], 1, 1)
                zhigh[1][h] = pltpu.roll(zhigh[1][h], edge - 2, 1)
        for b in range(nb):
            t = b // half_blocks
            place = b % half_blocks
            if layers > 1:
                low = jnp.where(grp == place, ylow[0][t], ylow[1][t])
                high = jnp.where(grp == place, yhigh[0][t], yhigh[1][t])
            else:
                low = ylow[0][t]
                high = yhigh[0][t]
            low = pltpu.roll(low, (LANES - edge * place) % LANES, 1)
            high = pltpu.roll(high, edge * (half_blocks - 1 - place) % LANES, 1)
            parts = [
                jnp.where(grp < layers, low, 0.0),
                jnp.where(grp >= half_blocks - layers, high, 0.0),
            ]
            xrows = [
                add_ref[rt, layer, pl.ds(c * nb + b, 1), :] for layer in range(layers)
            ]
            for h in range(2):
                lanes = slice(h * LANES, (h + 1) * LANES)
                if layers > 1:
                    z = jnp.where(
                        sub == b,
                        zlow[0][h],
                        jnp.where(
                            sub == (b + 1) % edge,
                            zlow[1][h],
                            jnp.where(sub == (b + edge - 1) % edge, zhigh[0][h], zhigh[1][h]),
                        ),
                    )
                else:
                    z = jnp.where(sub == b, zlow[0][h], zhigh[0][h])
                if b:
                    z = pltpu.roll(z, LANES - b, 1)
                total = parts[h] + jnp.where((sub < layers) | (sub >= edge - layers), z, 0.0)
                x = jnp.where(row == (ROWS - 1) * rt, xrows[0][:, lanes], 0.0)
                if layers > 1:
                    x = jnp.where(row == 1 + (ROWS - 3) * rt, xrows[1][:, lanes], x)
                total = total + x
                out_ref[b, c, pl.ds(start, ROWS), lanes] = (
                    base_ref[b, c, pl.ds(start, ROWS), lanes] + total
                )
        return carry

    lax.fori_loop(0, 10, body, 0)


def take_lanes(v, index):
    return jnp.take_along_axis(v, index, axis=1, mode="promise_in_bounds")


def swap_row_group(v, edge):
    lane = iota((ROWS, LANES), 1)
    row = iota((ROWS, LANES), 0)
    g = take_lanes(v, (lane + edge * row) % LANES)
    for bit in (1, 2, 4):
        g = jnp.where(((lane // edge) & bit) != 0, pltpu.roll(g, bit, 0), g)
    return take_lanes(g, edge * ((row - lane // edge + ROWS) % ROWS) + lane % edge)


def swap_group_sub(v0, v1, half, edge):
    lane = iota((ROWS, LANES), 1)
    index = edge * (lane % ROWS) + (edge // 2) * half + lane // edge
    return jnp.where(lane % edge < edge // 2, take_lanes(v0, index), take_lanes(v1, index))


def common_tile(load, axis, m, half, edge):
    if axis == 0:
        return swap_row_group(load(m - m % 2 + half, m % 2), edge)
    if axis == 1:
        return load(m, half)
    return swap_group_sub(load(m, 0), load(m, 1), half, edge)


def plane_loader(ref, face, layer):
    def load(m, half):
        return ref[face, layer, m * ROWS : (m + 1) * ROWS, half * LANES : (half + 1) * LANES]

    return load


def interleave(plane_ref, first, second, mix_ref, edge):
    odd = (iota((ROWS, LANES), 1) // edge) % 2 == 1
    for face in range(6):
        axis = face // 2
        for index, (m1, m2) in enumerate(zip(first[1], second[1])):
            for half in range(2):
                a = common_tile(plane_loader(plane_ref, face, first[0]), axis, m1, half, edge)
                b = common_tile(plane_loader(plane_ref, face, second[0]), axis, m2, half, edge)
                at = slice(index * ROWS, (index + 1) * ROWS)
                mix_ref[face, 0, half, at, :] = jnp.where(odd, pltpu.roll(b, edge, 1), a)
                mix_ref[face, 1, half, at, :] = jnp.where(odd, b, pltpu.roll(a, LANES - edge, 1))


def disentangle(mix_ref, first, second, plane_ref, temp_ref, edge):
    odd = (iota((ROWS, LANES), 1) // edge) % 2 == 1
    for face in range(6):
        axis = face // 2
        for index, (m1, m2) in enumerate(zip(first[1], second[1])):
            for half in range(2):
                at = slice(index * ROWS, (index + 1) * ROWS)
                even_tile = mix_ref[face, 0, half, at, :]
                odd_tile = mix_ref[face, 1, half, at, :]
                lanes = slice(half * LANES, (half + 1) * LANES)
                a = jnp.where(odd, pltpu.roll(odd_tile, edge, 1), even_tile)
                b = jnp.where(odd, odd_tile, pltpu.roll(even_tile, LANES - edge, 1))
                target = plane_ref if axis == 1 else temp_ref
                target[face, first[0], m1 * ROWS : (m1 + 1) * ROWS, lanes] = a
                target[face, second[0], m2 * ROWS : (m2 + 1) * ROWS, lanes] = b
        if axis == 1:
            continue
        for layer in sorted({first[0], second[0]}):
            for m in range(10):
                for half in range(2):
                    plane_ref[
                        face, layer, m * ROWS : (m + 1) * ROWS, half * LANES : (half + 1) * LANES
                    ] = common_tile(plane_loader(temp_ref, face, layer), axis, m, half, edge)


def slot_place(slot, edge):
    per_tile = LANES // (2 * edge)
    return slot // per_tile, slot % per_tile


def pack_items(tab_ref, valid_row, slot_row, mix_ref, send_ref, rows, nb, edge):
    wide = 2 * edge
    lane_slot = iota((rows, LANES), 1) // wide

    def body(i, carry):
        def move():
            block = i // 6
            face = i % 6
            half = block // (nb // 2)
            place = (block % (nb // 2)) // 2
            group, q = slot_place(tab_ref[slot_row, i], edge)
            v = mix_ref[face, block % 2, half]
            v = pltpu.roll(v, (wide * (q - place) + LANES) % LANES, 1)
            at = pl.ds(pl.multiple_of(group * rows, ROWS), rows)
            target = tab_ref[0, i]
            send_ref[target, at, :] = jnp.where(lane_slot == q, v, send_ref[target, at, :])

        if valid_row is None:
            move()
        else:
            pl.when(tab_ref[valid_row, i] > 0)(move)
        return carry

    lax.fori_loop(0, 6 * nb, body, 0)


def unpack_items(tab_ref, valid_row, slot_row, recv_ref, mix_ref, rows, nb, edge):
    wide = 2 * edge
    lane_slot = iota((rows, LANES), 1) // wide
    per_half = nb // 4

    def body(k, carry):
        face = k % 6
        parity = (k // 6) % 2
        half = k // 12
        acc = jnp.zeros((rows, LANES), F32)
        for place in range(per_half):
            i = (half * (nb // 2) + 2 * place + parity) * 6 + face
            group, q = slot_place(tab_ref[slot_row, i], edge)
            at = pl.ds(pl.multiple_of(group * rows, ROWS), rows)
            v = recv_ref[tab_ref[0, i], at, :]
            v = pltpu.roll(v, (wide * (place - q) + LANES) % LANES, 1)
            keep = lane_slot == place
            if valid_row is not None:
                keep = keep & (tab_ref[valid_row, i] > 0)
            acc = jnp.where(keep, v, acc)
        mix_ref[face, parity, half] = acc
        return carry

    lax.fori_loop(0, 24, body, 0)


def interior_kernel(nb, edge, u_ref, d_ref):
    square = edge * edge

    def sweep(u, axis, index, size, step, dim):
        n = 1 + axis
        below = [x - pltpu.roll(x, step, dim) for x in u]
        above = [pltpu.roll(x, size - step, dim) for x in below]
        low, high = evolve(u, below, above, n)
        prev = [pltpu.roll(x, step, dim) for x in high]
        inside = (index >= 2) & (index <= edge - 2)
        flux = [jnp.where(inside, x, 0.0) for x in hllc(prev, low, n)]
        return [pltpu.roll(x, size - step, dim) - x for x in flux]

    def body(b, carry):
        for rt in range(edge // ROWS):
            rows = slice(rt * ROWS, (rt + 1) * ROWS)
            u = [u_ref[b, c, rows, :] for c in range(5)]
            div = sweep(u, 1, iota((ROWS, square), 1) // edge, square, edge, 1)
            for c in range(5):
                d_ref[b, c, rows, :] = u[c] - STEP_RATIO * div[c]
        for half in range(square // LANES):
            lanes = slice(half * LANES, (half + 1) * LANES)
            u = [u_ref[b, c, :, lanes] for c in range(5)]
            div = sweep(u, 0, iota((edge, LANES), 0), edge, 1, 0)
            more = sweep(u, 2, iota((edge, LANES), 1) % edge, LANES, 1, 1)
            for c in range(5):
                d_ref[b, c, :, lanes] = d_ref[b, c, :, lanes] - STEP_RATIO * (div[c] + more[c])
        return carry

    lax.fori_loop(0, nb, body, 0)


def face_fluxes(plane_ref, ghost_ref, add_ref, face_ref, nb):
    for face in range(6):
        axis = face // 2
        side = face % 2
        n = 1 + axis
        sign = 1.0 - 2.0 * side

        def body(rt, carry):
            def load(ref, layer):
                return [
                    ref[face, layer, pl.ds(pl.multiple_of(c * nb + rt * ROWS, ROWS), ROWS), :]
                    for c in range(5)
                ]

            near, mid, deep = (load(plane_ref, layer) for layer in range(3))
            ghost, far = (load(ghost_ref, layer) for layer in range(2))

            def steps(a, b):
                return [sign * (y - x) for x, y in zip(a, b)]

            d0, d1, d2, d3 = steps(far, ghost), steps(ghost, near), steps(near, mid), steps(mid, deep)
            if side == 0:
                first = hllc(evolve(ghost, d0, d1, n)[1], evolve(near, d1, d2, n)[0], n)
                second = hllc(evolve(near, d1, d2, n)[1], evolve(mid, d2, d3, n)[0], n)
            else:
                first = hllc(evolve(near, d1, d2, n)[1], evolve(ghost, d0, d1, n)[0], n)
                second = hllc(evolve(mid, d2, d3, n)[1], evolve(near, d1, d2, n)[0], n)
            for c in range(5):
                at = pl.ds(pl.multiple_of(c * nb + rt * ROWS, ROWS), ROWS)
                face_ref[face, at, :] = first[c]
                add_ref[face, 0, at, :] = (sign * STEP_RATIO) * (first[c] - second[c])
                add_ref[face, 1, at, :] = (sign * STEP_RATIO) * second[c]
            return carry

        lax.fori_loop(0, nb // ROWS, body, 0)


ALL = tuple(range(10))
FIRST_HALF = tuple(range(5))
SECOND_HALF = tuple(range(5, 10))


def planes_kernel(nb, edge, u_ref, plane_ref):
    extract(u_ref, plane_ref, 3, nb, edge)


def pack_kernel(nb, edge, tab_ref, plane_ref, send_ref, mix_ref):
    interleave(plane_ref, (0, ALL), (1, ALL), mix_ref, edge)
    pack_items(tab_ref, None, 1, mix_ref, send_ref, 80, nb, edge)


def rim_place(p, face, edge):
    start = (face * 2 + p) * edge
    return start // LANES, start % LANES


def rims_kernel(nb, edge, parents_here, rows, tab_ref, recv_ref, rim_ref):
    slot_row = 2 if rows == 80 else 6
    lane_group = iota((rows, LANES), 1) // edge
    acc = {}
    for face in range(6):
        for p in range(parents_here):
            i = tab_ref[9, p] * 6 + face
            group, q = slot_place(tab_ref[slot_row, i], edge)
            at = pl.ds(pl.multiple_of(group * rows, ROWS), rows)
            v = recv_ref[tab_ref[0, i], at, :]
            half, lane = rim_place(p, face, edge)
            for part in range(80 // rows):
                turn = (lane - 2 * edge * q - edge * part + 2 * LANES) % LANES
                moved = pltpu.roll(v, turn, 1)
                old = acc.get((part, half), jnp.zeros((rows, LANES), F32))
                acc[part, half] = jnp.where(lane_group == lane // edge, moved, old)
    for (part, half), value in acc.items():
        rim_ref[part * rows : (part + 1) * rows, half * LANES : (half + 1) * LANES] = value


def coarse_kernel(
    nb, edge, tab_ref, d_ref, plane_ref, recv_ref, new_ref, face_ref, send_ref, mix_ref, ghost_ref,
    temp_ref, add_ref, near_ref, mix2_ref,
):
    unpack_items(tab_ref, None, 2, recv_ref, mix_ref, 80, nb, edge)
    disentangle(mix_ref, (0, ALL), (1, ALL), ghost_ref, temp_ref, edge)
    face_fluxes(plane_ref, ghost_ref, add_ref, face_ref, nb)
    expand_add(d_ref, add_ref, new_ref, 2, nb, edge)
    extract(new_ref, near_ref, 1, nb, edge)
    interleave(near_ref, (0, FIRST_HALF), (0, SECOND_HALF), mix2_ref, edge)
    pack_items(tab_ref, 3, 5, mix2_ref, send_ref, 40, nb, edge)


def kron_rows(size, edge, shift, transposed):
    i = iota((size, size), 0)
    j = iota((size, size), 1)
    if transposed:
        i, j = j, i
    hit = (i // edge == j // edge) & (j % edge == shift + (i % edge) // 2)
    return jnp.where(hit, 1.0, 0.0).astype(F32)


def key_matrix(key_row, face, edge, width):
    offset = (face * 2 * edge) % LANES
    return jnp.where(iota((2 * LANES, width), 0) == key_row + offset, 1.0, 0.0).astype(F32)


def fine_kernel(
    nb, edge, late, key_ref, d_ref, plane_ref, rim_ref, rim2_ref, new_ref, face_ref, ghost_ref,
    temp_ref, add_ref,
):
    width = nb * edge
    rim = 0.5 * (rim_ref[...] + rim2_ref[...]) if late else rim_ref[...]
    halves = [exact_dot(kron_rows(80, edge, h * (edge // 2), False), rim) for h in range(2)]
    for face in range(6):
        axis = face // 2
        side = face % 2
        opposite = face + 1 - 2 * side
        tile = (face * 2 * edge) // LANES
        both = jnp.concatenate([x[:, tile * LANES : (tile + 1) * LANES] for x in halves], axis=1)
        outer = exact_dot(both, key_matrix(key_ref[axis : axis + 1, :], face, edge, width))
        if axis == 0:
            temp_ref[face, 0] = outer
            for m in range(10):
                for half in range(2):
                    temp_ref[
                        face, 1, m * ROWS : (m + 1) * ROWS, half * LANES : (half + 1) * LANES
                    ] = common_tile(plane_loader(temp_ref, face, 0), 0, m, half, edge)
            outer = temp_ref[face, 1]
            sib = key_ref[16 : 16 + nb, 0:80]
            i = iota((80, 80), 0)
            j = iota((80, 80), 1)
            sib = jnp.concatenate([sib] * 5, axis=0)
            swap = jnp.where((j % nb == sib) & (i // nb == j // nb), 1.0, 0.0).astype(F32)
            outward = jnp.concatenate([key_ref[32 : 32 + nb, :]] * 5, axis=0) == side
        else:
            swap = jnp.where(
                iota((width, width), 0) == key_ref[2 + axis : 3 + axis, :], 1.0, 0.0
            ).astype(F32)
            outward = key_ref[4 + axis : 5 + axis, :] == side
        for layer in range(2):
            own = plane_ref[opposite, layer]
            inner = exact_dot(swap, own) if axis == 0 else exact_dot(own, swap)
            ghost_ref[face, layer] = jnp.where(outward, outer, inner)
    face_fluxes(plane_ref, ghost_ref, add_ref, face_ref, nb)
    expand_add(d_ref, add_ref, new_ref, 2, nb, edge)


def means_kernel(nb, edge, key_ref, first_ref, second_ref, mean_ref, temp_ref):
    width = nb * edge
    acc = [None, None]
    for face in range(6):
        axis = face // 2
        side = face % 2
        tile = (face * 2 * edge) // LANES
        total = first_ref[face] + second_ref[face]
        if axis == 0:
            outward = jnp.concatenate([key_ref[32 : 32 + nb, :]] * 5, axis=0) == side
            temp_ref[face, 0] = jnp.where(outward, total, 0.0)
            for m in range(10):
                for half in range(2):
                    temp_ref[
                        face, 1, m * ROWS : (m + 1) * ROWS, half * LANES : (half + 1) * LANES
                    ] = common_tile(plane_loader(temp_ref, face, 0), 0, m, half, edge)
            total = temp_ref[face, 1]
        else:
            total = jnp.where(key_ref[4 + axis : 5 + axis, :] == side, total, 0.0)
        part = exact_dot_nt(total, key_matrix(key_ref[axis : axis + 1, :], face, edge, width))
        acc[tile] = part if acc[tile] is None else acc[tile] + part
    for tile in range(2):
        mean_ref[:, tile * LANES : (tile + 1) * LANES] = 0.125 * sum(
            exact_dot(
                kron_rows(80, edge, h * (edge // 2), True),
                acc[tile][:, h * LANES : (h + 1) * LANES],
            )
            for h in range(2)
        )


def averages_kernel(nb, edge, octant_ref, u_ref, out_ref):
    square = edge * edge
    half = edge // 2
    i = iota((square, LANES), 0)
    pairs = jnp.where(
        iota((square, LANES), 1) == (i // edge // 2) * edge + (i % edge) // 2, 0.125, 0.0
    ).astype(F32)
    i = iota((5 * half, 5 * edge), 0)
    j = iota((5 * half, 5 * edge), 1)
    rows = jnp.where(j // 2 == i, 1.0, 0.0).astype(F32)
    high = (iota((5 * half, LANES), 1) % edge) // half
    out_ref[...] = jnp.zeros(out_ref.shape, F32)

    def body(b, carry):
        octant = octant_ref[0, b]
        p = octant_ref[1, b]
        oz = octant % 2
        u = u_ref[b].reshape(5 * edge, square)
        v = exact_dot(rows, exact_dot(u, pairs))
        v = jnp.where(high == oz, pltpu.roll(v, half * oz, 1), 0.0)
        lanes = pl.ds(pl.multiple_of((octant // 2 % 2) * LANES, LANES), LANES)
        at = pl.ds(pl.multiple_of((octant // 4) * ROWS, ROWS), ROWS)
        for c in range(5):
            out_ref[p, c, at, lanes] = out_ref[p, c, at, lanes] + v[c * half : (c + 1) * half, :]
        return carry

    lax.fori_loop(0, nb, body, 0)


def return_kernel(nb, edge, parents_here, tab_ref, mean_ref, send_ref):
    rows = 40
    lane_slot = iota((rows, LANES), 1) // edge
    for face in range(6):
        for p in range(parents_here):
            i = tab_ref[9, p] * 6 + face
            group, q = slot_place(tab_ref[7, i], edge)
            at = pl.ds(pl.multiple_of(group * rows, ROWS), rows)
            half, lane = rim_place(p, face, edge)
            target = tab_ref[0, i]
            value = send_ref[target, at, :]
            for part in range(2):
                v = mean_ref[part * rows : (part + 1) * rows, half * LANES : (half + 1) * LANES]
                turn = (2 * edge * q + edge * part - lane + LANES) % LANES
                v = pltpu.roll(v, turn, 1)
                value = jnp.where(lane_slot == 2 * q + part, v, value)
            send_ref[target, at, :] = value


def correct_kernel(
    nb, edge, parents_here, tab_ref, new_ref, face_ref, mask_ref, recv_ref, cells_ref, out_ref,
    mix_ref, mean_ref, temp_ref, add_ref, base_ref,
):
    unpack_items(tab_ref, 3, 8, recv_ref, mix_ref, 40, nb, edge)
    disentangle(mix_ref, (0, FIRST_HALF), (0, SECOND_HALF), mean_ref, temp_ref, edge)
    for face in range(6):
        sign = STEP_RATIO if face % 2 else -STEP_RATIO
        beside = jnp.concatenate([mask_ref[face]] * 5, axis=0) > 0.0
        add_ref[face, 0] = jnp.where(beside, sign * (face_ref[face] - mean_ref[face, 0]), 0.0)
    base_ref[...] = new_ref[...]
    for p in range(parents_here):
        base_ref[tab_ref[9, p]] = cells_ref[p]
    expand_add(base_ref, add_ref, out_ref, 1, nb, edge)


def run(kernel, outs, operands, scratch=(), scalars=0, flops=0):
    single = isinstance(outs[0], int)
    shapes = [outs] if single else list(outs)
    smem = pl.BlockSpec(memory_space=pltpu.SMEM)
    vmem = pl.BlockSpec(memory_space=pltpu.VMEM)
    result = pl.pallas_call(
        kernel,
        out_shape=[jax.ShapeDtypeStruct(s, F32) for s in shapes],
        in_specs=[smem if k < scalars else vmem for k in range(len(operands))],
        out_specs=[vmem] * len(shapes),
        scratch_shapes=[pltpu.VMEM(s, F32) for s in scratch],
        compiler_params=pltpu.CompilerParams(vmem_limit_bytes=VMEM_LIMIT),
        cost_estimate=pl.CostEstimate(
            flops=flops, bytes_accessed=4 * sum(o.size for o in operands), transcendentals=0
        ),
    )(*operands)
    return result[0] if single else result


def level_shift(array, source):
    return lax.ppermute(array, "level", [(source, 1 - source)])


def route(buffer):
    return lax.all_to_all(buffer, "blk", split_axis=0, concat_axis=0, tiled=True)


def local(fluid_state, neighbours, parents):
    level_id = lax.axis_index("level")
    blk_index = lax.axis_index("blk")
    devices = lax.axis_size("blk")
    u = fluid_state[0]
    nb, _, edge, square = u.shape
    width = nb * edge
    parents_here = nb // 8
    capacity = 2 * ((6 * nb + devices - 1) // devices)
    per_tile = LANES // (2 * edge)
    groups = (capacity + per_tile - 1) // per_tile

    own_rows = lax.dynamic_slice_in_dim(neighbours, blk_index * nb, nb, 0)
    parent_rows = lax.dynamic_slice_in_dim(parents, blk_index * nb, nb, 0)
    parent_of = parent_rows[:, 0] - blk_index * nb
    octants = parent_rows[:, 1]
    beside = jnp.any(own_rows[:, :, None] == parents[None, None, :, 0], axis=2)
    is_parent = jnp.any(jnp.arange(nb)[:, None] == parent_of[None, :], axis=1)
    flat = own_rows.reshape(-1)
    items = jnp.arange(6 * nb, dtype=I32)
    targets = flat // nb
    faces = items % 6
    wanted = flat % nb * 6 + faces + 1 - 2 * (faces % 2)
    beside_item = beside.reshape(-1)
    parent_item = jnp.repeat(is_parent, 6)
    same = targets[:, None] == targets[None, :]
    by_own = same & (items[None, :] < items[:, None])
    by_wanted = same & (wanted[None, :] < wanted[:, None])

    def rank(order, mask=None):
        return jnp.sum(order if mask is None else order & mask[None, :], axis=1, dtype=I32)

    slot_of_block = jnp.sum(parent_of[None, :] < parent_of[:, None], axis=1, dtype=I32) // 8
    parent_list = jnp.sum(
        jnp.where(
            (slot_of_block[None, :] == jnp.arange(6 * nb)[:, None]) & (octants[None, :] == 0),
            parent_of[None, :],
            0,
        ),
        axis=1,
        dtype=I32,
    )
    table = jnp.stack(
        [
            targets,
            rank(by_own),
            rank(by_wanted),
            beside_item.astype(I32),
            parent_item.astype(I32),
            rank(by_own, beside_item),
            rank(by_wanted, parent_item),
            rank(by_own, parent_item),
            rank(by_wanted, beside_item),
            parent_list,
        ]
    )
    siblings = []
    bits = []
    keys = []
    for axis in range(3):
        bit = BIT_OF[axis]
        partner = octants + bit - 2 * bit * (octants // bit % 2)
        match = (parent_of[:, None] == parent_of[None, :]) & (octants[None, :] == partner[:, None])
        siblings.append(jnp.sum(jnp.where(match, jnp.arange(nb)[None, :], 0), axis=1, dtype=I32))
        bits.append(octants // bit % 2)
        first = octants // TANGENT[axis][0] % 2
        second = octants // TANGENT[axis][1] % 2
        keys.append(first * LANES + slot_of_block * edge + second * (edge // 2))
    along = jnp.arange(edge, dtype=I32)

    def block_major(per_block, per_edge):
        return (per_block[:, None] + per_edge[None, :]).reshape(-1)

    def edge_major(per_block, per_edge):
        return (per_block[None, :] + per_edge[:, None]).reshape(-1)

    none = 0 * along
    key_rows = [
        block_major(keys[0], along // 2),
        block_major(keys[1], along // 2),
        edge_major(keys[2], along // 2),
        block_major(siblings[1] * edge, along),
        edge_major(siblings[2], along * edge),
        block_major(bits[1], none),
        edge_major(bits[2], none),
    ]
    key_table = jnp.concatenate(
        [
            jnp.pad(jnp.stack(key_rows), ((0, 16 - len(key_rows)), (0, 0))),
            jnp.broadcast_to(siblings[0][:, None], (nb, width)),
            jnp.broadcast_to(bits[0][:, None], (nb, width)),
        ],
        axis=0,
    )
    octant_table = jnp.stack([octants, slot_of_block])
    beside_f = beside.astype(F32)
    zeros = jnp.zeros((nb, edge), F32)
    mask = jnp.stack(
        [
            jnp.broadcast_to(beside_f[:, 0][:, None], (nb, width)),
            jnp.broadcast_to(beside_f[:, 1][:, None], (nb, width)),
            jnp.broadcast_to((beside_f[:, 2][:, None] + zeros).reshape(1, -1), (nb, width)),
            jnp.broadcast_to((beside_f[:, 3][:, None] + zeros).reshape(1, -1), (nb, width)),
            jnp.broadcast_to((beside_f[:, 4][None, :] + zeros.T).reshape(1, -1), (nb, width)),
            jnp.broadcast_to((beside_f[:, 5][None, :] + zeros.T).reshape(1, -1), (nb, width)),
        ]
    )

    part = functools.partial
    cell_shape = u.shape
    plane_shape = (6, 3, 5 * edge, width)
    ghost_shape = (6, 2, 5 * edge, width)
    layer_shape = (6, 1, 5 * edge, width)
    face_shape = (6, 5 * edge, width)
    rim_shape = (5 * edge, 2 * LANES)
    wide_send = (devices, groups * 5 * edge, LANES)
    thin_rows = 5 * edge // 2
    thin_send = (devices, groups * thin_rows, LANES)
    wide_mix = (6, 2, 2, 5 * edge, LANES)
    thin_mix = (6, 2, 2, thin_rows, LANES)
    work = 220 * 3 * 5 * nb * edge * square

    planes = run(part(planes_kernel, nb, edge), plane_shape, [u])

    def interior(cells):
        return run(part(interior_kernel, nb, edge), cell_shape, [cells], flops=work)

    def coarse_first(planes, u):
        send = run(part(pack_kernel, nb, edge), wide_send, [table, planes], [wide_mix], 1)
        received = route(send)
        partial_new = interior(u)
        rims = run(
            part(rims_kernel, nb, edge, parents_here, 80), rim_shape, [table, received], (), 1
        )
        return partial_new, received, rims

    def fine_first(planes, u):
        return interior(u), jnp.zeros(wide_send, F32), jnp.zeros(rim_shape, F32)

    partial_new, received, rims = lax.cond(level_id == 0, coarse_first, fine_first, planes, u)
    early_rims = level_shift(rims, 0)

    def coarse_second(partial_new, planes, received, early_rims):
        cells, faces, send = run(
            part(coarse_kernel, nb, edge),
            [cell_shape, face_shape, thin_send],
            [table, partial_new, planes, received],
            [wide_mix, ghost_shape, ghost_shape, ghost_shape, layer_shape, thin_mix],
            1,
        )
        late = run(
            part(rims_kernel, nb, edge, parents_here, thin_rows),
            rim_shape,
            [table, route(send)],
            (),
            1,
        )
        return cells, faces, late, planes, cells

    def advance_fine(late, partial_new, planes, rim, rim2):
        return run(
            part(fine_kernel, nb, edge, late),
            [cell_shape, face_shape],
            [key_table, partial_new, planes, rim, rim2],
            [ghost_shape, ghost_shape, ghost_shape],
        )

    def fine_second(partial_new, planes, received, early_rims):
        cells, faces = advance_fine(False, partial_new, planes, early_rims, early_rims)
        new_planes = run(part(planes_kernel, nb, edge), plane_shape, [cells])
        return cells, faces, early_rims, new_planes, interior(cells)

    cells, faces, late, planes, partial_new = lax.cond(
        level_id == 0, coarse_second, fine_second, partial_new, planes, received, early_rims
    )
    late_rims = level_shift(late, 0)

    def fine_third(partial_new, planes, faces, early_rims, late_rims):
        out, more = advance_fine(True, partial_new, planes, early_rims, late_rims)
        means = run(
            part(means_kernel, nb, edge), rim_shape, [key_table, faces, more], [ghost_shape]
        )
        averages = run(
            part(averages_kernel, nb, edge),
            (parents_here,) + cell_shape[1:],
            [octant_table, out],
            (),
            1,
        )
        return out, means, averages

    def coarse_third(partial_new, planes, faces, early_rims, late_rims):
        return (
            partial_new,
            early_rims,
            jnp.zeros((parents_here,) + cell_shape[1:], F32),
        )

    out, means, averages = lax.cond(
        level_id == 0, coarse_third, fine_third, partial_new, planes, faces, early_rims, late_rims
    )
    means = level_shift(means, 1)
    averages = level_shift(averages, 1)

    def coarse_fourth(out, cells, faces, means, averages):
        send = run(
            part(return_kernel, nb, edge, parents_here), thin_send, [table, means], (), 1
        )
        return run(
            part(correct_kernel, nb, edge, parents_here),
            cell_shape,
            [table, cells, faces, mask, route(send), averages],
            [thin_mix, layer_shape, layer_shape, layer_shape, cell_shape],
            1,
        )

    def fine_fourth(out, cells, faces, means, averages):
        return out

    finished = lax.cond(
        level_id == 0, coarse_fourth, fine_fourth, out, cells, faces, means, averages
    )
    return finished[None]


def solution(mesh):
    return jax.shard_map(
        local,
        mesh=mesh,
        in_specs=(P("level", "blk", None, None, None), P(), P()),
        out_specs=P("level", "blk", None, None, None),
        check_vma=False,
    )
```

time: 837 us -> 157 us (0.19); the launches traced: 822 us -> 157 us
  local copies, waits for them, and re-layouts: 538 us -> 6.51 us
  waiting for transfers between devices: 172 us -> 49.2 us
  other arithmetic: 68.6 us -> 1.37 us
  Pallas kernels: 0 us -> 57.7 us
  blocking collectives: 0 us -> 20.9 us
  starting transfers between devices: 30.7 us -> 20.7 us
  loops' own time: 9.99 us -> 0.06 us
    reshape x36 -> x6, local copies, waits for them, and re-layouts: 190 us -> 0.51 us  [the longest x2 0.18 us: local(): flat = own_rows.reshape(-1)]
    gather x64 -> x0, local copies, waits for them, and re-layouts: 124 us -> none  [the longest x2 51.2 us: local(): neighbours.reshape(-1)]
    ppermute x3 -> x4, waiting for transfers between devices: 138 us -> 21.9 us  [level_shift(): return lax.ppermute(array, 'level', [(source, 1 - source)])]
    transpose x14 -> x0, local copies, waits for them, and re-layouts: 75.2 us -> none  [the longest x2 24.6 us: restored(): cube_cells = cube_cells.transpose(0, 1, 3, 4, 2)]
    pallas_call x0 -> x8, Pallas kernels: none -> 57.7 us  [run(): pl.pallas_call(kernel, out_shape=[jax.ShapeDtypeStruct(s, F32) for s in s...]
    another operation x28 -> x6, local copies, waits for them, and re-layouts: 34.5 us -> 0.26 us  [the longest x3 0.19 us: local(): jnp.stack(key_rows)]
    scatter x9 -> x0, local copies, waits for them, and re-layouts: 32.3 us -> none  [the longest x5 28.1 us: spread(): return jnp.zeros((device_count, capacity) + payload.shape[1:], payload.dt...]
    unnamed x198 -> x9, local copies, waits for them, and re-layouts: 28.1 us -> 0.17 us
  transfers between devices with their start and end apart: 6 -> 6, of which waited for: 4 -> 4; matrix products, arithmetic and copies ran while one was open for 10% -> 3% of each run, Pallas kernels for 0% -> 6%
where the time goes in v1:
time: 157 us
  Pallas kernels  57.7 us (37%)
  waiting for transfers between devices  49.2 us (31%)
  blocking collectives  20.9 us (13%)
  starting transfers between devices  20.7 us (13%)
  local copies, waits for them, and re-layouts  6.51 us (4%)
    pallas_call x8, Pallas kernels, run(): pl.pallas_call(kernel, out_shape=[jax.ShapeDtypeStruct(s, F32) for s in s...  57.7 us
    all_to_all x2, waiting for transfers between devices, route(): lax.all_to_all(buffer, 'blk', split_axis=0, concat_axis=0, tiled=True)  27.3 us
    ppermute x4, waiting for transfers between devices, level_shift(): return lax.ppermute(array, 'level', [(source, 1 - source)])  21.9 us
    all_to_all x1, blocking collectives, route(): lax.all_to_all(buffer, 'blk', split_axis=0, concat_axis=0, tiled=True)  20.9 us
    all_to_all x2, starting transfers between devices, route(): lax.all_to_all(buffer, 'blk', split_axis=0, concat_axis=0, tiled=True)  15.5 us
    ppermute x4, starting transfers between devices, level_shift(): return lax.ppermute(array, 'level', [(source, 1 - source)])  5.17 us
  transfers between devices with their start and end apart: 6, of which 4 were waited for; matrix products, arithmetic and copies ran while one was open for 3% of the time, Pallas kernels for 6%

profile of v1, /device:TPU:0, one launch (start us, length us, event | category | flops | bytes accessed | tf_op | source)
XLA Modules:
  0.0 156.7 jit_solution(3340931167815982428)
XLA Ops:
  0.0 0.8 constant_dynamic-slice_fusion.1
  3.2 3.7 %shard_map.39 = f32[6,3,80,256]{3,2,1,0:T(8,128)S(1)} custom-call(f32[16,5,16,256]{3,2,1,0:T(8,128)} %bitcast.70), custom_call_target="tpu_custom_call" | custom-call | bytes 1310720 | tf_op jit(solution)/shard_map/pallas_call | solution.py:635
  7.4 49.4 %conditional.4 = (f32[16,5,16,256]{3,2,1,0:T(8,128)}, f32[16,240,128]{2,1,0:T(8,128)}, f32[80,256]{1,0:T(8,128)S(1)}) conditional(s32[]{:T(128)} %convert_element_type.57, f32[16,5,16,256]{3,2,1,0:T(8,128)S(1)} %bitcast.71, (f32[16,5,16,256]{3,2,1,0:T(8,128)S(1)}, s32[10,96]{1,0:T(8,128)S(1)}, f32[6,3,80,256]{3,2,1,0:T(8,128)S(1)}) %tuple.85), branch_computations={%region_13.14_spmd, %region_14.15_spmd} | conditional | flops 216268800 | bytes 10657336 | solution.py:796
  7.4 14.9 %branch_1_fun.8 = f32[16,240,128]{2,1,0:T(8,128)} custom-call(s32[10,96]{1,0:T(8,128)S(1)} %get-tuple-element.65.tab_ref, f32[6,3,80,256]{3,2,1,0:T(8,128)S(1)} %get-tuple-element.66.plane_ref), custom_call_target="tpu_custom_call" | custom-call | bytes 1478400 | tf_op jit(solution)/shard_map/cond/branch_1_fun/pallas_call | solution.py:635
  22.4 8.4 %all-to-all-start = ((f32[16,240,128]{2,1,0:T(8,128)}), f32[16,240,128]{2,1,0:T(8,128)}, u32[]{:S(2)}, u32[]{:S(2)}) async-start(f32[16,240,128]{2,1,0:T(8,128)} %branch_1_fun.8), calls=%async_computation | async-start | bytes 3932160 | tf_op jit(solution)/shard_map/cond/branch_1_fun/all_to_all | solution.py:654
  30.7 9.5 %branch_1_fun.7 = f32[16,5,16,256]{3,2,1,0:T(8,128)} custom-call(f32[16,5,16,256]{3,2,1,0:T(8,128)S(1)} %get-tuple-element.64.u_ref), custom_call_target="tpu_custom_call" | custom-call | flops 216268800 | bytes 1310720 | tf_op jit(solution)/shard_map/cond/branch_1_fun/pallas_call | solution.py:635
  40.2 14.8 %all-to-all-done.recv_ref = f32[16,240,128]{2,1,0:T(8,128)} async-done(((f32[16,240,128]{2,1,0:T(8,128)}), f32[16,240,128]{2,1,0:T(8,128)}, u32[]{:S(2)}, u32[]{:S(2)}) %all-to-all-start) | async-done | bytes 1966112 | tf_op jit(solution)/shard_map/cond/branch_1_fun/all_to_all | solution.py:654
  55.1 1.8 %branch_1_fun.9 = f32[80,256]{1,0:T(8,128)S(1)} custom-call(s32[10,96]{1,0:T(8,128)S(1)} %get-tuple-element.65.tab_ref, f32[16,240,128]{2,1,0:T(8,128)} %all-to-all-done.recv_ref), custom_call_target="tpu_custom_call" | custom-call | bytes 1969920 | tf_op jit(solution)/shard_map/cond/branch_1_fun/pallas_call | solution.py:635
  56.8 1.3 collective-permute-start
  60.0 41.2 %conditional.5 = (f32[16,5,16,256]{3,2,1,0:T(8,128)}, f32[6,80,256]{2,1,0:T(8,128)S(1)}, f32[80,256]{1,0:T(8,128)S(1)}, f32[6,3,80,256]{3,2,1,0:T(8,128)S(1)}, f32[16,5,16,256]{3,2,1,0:T(8,128)}) conditional(s32[]{:T(128)} %convert_element_type.57, (s32[48,256]{1,0:T(8,128)S(1)}, f32[16,5,16,256]{3,2,1,0:T(8,128)}, ...), branch_computations={%region_15.16_spmd, %region_16.17_spmd} | conditional | flops 216268800 | bytes 11312712 | solution.py:829
  60.0 18.2 %branch_1_fun.10 = (f32[16,5,16,256]{3,2,1,0:T(8,128)}, f32[6,80,256]{2,1,0:T(8,128)S(1)}, f32[16,120,128]{2,1,0:T(8,128)}) custom-call(s32[10,96]{1,0:T(8,128)S(1)} %get-tuple-element.73.tab_ref, f32[16,5,16,256]{3,2,1,0:T(8,128)} %get-tuple-element.74.d_ref, f32[6,3,80,256]{3,2,1,0:T(8,128)S(1)} %get-tuple-element.178.plane_ref, ...), custom_call_target="tpu_custom_call" | custom-call | bytes 4755200 | tf_op jit(solution)/shard_map/cond/branch_1_fun/pallas_call | solution.py:635
  78.2 7.1 %all-to-all-start.1 = ((f32[16,120,128]{2,1,0:T(8,128)}), f32[16,120,128]{2,1,0:T(8,128)S(1)}, u32[]{:S(2)}, u32[]{:S(2)}) async-start(f32[16,120,128]{2,1,0:T(8,128)} %get-tuple-element.79), calls=%async_computation.1 | async-start | bytes 1966080 | tf_op jit(solution)/shard_map/cond/branch_1_fun/all_to_all | solution.py:654
  85.3 2.5 %copy.35 = f32[16,5,16,256]{3,2,1,0:T(8,128)} copy(f32[16,5,16,256]{3,2,1,0:T(8,128)} %get-tuple-element.179) | data formatting | bytes 2621440 | tf_op jit(solution)/shard_map/cond
  87.8 12.5 %all-to-all-done.1.recv_ref = f32[16,120,128]{2,1,0:T(8,128)S(1)} async-done(((f32[16,120,128]{2,1,0:T(8,128)}), f32[16,120,128]{2,1,0:T(8,128)S(1)}, u32[]{:S(2)}, u32[]{:S(2)}) %all-to-all-start.1) | async-done | bytes 983072 | tf_op jit(solution)/shard_map/cond/branch_1_fun/all_to_all | solution.py:654
  100.3 0.9 branch_1_fun.11
  101.2 1.3 collective-permute-start.1
  102.5 0.9 collective-permute-done.1
  103.4 1.3 collective-permute-start.3
  104.7 1.3 collective-permute-start.2
  106.0 21.0 %collective-permute-done.2 = f32[80,256]{1,0:T(8,128)S(1)} collective-permute-done((f32[80,256]{1,0:T(8,128)S(1)}, f32[80,256]{1,0:T(8,128)S(1)}, u32[]{:S(2)}, u32[]{:S(2)}) %collective-permute-start.2) | collective-permute-done | bytes 81952 | tf_op jit(solution)/shard_map/ppermute | solution.py:650
  127.0 29.6 %conditional.7 = (f32[1,16,5,16,256]{4,3,2,1,0:T(8,128)}) conditional(s32[]{:T(128)} %convert_element_type.57, f32[16,5,16,256]{3,2,1,0:T(8,128)} %get-tuple-element.115, (s32[10,96]{1,0:T(8,128)S(1)}, f32[80,256]{1,0:T(8,128)S(1)}, f32[16,5,16,256]{3,2,1,0:T(8,128)}, f32[6,80,256]{2,1,0:T(8,128)S(1)}, f32[6,16,256]{2,1,0:T(8,128)S(1)}, ...), branch_computations={%region_19.20_spmd, %region_20.21_spmd} | conditional | bytes 5103112 | solution.py:876
  127.1 0.9 branch_1_fun.12
  128.0 20.9 %all_to_all.12.recv_ref = f32[16,120,128]{2,1,0:T(8,128)S(1)} all-to-all(f32[16,120,128]{2,1,0:T(8,128)S(1)} %branch_1_fun.12), channel_id=1, replica_groups=mesh['level'=2,'blk'=16] {'blk'}, dimensions={0} | all-to-all | bytes 1966080 | tf_op jit(solution)/shard_map/cond/branch_1_fun/all_to_all | solution.py:654
  148.9 7.8 %branch_1_fun.13 = f32[16,5,16,256]{3,2,1,0:T(8,128)} custom-call(s32[10,96]{1,0:T(8,128)S(1)} %get-tuple-element.91.tab_ref, f32[16,5,16,256]{3,2,1,0:T(8,128)} %get-tuple-element.92.new_ref, f32[6,80,256]{2,1,0:T(8,128)S(1)} %get-tuple-element.93.face_ref, f32[6,16,256]{2,1,0:T(8,128)S(1)} %get-tuple-element.94.mask_ref, ...), custom_call_target="tpu_custom_call" | custom-call | bytes 3051264 | tf_op jit(solution)/shard_map/cond/branch_1_fun/pallas_call | solution.py:635
  (71 shorter events, 4.7 us)
Async XLA Ops:
  0.0 1.5 copy-start
  3.2 4.2 %copy-start.1 = (f32[1,16,5,16,256]{4,3,2,1,0:T(8,128)S(1)}, f32[1,16,5,16,256]{4,3,2,1,0:T(8,128)}, u32[]{:S(2)}) copy-start(f32[1,16,5,16,256]{4,3,2,1,0:T(8,128)} %param.11) | copy-start | bytes 3932164
  22.4 32.7 %all-to-all-start = ((f32[16,240,128]{2,1,0:T(8,128)}), f32[16,240,128]{2,1,0:T(8,128)}, u32[]{:S(2)}, u32[]{:S(2)}) async-start(f32[16,240,128]{2,1,0:T(8,128)} %branch_1_fun.8), calls=%async_computation | async-start | bytes 3932160 | tf_op jit(solution)/shard_map/cond/branch_1_fun/all_to_all | solution.py:654
  56.8 3.2 %collective-permute-start = (f32[80,256]{1,0:T(8,128)S(1)}, f32[80,256]{1,0:T(8,128)S(1)}, u32[]{:S(2)}, u32[]{:S(2)}) collective-permute-start(f32[80,256]{1,0:T(8,128)S(1)} %get-tuple-element.109), channel_id=1, source_target_pairs={{0,16},{1,17},{2,18},{3,19},{4,20},{5,21},{6,22},{7,23},{8,24},{9,... | collective-permute-start | bytes 245768 | tf_op jit(solution)/shard_map/ppermute | solution.py:650
  78.2 22.1 %all-to-all-start.1 = ((f32[16,120,128]{2,1,0:T(8,128)}), f32[16,120,128]{2,1,0:T(8,128)S(1)}, u32[]{:S(2)}, u32[]{:S(2)}) async-start(f32[16,120,128]{2,1,0:T(8,128)} %get-tuple-element.79), calls=%async_computation.1 | async-start | bytes 1966080 | tf_op jit(solution)/shard_map/cond/branch_1_fun/all_to_all | solution.py:654
  101.2 2.2 %collective-permute-start.1 = (f32[80,256]{1,0:T(8,128)S(1)}, f32[80,256]{1,0:T(8,128)S(1)}, u32[]{:S(2)}, u32[]{:S(2)}) collective-permute-start(f32[80,256]{1,0:T(8,128)S(1)} %get-tuple-element.113), channel_id=1, source_target_pairs={{0,16},{1,17},{2,18},{3,19},{4,20},{5,21},{6,22},{7,23},{8,24},{9,... | collective-permute-start | bytes 245768 | tf_op jit(solution)/shard_map/ppermute | solution.py:650
  103.4 23.6 %collective-permute-start.3 = (f32[2,5,16,256]{3,2,1,0:T(8,128)S(1)}, f32[2,5,16,256]{3,2,1,0:T(8,128)S(1)}, u32[]{:S(2)}, u32[]{:S(2)}) collective-permute-start(f32[2,5,16,256]{3,2,1,0:T(8,128)S(1)} %get-tuple-element.118), channel_id=1, source_target_pairs={{16,0},{17,1},{18,2},{19,3},{20,4},{21,5},{22,6},{23,7},{24,8},{25... | collective-permute-start | bytes 491528 | tf_op jit(solution)/shard_map/ppermute | solution.py:650
  104.7 22.3 %collective-permute-start.2 = (f32[80,256]{1,0:T(8,128)S(1)}, f32[80,256]{1,0:T(8,128)S(1)}, u32[]{:S(2)}, u32[]{:S(2)}) collective-permute-start(f32[80,256]{1,0:T(8,128)S(1)} %get-tuple-element.116), channel_id=1, source_target_pairs={{16,0},{17,1},{18,2},{19,3},{20,4},{21,5},{22,6},{23,7},{24,8},{25... | collective-permute-start | bytes 245768 | tf_op jit(solution)/shard_map/ppermute | solution.py:650

commit v2 on v1

v2 whole, which is shorter than its diff:
```python
import functools
import math

import jax
import jax.numpy as jnp
from jax import lax
from jax.experimental import pallas as pl
from jax.experimental.pallas import tpu as pltpu
from jax.sharding import PartitionSpec as P

GAS_GAMMA = 1.4
STEP_RATIO = 0.12
BIT_OF = (4, 2, 1)
TANGENT = ((2, 1), (4, 1), (4, 2))
F32 = jnp.float32
I32 = jnp.int32
SPARE = 8 * 1024 * 1024
LANES = 128
ROWS = 8


def iota(shape, dim):
    return lax.broadcasted_iota(I32, shape, dim)


def reciprocal(x):
    return pltpu.reciprocal(x, approx=True)


def exact_dot(a, b):
    return jnp.dot(a, b, precision=lax.Precision.HIGHEST, preferred_element_type=F32)


def physical_flux(s, n):
    inv = reciprocal(s[0])
    vn = s[n] * inv
    kinetic = s[1] * s[1] + s[2] * s[2] + s[3] * s[3]
    p = (GAS_GAMMA - 1.0) * (s[4] - 0.5 * (kinetic * inv))
    out = [s[n], s[1] * vn, s[2] * vn, s[3] * vn, (s[4] + p) * vn]
    out[n] = out[n] + p
    return out


def evolve(u, below, above, n):
    low = []
    high = []
    for c in range(5):
        d = jnp.maximum(jnp.minimum(below[c], above[c]), 0.0) + jnp.minimum(
            jnp.maximum(below[c], above[c]), 0.0
        )
        d = 0.5 * d
        low.append(u[c] - d)
        high.append(u[c] + d)
    fl = physical_flux(low, n)
    fh = physical_flux(high, n)
    for c in range(5):
        change = (0.5 * STEP_RATIO) * (fl[c] - fh[c])
        low[c] = low[c] + change
        high[c] = high[c] + change
    return low, high


def side_values(s, n):
    inv = reciprocal(s[0])
    vn = s[n] * inv
    kinetic = s[1] * s[1] + s[2] * s[2] + s[3] * s[3]
    p = (GAS_GAMMA - 1.0) * (s[4] - 0.5 * (kinetic * inv))
    square = GAS_GAMMA * p * inv
    sound = square * lax.rsqrt(square)
    return vn, p, sound


def hllc(a, b, n):
    va, pa, ca = side_values(a, n)
    vb, pb, cb = side_values(b, n)
    slow = jnp.minimum(va - ca, vb - cb)
    fast = jnp.maximum(va + ca, vb + cb)
    qa = a[0] * (slow - va)
    qb = b[0] * (fast - vb)
    contact = (pb - pa + va * qa - vb * qb) * reciprocal(qa - qb)
    is_low = contact >= 0.0

    def pick(x, y):
        return jnp.where(is_low, x, y)

    s = [pick(a[c], b[c]) for c in range(5)]
    v = pick(va, vb)
    p = pick(pa, pb)
    q = pick(qa, qb)
    speed = pick(slow, fast)
    clipped = pick(jnp.minimum(slow, 0.0), jnp.maximum(fast, 0.0))
    extra = clipped * (contact - v) * reciprocal(speed - contact)
    h = v + extra
    push = extra * q
    out = [s[0] * h, s[1] * h, s[2] * h, s[3] * h, (s[4] + p) * h + push * contact]
    out[n] = out[n] + p + push
    return out


def lane_of():
    return iota((ROWS, LANES), 1)


def row_of():
    return iota((ROWS, LANES), 0)


def take_lanes(v, index):
    return jnp.take_along_axis(v, index, axis=1, mode="promise_in_bounds")


def slide_groups(tiles, edge):
    group = lane_of() // edge
    for bit in (1, 2, 4):
        moves = (group & bit) != 0
        tiles = [jnp.where(moves, pltpu.roll(g, bit, 0), g) for g in tiles]
    return tiles


def swap_front(tiles, edge, skews):
    base = lane_of() + edge * row_of()
    return slide_groups(
        [take_lanes(v, (base + skew) % LANES) for v, skew in zip(tiles, skews)], edge
    )


def swap_back_index(lane, edge):
    return edge * ((row_of() - lane // edge + ROWS) % ROWS) + lane % edge


def extract(u_ref, plane_ref, layers, nb, edge):
    groups = LANES // edge
    for side in range(2):
        for layer in range(layers):
            x = layer if side == 0 else edge - 1 - layer
            for c in range(5):
                for half in range(2):
                    at = (layer * 2 + half) * nb
                    plane_ref[side, c, at : at + nb, :] = u_ref[
                        :, c, x, half * LANES : (half + 1) * LANES
                    ]
    lane = lane_of()
    row = row_of()
    grp = lane // edge
    sub = lane % edge
    zero = jnp.zeros((ROWS, LANES), F32)
    offsets = [o for layer in range(layers) for o in (layer, edge - 1 - layer)]

    def rows_at(layer, rt, h):
        at = (layer * 2 + rt) * nb + h * ROWS
        return slice(at, at + ROWS)

    def gather(c, carry):
        for rt in range(2):
            rows = slice(rt * ROWS, (rt + 1) * ROWS)
            ylow = [[zero, zero] for _ in range(layers)]
            yhigh = [[zero, zero] for _ in range(layers)]
            for b in range(nb):
                t = b // groups
                turn = edge * b % LANES
                low = u_ref[b, c, rows, :LANES]
                high = u_ref[b, c, rows, LANES:]
                low = pltpu.roll(low, turn, 1) if turn else low
                high = pltpu.roll(high, turn, 1) if turn else high
                for layer in range(layers):
                    ylow[layer][t] = jnp.where(grp == (b + layer) % groups, low, ylow[layer][t])
                    yhigh[layer][t] = jnp.where(
                        grp == (b + groups - 1 - layer) % groups, high, yhigh[layer][t]
                    )
            for layer in range(layers):
                for h in range(2):
                    plane_ref[2, c, rows_at(layer, rt, h), :] = ylow[layer][h]
                    plane_ref[3, c, rows_at(layer, rt, h), :] = yhigh[layer][h]
            for h in range(2):
                zacc = {o: zero for o in offsets}
                for b in range(nb):
                    r = u_ref[b, c, rows, h * LANES : (h + 1) * LANES]
                    r = pltpu.roll(r, b, 1) if b else r
                    for o in offsets:
                        zacc[o] = jnp.where(sub == (b + o) % edge, r, zacc[o])
                for layer in range(layers):
                    plane_ref[4, c, rows_at(layer, rt, h), :] = zacc[layer]
                    plane_ref[5, c, rows_at(layer, rt, h), :] = zacc[edge - 1 - layer]
        return carry

    lax.fori_loop(0, 5, gather, 0)

    def turn(c, carry):
        last = swap_back_index(lane, edge)
        places = [
            (face, rows_at(layer, rt, h), skew)
            for layer in range(layers)
            for face, skew in ((2, edge * layer), (3, edge * (groups - 1 - layer)))
            for rt in range(2)
            for h in range(2)
        ]
        tiles = swap_front(
            [plane_ref[face, c, at, :] for face, at, _ in places], edge, [p[2] for p in places]
        )
        tiles = [take_lanes(v, last) for v in tiles]
        for (face, at, _), v in zip(places, tiles):
            plane_ref[face, c, at, :] = v
        places = []
        tiles = []
        for layer in range(layers):
            for face, o in ((4, layer), (5, edge - 1 - layer)):
                for rt in range(2):
                    raw = [plane_ref[face, c, rows_at(layer, rt, h), :] for h in range(2)]
                    for h in range(2):
                        index = (edge * (sub % ROWS) + ROWS * h + (grp + row) % ROWS + o) % LANES
                        tiles.append([take_lanes(v, index) for v in raw])
                        places.append((face, rows_at(layer, rt, h)))
        tiles = slide_groups([jnp.where(sub < ROWS, v, w) for v, w in tiles], edge)
        tiles = [take_lanes(v, last) for v in tiles]
        for (face, at), v in zip(places, tiles):
            plane_ref[face, c, at, :] = v
        return carry

    lax.fori_loop(0, 5, turn, 0)


def expand_add(base_ref, add_ref, out_ref, layers, nb, edge):
    groups = LANES // edge
    lane = lane_of()
    row = row_of()
    grp = lane // edge
    sub = lane % edge

    def rows_at(layer, rt, h):
        at = (layer * 2 + rt) * nb + h * ROWS
        return slice(at, at + ROWS)

    def turn(c, carry):
        places = [
            (face, layer, rt, skew)
            for layer in range(layers)
            for face, skew in (
                (2, edge * layer),
                (3, (LANES - edge * layer) % LANES),
                (4, layer),
                (5, edge - 1 - layer),
            )
            for rt in range(2)
        ]
        loaded = [
            add_ref[face, c, rows_at(layer, rt, h), :]
            for face, layer, rt, _ in places
            for h in range(2)
        ]
        mid = swap_front(loaded, edge, [0] * len(loaded))
        out = []
        for k, (face, layer, rt, skew) in enumerate(places):
            moved = (lane - skew + LANES) % LANES
            pair = mid[2 * k : 2 * k + 2]
            if face < 4:
                index = swap_back_index(moved, edge)
                out.append([take_lanes(v, index) for v in pair])
            else:
                block = moved % edge
                base = edge * ((row - block % ROWS + ROWS) % ROWS) + moved // edge
                parts = [[take_lanes(v, base + ROWS * h) for v in pair] for h in range(2)]
                out.append([jnp.where(block < ROWS, v, w) for v, w in parts])
        for (face, layer, rt, _), pair in zip(places, out):
            for h in range(2):
                add_ref[face, c, rows_at(layer, rt, h), :] = pair[h]
        return carry

    lax.fori_loop(0, 5, turn, 0)

    def spread(c, carry):
        for rt in range(2):
            rows = slice(rt * ROWS, (rt + 1) * ROWS)

            def tile(face, h):
                return [add_ref[face, c, rows_at(layer, rt, h), :] for layer in range(layers)]

            ylow = [tile(2, h) for h in range(2)]
            yhigh = [tile(3, h) for h in range(2)]
            zlow = [tile(4, h) for h in range(2)]
            zhigh = [tile(5, h) for h in range(2)]
            for b in range(nb):
                t = b // groups
                place = b % groups
                low = ylow[t][0]
                high = yhigh[t][0]
                if layers > 1:
                    low = jnp.where(grp == place, low, ylow[t][1])
                    high = jnp.where(grp == place, high, yhigh[t][1])
                low = pltpu.roll(low, (LANES - edge * place) % LANES, 1)
                high = pltpu.roll(high, edge * (groups - 1 - place) % LANES, 1)
                parts = [
                    jnp.where(grp < layers, low, 0.0),
                    jnp.where(grp >= groups - layers, high, 0.0),
                ]
                for h in range(2):
                    lanes = slice(h * LANES, (h + 1) * LANES)
                    z = zhigh[h][0]
                    if layers > 1:
                        z = jnp.where(sub == (b + edge - 1) % edge, z, zhigh[h][1])
                        z = jnp.where(sub == (b + 1) % edge, zlow[h][1], z)
                    z = jnp.where(sub == b, zlow[h][0], z)
                    if b:
                        z = pltpu.roll(z, LANES - b, 1)
                    total = parts[h] + jnp.where((sub < layers) | (sub >= edge - layers), z, 0.0)
                    x = add_ref[rt, c, h * nb + b : h * nb + b + 1, :]
                    x = jnp.where(row == (ROWS - 1) * rt, x, 0.0)
                    if layers > 1:
                        deeper = add_ref[rt, c, (2 + h) * nb + b : (2 + h) * nb + b + 1, :]
                        x = jnp.where(row == 1 + (ROWS - 3) * rt, deeper, x)
                    out_ref[b, c, rows, lanes] = base_ref[b, c, rows, lanes] + (total + x)
        return carry

    lax.fori_loop(0, 5, spread, 0)


def block_rows(block, nb, count):
    return pl.ds(block, count, stride=nb)


def pack(tab_ref, valid_row, slot_row, plane_ref, send_ref, count, nb):
    for face in range(6):
        for block in range(nb):
            item = block * 6 + face

            def move(item=item, face=face, block=block):
                target = tab_ref[0, item]
                first = tab_ref[slot_row, item] * 5
                for c in range(5):
                    send_ref[target, first + c] = plane_ref[
                        face, c, block_rows(block, nb, count), :
                    ]

            if valid_row is None:
                move()
            else:
                pl.when(tab_ref[valid_row, item] > 0)(move)


def unpack(tab_ref, valid_row, slot_row, recv_ref, plane_ref, count, nb):
    for face in range(6):
        for block in range(nb):
            item = block * 6 + face

            def move(item=item, face=face, block=block):
                target = tab_ref[0, item]
                first = tab_ref[slot_row, item] * 5
                for c in range(5):
                    plane_ref[face, c, block_rows(block, nb, count), :] = recv_ref[
                        target, first + c
                    ]

            if valid_row is None:
                move()
            else:
                pl.when(tab_ref[valid_row, item] > 0)(move)


def take_rims(tab_ref, slot_row, recv_ref, rim_ref, parents_here):
    for face in range(6):
        for p in range(parents_here):
            item = tab_ref[9, p] * 6 + face
            target = tab_ref[0, item]
            first = tab_ref[slot_row, item] * 5
            for c in range(5):
                rim_ref[face, c, 2 * p : 2 * p + 2, :] = recv_ref[target, first + c, 0:2, :]


def interior(nb, edge, u_ref, d_ref):
    square = edge * edge

    def sweep(u, axis, index, size, step, dim):
        n = 1 + axis
        below = [x - pltpu.roll(x, step, dim) for x in u]
        above = [pltpu.roll(x, size - step, dim) for x in below]
        low, high = evolve(u, below, above, n)
        prev = [pltpu.roll(x, step, dim) for x in high]
        inside = (index >= 2) & (index <= edge - 2)
        flux = [jnp.where(inside, x, 0.0) for x in hllc(prev, low, n)]
        return [pltpu.roll(x, size - step, dim) - x for x in flux]

    def body(b, carry):
        for rt in range(edge // ROWS):
            rows = slice(rt * ROWS, (rt + 1) * ROWS)
            u = [u_ref[b, c, rows, :] for c in range(5)]
            div = sweep(u, 1, iota((ROWS, square), 1) // edge, square, edge, 1)
            for c in range(5):
                d_ref[b, c, rows, :] = u[c] - STEP_RATIO * div[c]
        for half in range(square // LANES):
            lanes = slice(half * LANES, (half + 1) * LANES)
            u = [u_ref[b, c, :, lanes] for c in range(5)]
            div = sweep(u, 0, iota((edge, LANES), 0), edge, 1, 0)
            more = sweep(u, 2, iota((edge, LANES), 1) % edge, LANES, 1, 1)
            for c in range(5):
                d_ref[b, c, :, lanes] = d_ref[b, c, :, lanes] - STEP_RATIO * (div[c] + more[c])
        return carry

    lax.fori_loop(0, nb, body, 0)


def face_fluxes(plane_ref, ghost_ref, add_ref, face_ref, nb):
    for face in range(6):
        axis = face // 2
        side = face % 2
        n = 1 + axis
        sign = 1.0 - 2.0 * side

        def body(half, carry):
            def rows(layer):
                return pl.ds(pl.multiple_of((layer * 2 + half) * nb, ROWS), nb)

            def load(ref, layer):
                return [ref[face, c, rows(layer), :] for c in range(5)]

            near, mid, deep = (load(plane_ref, layer) for layer in range(3))
            ghost, far = (load(ghost_ref, layer) for layer in range(2))

            def steps(a, b):
                return [sign * (y - x) for x, y in zip(a, b)]

            d0, d1, d2, d3 = steps(far, ghost), steps(ghost, near), steps(near, mid), steps(mid, deep)
            if side == 0:
                first = hllc(evolve(ghost, d0, d1, n)[1], evolve(near, d1, d2, n)[0], n)
                second = hllc(evolve(near, d1, d2, n)[1], evolve(mid, d2, d3, n)[0], n)
            else:
                first = hllc(evolve(near, d1, d2, n)[1], evolve(ghost, d0, d1, n)[0], n)
                second = hllc(evolve(mid, d2, d3, n)[1], evolve(near, d1, d2, n)[0], n)
            for c in range(5):
                face_ref[face, c, rows(0), :] = first[c]
                add_ref[face, c, rows(0), :] = (sign * STEP_RATIO) * (first[c] - second[c])
                add_ref[face, c, rows(1), :] = (sign * STEP_RATIO) * second[c]
            return carry

        lax.fori_loop(0, 2, body, 0)


def inner_kernel(nb, edge, u_ref, d_ref, plane_ref):
    extract(u_ref, plane_ref, 3, nb, edge)
    interior(nb, edge, u_ref, d_ref)


def send_kernel(nb, edge, tab_ref, u_ref, send_ref, plane_ref):
    extract(u_ref, plane_ref, 2, nb, edge)
    pack(tab_ref, None, 1, plane_ref, send_ref, 4, nb)


def coarse_kernel(
    nb, edge, parents_here, tab_ref, d_ref, plane_ref, recv_ref, new_ref, face_ref, send_ref,
    rim_ref, ghost_ref, add_ref, near_ref,
):
    take_rims(tab_ref, 2, recv_ref, rim_ref, parents_here)
    unpack(tab_ref, None, 2, recv_ref, ghost_ref, 4, nb)
    face_fluxes(plane_ref, ghost_ref, add_ref, face_ref, nb)
    expand_add(d_ref, add_ref, new_ref, 2, nb, edge)
    extract(new_ref, near_ref, 1, nb, edge)
    pack(tab_ref, 3, 5, near_ref, send_ref, 2, nb)


def rims_kernel(parents_here, tab_ref, recv_ref, rim_ref):
    take_rims(tab_ref, 6, recv_ref, rim_ref, parents_here)


def fine_ghosts(nb, edge, fam_ref, bits_ref, plane_ref, rim_ref, rim2_ref, ghost_ref, parents_here):
    lane = lane_of()
    for face in range(6):
        axis = face // 2
        side = face % 2
        opposite = face + 1 - 2 * side
        for block in range(nb):
            sibling = fam_ref[2 + axis, block]
            for c in range(5):
                ghost_ref[face, c, block_rows(block, nb, 4), :] = plane_ref[
                    opposite, c, block_rows(sibling, nb, 4), :
                ]
        for rt in range(nb // ROWS):
            octant = bits_ref[rt * ROWS : (rt + 1) * ROWS, :]
            slot = bits_ref[nb + rt * ROWS : nb + (rt + 1) * ROWS, :]
            outward = (octant // BIT_OF[axis]) % 2 == side
            first = (octant // TANGENT[axis][0]) % 2
            second = (octant // TANGENT[axis][1]) % 2
            which = 2 * slot + first
            for c in range(5):
                rims = rim_ref[face, c]
                if rim2_ref is not None:
                    rims = 0.5 * (rims + rim2_ref[face, c])
                source = jnp.broadcast_to(rims[0:1, :], (ROWS, LANES))
                for k in range(1, 2 * parents_here):
                    source = jnp.where(which == k, rims[k : k + 1, :], source)
                for half in range(2):
                    index = (
                        edge * ((edge // 4) * half + lane // edge // 2)
                        + (edge // 2) * second
                        + lane % edge // 2
                    )
                    outer = take_lanes(source, index)
                    for layer in range(2):
                        at = (layer * 2 + half) * nb + rt * ROWS
                        at = slice(at, at + ROWS)
                        ghost_ref[face, c, at, :] = jnp.where(
                            outward, outer, ghost_ref[face, c, at, :]
                        )


def fine_kernel(
    nb, edge, parents_here, fam_ref, bits_ref, d_ref, plane_ref, rim_ref, new_ref, face_ref,
    ghost_ref, add_ref,
):
    fine_ghosts(nb, edge, fam_ref, bits_ref, plane_ref, rim_ref, None, ghost_ref, parents_here)
    face_fluxes(plane_ref, ghost_ref, add_ref, face_ref, nb)
    expand_add(d_ref, add_ref, new_ref, 2, nb, edge)


def face_means(nb, edge, parents_here, fam_ref, one_ref, two_ref, mean_ref, quarter_ref):
    lane = lane_of()
    group = lane // edge
    sub = lane % edge
    index = edge * (2 * (group % (ROWS // 2))) + 2 * (sub % (edge // 2))
    for face in range(6):
        places = [
            (c, slice(half * nb + rt * ROWS, half * nb + (rt + 1) * ROWS))
            for c in range(5)
            for rt in range(nb // ROWS)
            for half in range(2)
        ]
        tiles = [one_ref[face, c, at, :] + two_ref[face, c, at, :] for c, at in places]
        tiles = [v + pltpu.roll(v, LANES - 1, 1) for v in tiles]
        tiles = [v + pltpu.roll(v, LANES - edge, 1) for v in tiles]
        tiles = [0.125 * take_lanes(v, index) for v in tiles]
        for k in range(0, len(tiles), 2):
            at = k // 2 * ROWS
            quarter_ref[face, at : at + ROWS, :] = jnp.where(
                group < ROWS // 2, tiles[k], tiles[k + 1]
            )
    left = iota((5, LANES), 1) % edge < edge // 2
    for face in range(6):
        axis = face // 2
        for p in range(parents_here):
            for half in range(2):
                octant = (face % 2) * BIT_OF[axis] + half * TANGENT[axis][0]
                one = fam_ref[5 + p, octant]
                two = fam_ref[5 + p, octant + TANGENT[axis][1]]
                value = jnp.where(
                    left,
                    quarter_ref[face, pl.ds(one, 5, stride=nb), :],
                    quarter_ref[face, pl.ds(two, 5, stride=nb), :],
                )
                for c in range(5):
                    mean_ref[face, c, 2 * p + half : 2 * p + half + 1, :] = value[c : c + 1, :]


def last_fine_kernel(
    nb, edge, parents_here, fam_ref, bits_ref, d_ref, plane_ref, rim_ref, rim2_ref, one_ref,
    new_ref, mean_ref, ghost_ref, add_ref, face_ref, quarter_ref,
):
    fine_ghosts(nb, edge, fam_ref, bits_ref, plane_ref, rim_ref, rim2_ref, ghost_ref, parents_here)
    face_fluxes(plane_ref, ghost_ref, add_ref, face_ref, nb)
    face_means(nb, edge, parents_here, fam_ref, one_ref, face_ref, mean_ref, quarter_ref)
    expand_add(d_ref, add_ref, new_ref, 2, nb, edge)


def averages_kernel(nb, edge, family_ref, u_ref, out_ref):
    square = edge * edge
    half = edge // 2
    i = iota((square, LANES), 0)
    pairs = jnp.where(
        iota((square, LANES), 1) == (i // edge // 2) * edge + (i % edge) // 2, 0.125, 0.0
    ).astype(F32)
    i = iota((5 * half, 5 * edge), 0)
    j = iota((5 * half, 5 * edge), 1)
    rows = jnp.where(j // 2 == i, 1.0, 0.0).astype(F32)
    high = (iota((5 * half, LANES), 1) % edge) // half
    out_ref[...] = jnp.zeros(out_ref.shape, F32)

    def body(b, carry):
        octant = family_ref[0, b]
        p = family_ref[1, b]
        oz = octant % 2
        u = u_ref[b].reshape(5 * edge, square)
        v = exact_dot(rows, exact_dot(u, pairs))
        v = jnp.where(high == oz, pltpu.roll(v, half * oz, 1), 0.0)
        lanes = pl.ds(pl.multiple_of((octant // 2 % 2) * LANES, LANES), LANES)
        at = pl.ds(pl.multiple_of((octant // 4) * ROWS, ROWS), ROWS)
        for c in range(5):
            out_ref[p, c, at, lanes] = out_ref[p, c, at, lanes] + v[c * half : (c + 1) * half, :]
        return carry

    lax.fori_loop(0, nb, body, 0)


def return_kernel(parents_here, tab_ref, mean_ref, send_ref):
    for face in range(6):
        for p in range(parents_here):
            item = tab_ref[9, p] * 6 + face
            target = tab_ref[0, item]
            first = tab_ref[7, item] * 5
            for c in range(5):
                send_ref[target, first + c] = mean_ref[face, c, 2 * p : 2 * p + 2, :]


def correct_kernel(
    nb, edge, parents_here, tab_ref, bits_ref, new_ref, face_ref, recv_ref, cells_ref, out_ref,
    mean_ref, add_ref, base_ref,
):
    unpack(tab_ref, 3, 8, recv_ref, mean_ref, 2, nb)
    beside = bits_ref[2 * nb : 3 * nb, :]
    for face in range(6):
        sign = STEP_RATIO if face % 2 else -STEP_RATIO
        hit = (beside // (1 << face)) % 2 > 0
        for c in range(5):
            for half in range(2):
                at = slice(half * nb, (half + 1) * nb)
                add_ref[face, c, at, :] = jnp.where(
                    hit, sign * (face_ref[face, c, at, :] - mean_ref[face, c, at, :]), 0.0
                )
    base_ref[...] = new_ref[...]
    for p in range(parents_here):
        base_ref[tab_ref[9, p]] = cells_ref[p]
    expand_add(base_ref, add_ref, out_ref, 1, nb, edge)


def run(kernel, outs, operands, scratch=(), scalars=0, flops=0):
    single = isinstance(outs[0], int)
    shapes = [outs] if single else list(outs)
    held = [o.shape for o in operands] + shapes + list(scratch)
    limit = sum(4 * max(math.prod(s), 8 * LANES) for s in held) + SPARE
    smem = pl.BlockSpec(memory_space=pltpu.SMEM)
    vmem = pl.BlockSpec(memory_space=pltpu.VMEM)
    result = pl.pallas_call(
        kernel,
        out_shape=[jax.ShapeDtypeStruct(s, F32) for s in shapes],
        in_specs=[smem if k < scalars else vmem for k in range(len(operands))],
        out_specs=[vmem] * len(shapes),
        scratch_shapes=[pltpu.VMEM(s, F32) for s in scratch],
        compiler_params=pltpu.CompilerParams(vmem_limit_bytes=limit),
        cost_estimate=pl.CostEstimate(
            flops=flops, bytes_accessed=4 * sum(o.size for o in operands), transcendentals=0
        ),
    )(*operands)
    return result[0] if single else result


def blank(*shapes):
    return pl.pallas_call(
        lambda *refs: None,
        out_shape=[jax.ShapeDtypeStruct(s, F32) for s in shapes],
        out_specs=[pl.BlockSpec(memory_space=pl.ANY)] * len(shapes),
    )()


def level_shift(array, source):
    return lax.ppermute(array, "level", [(source, 1 - source)])


def route(buffer):
    return lax.all_to_all(buffer, "blk", split_axis=0, concat_axis=0, tiled=True)


def local(fluid_state, neighbours, parents):
    level_id = lax.axis_index("level")
    blk_index = lax.axis_index("blk")
    devices = lax.axis_size("blk")
    u = fluid_state[0]
    nb, _, edge, square = u.shape
    parents_here = nb // 8
    capacity = 2 * ((6 * nb + devices - 1) // devices)

    own_rows = lax.dynamic_slice_in_dim(neighbours, blk_index * nb, nb, 0)
    parent_rows = lax.dynamic_slice_in_dim(parents, blk_index * nb, nb, 0)
    parent_of = parent_rows[:, 0] - blk_index * nb
    octants = parent_rows[:, 1]
    beside = jnp.any(own_rows[:, :, None] == parents[None, None, :, 0], axis=2)
    is_parent = jnp.any(jnp.arange(nb)[:, None] == parent_of[None, :], axis=1)
    flat = own_rows.reshape(-1)
    items = jnp.arange(6 * nb, dtype=I32)
    targets = flat // nb
    faces = items % 6
    wanted = flat % nb * 6 + faces + 1 - 2 * (faces % 2)
    beside_item = beside.reshape(-1)
    parent_item = jnp.repeat(is_parent, 6)
    same = targets[:, None] == targets[None, :]
    by_own = same & (items[None, :] < items[:, None])
    by_wanted = same & (wanted[None, :] < wanted[:, None])

    def rank(order, mask=None):
        return jnp.sum(order if mask is None else order & mask[None, :], axis=1, dtype=I32)

    slot_of_block = jnp.sum(parent_of[None, :] < parent_of[:, None], axis=1, dtype=I32) // 8
    parent_list = jnp.sum(
        jnp.where(
            (slot_of_block[None, :] == jnp.arange(6 * nb)[:, None]) & (octants[None, :] == 0),
            parent_of[None, :],
            0,
        ),
        axis=1,
        dtype=I32,
    )
    table = jnp.stack(
        [
            targets,
            rank(by_own),
            rank(by_wanted),
            beside_item.astype(I32),
            parent_item.astype(I32),
            rank(by_own, beside_item),
            rank(by_wanted, parent_item),
            rank(by_own, parent_item),
            rank(by_wanted, beside_item),
            parent_list,
        ]
    )
    blocks = jnp.arange(nb, dtype=I32)
    family = [octants, slot_of_block]
    for axis in range(3):
        bit = BIT_OF[axis]
        partner = octants + bit - 2 * bit * (octants // bit % 2)
        match = (parent_of[:, None] == parent_of[None, :]) & (octants[None, :] == partner[:, None])
        family.append(jnp.sum(jnp.where(match, blocks[None, :], 0), axis=1, dtype=I32))
    for p in range(parents_here):
        match = (slot_of_block[None, :] == p) & (octants[None, :] == blocks[:, None])
        family.append(jnp.sum(jnp.where(match, blocks[None, :], 0), axis=1, dtype=I32))
    family = jnp.stack(family)
    beside_bits = jnp.sum(
        beside.astype(I32) * (1 << jnp.arange(6, dtype=I32))[None, :], axis=1, dtype=I32
    )
    bits = jnp.broadcast_to(
        jnp.concatenate([octants, slot_of_block, beside_bits])[:, None], (3 * nb, LANES)
    )

    part = functools.partial
    cell_shape = u.shape
    plane_shape = (6, 5, 6 * nb, LANES)
    ghost_shape = (6, 5, 4 * nb, LANES)
    face_shape = (6, 5, 2 * nb, LANES)
    rim_shape = (6, 5, 2 * parents_here, LANES)
    wide_send = (devices, capacity * 5, 4, LANES)
    thin_send = (devices, capacity * 5, 2, LANES)
    average_shape = (parents_here,) + cell_shape[1:]
    work = 220 * 3 * 5 * nb * edge * square

    def inner(cells):
        return run(part(inner_kernel, nb, edge), [cell_shape, plane_shape], [cells], flops=work)

    def coarse_first(u):
        send = run(part(send_kernel, nb, edge), wide_send, [table, u], [ghost_shape], 1)
        received = route(send)
        partial_new, planes = inner(u)
        cells, faces, send, rims = run(
            part(coarse_kernel, nb, edge, parents_here),
            [cell_shape, face_shape, thin_send, rim_shape],
            [table, partial_new, planes, received],
            [ghost_shape, ghost_shape, face_shape],
            1,
        )
        (unused,) = blank(plane_shape)
        return cells, faces, send, rims, unused

    def fine_first(u):
        partial_new, planes = inner(u)
        faces, send, rims = blank(face_shape, thin_send, rim_shape)
        return partial_new, faces, send, rims, planes

    cells, faces, send, rims, planes = lax.cond(level_id == 0, coarse_first, fine_first, u)
    early_rims = level_shift(rims, 0)

    def coarse_second(cells, send, planes, early_rims):
        late = run(
            part(rims_kernel, parents_here), rim_shape, [table, route(send)], (), 1
        )
        return (late, *blank(cell_shape, plane_shape, face_shape))

    def fine_second(cells, send, planes, early_rims):
        half, faces = run(
            part(fine_kernel, nb, edge, parents_here),
            [cell_shape, face_shape],
            [family, bits, cells, planes, early_rims],
            [ghost_shape, ghost_shape],
            1,
        )
        (late,) = blank(rim_shape)
        return (late, *inner(half), faces)

    late, half_cells, half_planes, half_faces = lax.cond(
        level_id == 0, coarse_second, fine_second, cells, send, planes, early_rims
    )
    late_rims = level_shift(late, 0)

    def coarse_third(half_cells, half_planes, half_faces, early_rims, late_rims):
        return tuple(blank(cell_shape, rim_shape))

    def fine_third(half_cells, half_planes, half_faces, early_rims, late_rims):
        return tuple(
            run(
                part(last_fine_kernel, nb, edge, parents_here),
                [cell_shape, rim_shape],
                [family, bits, half_cells, half_planes, early_rims, late_rims, half_faces],
                [ghost_shape, ghost_shape, face_shape, (6, 5 * nb, LANES)],
                1,
            )
        )

    out, means = lax.cond(
        level_id == 0, coarse_third, fine_third,
        half_cells, half_planes, half_faces, early_rims, late_rims,
    )
    means = level_shift(means, 1)

    def coarse_fourth(means, out):
        send = run(part(return_kernel, parents_here), thin_send, [table, means], (), 1)
        return route(send), blank(average_shape)[0]

    def fine_fourth(means, out):
        averages = run(part(averages_kernel, nb, edge), average_shape, [family, out], (), 1)
        return blank(thin_send)[0], averages

    returned, averages = lax.cond(level_id == 0, coarse_fourth, fine_fourth, means, out)
    averages = level_shift(averages, 1)

    def correct(out, cells, faces, returned, averages):
        return run(
            part(correct_kernel, nb, edge, parents_here),
            cell_shape,
            [table, bits, cells, faces, returned, averages],
            [face_shape, face_shape, cell_shape],
            1,
        )

    finished = lax.cond(
        level_id == 0, correct, lambda out, *rest: out, out, cells, faces, returned, averages
    )
    return finished[None]


def solution(mesh):
    return jax.shard_map(
        local,
        mesh=mesh,
        in_specs=(P("level", "blk", None, None, None), P(), P()),
        out_specs=P("level", "blk", None, None, None),
        check_vma=False,
    )
```

time: 157 us -> 121 us (0.77)
  Pallas kernels: 57.7 us -> 33.7 us
  blocking collectives: 20.9 us -> 0 us
  starting transfers between devices: 20.7 us -> 25.7 us
  waiting for transfers between devices: 49.2 us -> 52.2 us
    pallas_call x8 -> x6, Pallas kernels: 57.7 us -> 33.7 us  [run(): pl.pallas_call(kernel, out_shape=[jax.ShapeDtypeStruct(s, F32) for s in s...]
    all_to_all x1 -> x0, blocking collectives: 20.9 us -> none  [route(): lax.all_to_all(buffer, 'blk', split_axis=0, concat_axis=0, tiled=True)]
    all_to_all x2 -> x3, waiting for transfers between devices: 27.3 us -> 40.5 us  [route(): lax.all_to_all(buffer, 'blk', split_axis=0, concat_axis=0, tiled=True)]
    ppermute x4, waiting for transfers between devices: 21.9 us -> 11.7 us  [level_shift(): return lax.ppermute(array, 'level', [(source, 1 - source)])]
    all_to_all x2 -> x3, starting transfers between devices: 15.5 us -> 20.6 us  [route(): lax.all_to_all(buffer, 'blk', split_axis=0, concat_axis=0, tiled=True)]
    cond x2 -> x6, local copies, waits for them, and re-layouts: 2.48 us -> 3.64 us
  transfers between devices with their start and end apart: 6 -> 7, of which waited for: 4 -> 7; matrix products, arithmetic and copies ran while one was open for 3% -> 0% of each run, Pallas kernels for 6% -> 11%
where the time goes in v2:
time: 121 us
  waiting for transfers between devices  52.2 us (43%)
  Pallas kernels  33.7 us (28%)
  starting transfers between devices  25.7 us (21%)
  local copies, waits for them, and re-layouts  7.33 us (6%)
  other arithmetic  1.41 us (1%)
    all_to_all x3, waiting for transfers between devices, route(): lax.all_to_all(buffer, 'blk', split_axis=0, concat_axis=0, tiled=True)  40.5 us
    pallas_call x6, Pallas kernels, run(): pl.pallas_call(kernel, out_shape=[jax.ShapeDtypeStruct(s, F32) for s in s...  33.7 us
    all_to_all x3, starting transfers between devices, route(): lax.all_to_all(buffer, 'blk', split_axis=0, concat_axis=0, tiled=True)  20.6 us
    ppermute x4, waiting for transfers between devices, level_shift(): return lax.ppermute(array, 'level', [(source, 1 - source)])  11.7 us
    ppermute x4, starting transfers between devices, level_shift(): return lax.ppermute(array, 'level', [(source, 1 - source)])  5.13 us
    cond x6, local copies, waits for them, and re-layouts  3.64 us
  transfers between devices with their start and end apart: 7, of which 7 were waited for; matrix products, arithmetic and copies ran while one was open for 0% of the time, Pallas kernels for 11%

profile of v2, /device:TPU:0, one launch (start us, length us, event | category | flops | bytes accessed | tf_op | source)
XLA Modules:
  0.0 120.6 jit_solution(15230613575376262973)
XLA Ops:
  3.6 49.1 %conditional.5 = (f32[16,5,16,256]{3,2,1,0:T(8,128)}, f32[6,5,32,128]{3,2,1,0:T(8,128)}, f32[16,60,2,128]{3,2,1,0:T(2,128)}, f32[6,5,4,128]{3,2,1,0:T(4,128)}, f32[6,5,96,128]{3,2,1,0:T(8,128)}) conditional(s32[]{:T(128)} %convert_element_type.56, f32[16,5,16,256]{3,2,1,0:T(8,128)} %bitcast.37, (f32[16,5,16,256]{3,2,1,0:T(8,128)}, ...), branch_computations={%region_16.17_spmd, %region_17.18_spmd} | conditional | flops 216268800 | bytes 31628956 | solution.py:761
  3.6 4.1 %branch_1_fun.12 = f32[16,60,4,128]{3,2,1,0:T(4,128)S(1)} custom-call(s32[10,96]{1,0:T(8,128)S(1)} %get-tuple-element.84.tab_ref, f32[16,5,16,256]{3,2,1,0:T(8,128)} %get-tuple-element.85.u_ref), custom_call_target="tpu_custom_call" | custom-call | bytes 1314560 | tf_op jit(solution)/shard_map/cond/branch_1_fun/pallas_call | solution.py:627
  7.7 1.3 %copy-done.1 = f32[16,60,4,128]{3,2,1,0:T(4,128)} copy-done((f32[16,60,4,128]{3,2,1,0:T(4,128)}, f32[16,60,4,128]{3,2,1,0:T(4,128)S(1)}, u32[]{:S(2)}) %copy-start.1) | copy-done | bytes 1966104 | tf_op jit(solution)/shard_map/cond
  8.9 8.3 %all-to-all-start = ((f32[16,60,4,128]{3,2,1,0:T(4,128)}), f32[16,60,4,128]{3,2,1,0:T(4,128)S(1)}, u32[]{:S(2)}, u32[]{:S(2)}) async-start(f32[16,60,4,128]{3,2,1,0:T(4,128)} %copy-done.1), calls=%async_computation | async-start | bytes 3932160 | tf_op jit(solution)/shard_map/cond/branch_1_fun/all_to_all | solution.py:654
  17.3 12.7 %branch_1_fun.11 = (f32[16,5,16,256]{3,2,1,0:T(8,128)S(1)}, f32[6,5,96,128]{3,2,1,0:T(8,128)S(1)}) custom-call(f32[16,5,16,256]{3,2,1,0:T(8,128)} %get-tuple-element.85.u_ref), custom_call_target="tpu_custom_call" | custom-call | flops 216268800 | bytes 1310720 | tf_op jit(solution)/shard_map/cond/branch_1_fun/pallas_call | solution.py:627
  30.0 1.0 copy-done.2
  31.0 10.5 %all-to-all-done.recv_ref = f32[16,60,4,128]{3,2,1,0:T(4,128)S(1)} async-done(((f32[16,60,4,128]{3,2,1,0:T(4,128)}), f32[16,60,4,128]{3,2,1,0:T(4,128)S(1)}, u32[]{:S(2)}, u32[]{:S(2)}) %all-to-all-start) | async-done | bytes 1966112 | tf_op jit(solution)/shard_map/cond/branch_1_fun/all_to_all | solution.py:654
  41.5 1.3 %copy-done.3 = f32[16,5,16,256]{3,2,1,0:T(8,128)S(1)} copy-done((f32[16,5,16,256]{3,2,1,0:T(8,128)S(1)}, f32[16,5,16,256]{3,2,1,0:T(8,128)}, u32[]{:S(2)}) %copy-start.3) | copy-done | bytes 1310744 | tf_op jit(solution)/shard_map/cond
  42.8 9.8 %branch_1_fun.13 = (f32[16,5,16,256]{3,2,1,0:T(8,128)}, f32[6,5,32,128]{3,2,1,0:T(8,128)}, f32[16,60,2,128]{3,2,1,0:T(2,128)}, f32[6,5,4,128]{3,2,1,0:T(4,128)}) custom-call(s32[10,96]{1,0:T(8,128)S(1)} %get-tuple-element.84.tab_ref, f32[16,5,16,256]{3,2,1,0:T(8,128)S(1)} %copy-done.3, f32[6,5,96,128]{3,2,1,0:T(8,128)S(1)} %get-tuple-element.87.plane_ref, ...), custom_call_target="tpu_custom_call" | custom-call | bytes 4755200 | tf_op jit(solution)/shard_map/cond/branch_1_fun/pallas_call | solution.py:627
  52.6 1.3 %collective-permute-start = (f32[6,5,4,128]{3,2,1,0:T(4,128)}, f32[6,5,4,128]{3,2,1,0:T(4,128)S(1)}, u32[]{:S(2)}, u32[]{:S(2)}) collective-permute-start(f32[6,5,4,128]{3,2,1,0:T(4,128)} %get-tuple-element.142), channel_id=1, source_target_pairs={{0,16},{1,17},{2,18},{3,19},{4,20},{5,21},{6,22},{7,23},{8,24},{9,... | collective-permute-start | bytes 184328 | tf_op jit(solution)/shard_map/ppermute | solution.py:650
  55.1 22.8 %conditional.6 = (f32[6,5,4,128]{3,2,1,0:T(4,128)S(1)}, f32[16,5,16,256]{3,2,1,0:T(8,128)}, f32[6,5,96,128]{3,2,1,0:T(8,128)S(1)}, f32[6,5,32,128]{3,2,1,0:T(8,128)S(1)}) conditional(s32[]{:T(128)} %convert_element_type.56, (s32[7,16]{1,0:T(8,128)S(1)}, s32[48,128]{1,0:T(8,128)S(1)}, f32[16,5,16,256]{3,2,1,0:T(8,128)}, ...), branch_computations={%region_18.19_spmd, %region_19.20_spmd} | conditional | flops 216268800 | bytes 4182496 | solution.py:781
  55.1 7.1 %all-to-all-start.1 = ((f32[16,60,2,128]{3,2,1,0:T(2,128)}), f32[16,60,2,128]{3,2,1,0:T(2,128)S(1)}, u32[]{:S(2)}, u32[]{:S(2)}) async-start(f32[16,60,2,128]{3,2,1,0:T(2,128)} %get-tuple-element.102), calls=%async_computation.1 | async-start | bytes 1966080 | tf_op jit(solution)/shard_map/cond/branch_1_fun/all_to_all | solution.py:654
  62.2 15.0 %all-to-all-done.1.recv_ref = f32[16,60,2,128]{3,2,1,0:T(2,128)S(1)} async-done(((f32[16,60,2,128]{3,2,1,0:T(2,128)}), f32[16,60,2,128]{3,2,1,0:T(2,128)S(1)}, u32[]{:S(2)}, u32[]{:S(2)}) %all-to-all-start.1) | async-done | bytes 983072 | tf_op jit(solution)/shard_map/cond/branch_1_fun/all_to_all | solution.py:654
  77.9 1.3 %collective-permute-start.1 = (f32[6,5,4,128]{3,2,1,0:T(4,128)S(1)}, f32[6,5,4,128]{3,2,1,0:T(4,128)S(1)}, u32[]{:S(2)}, u32[]{:S(2)}) collective-permute-start(f32[6,5,4,128]{3,2,1,0:T(4,128)S(1)} %get-tuple-element.146), channel_id=1, source_target_pairs={{0,16},{1,17},{2,18},{3,19},{4,20},{5,21},{6,22},{7,23},{8,24},{9,... | collective-permute-start | bytes 184328 | tf_op jit(solution)/shard_map/ppermute | solution.py:650
  80.1 1.3 %collective-permute-start.2 = (f32[6,5,4,128]{3,2,1,0:T(4,128)S(1)}, f32[6,5,4,128]{3,2,1,0:T(4,128)S(1)}, u32[]{:S(2)}, u32[]{:S(2)}) collective-permute-start(f32[6,5,4,128]{3,2,1,0:T(4,128)S(1)} %get-tuple-element.150), channel_id=1, source_target_pairs={{16,0},{17,1},{18,2},{19,3},{20,4},{21,5},{22,6},{23,7},{24,8},{25... | collective-permute-start | bytes 184328 | tf_op jit(solution)/shard_map/ppermute | solution.py:650
  81.4 8.2 %collective-permute-done.2 = f32[6,5,4,128]{3,2,1,0:T(4,128)S(1)} collective-permute-done((f32[6,5,4,128]{3,2,1,0:T(4,128)S(1)}, f32[6,5,4,128]{3,2,1,0:T(4,128)S(1)}, u32[]{:S(2)}, u32[]{:S(2)}) %collective-permute-start.2) | collective-permute-done | bytes 61472 | tf_op jit(solution)/shard_map/ppermute | solution.py:650
  89.6 21.8 %conditional.8 = (f32[16,60,2,128]{3,2,1,0:T(2,128)}, f32[2,5,16,256]{3,2,1,0:T(8,128)S(1)}) conditional(s32[]{:T(128)} %convert_element_type.56, (s32[7,16]{1,0:T(8,128)S(1)}, f32[16,5,16,256]{3,2,1,0:T(8,128)S(1)}) %tuple.62, (s32[10,96]{1,0:T(8,128)S(1)}, f32[6,5,4,128]{3,2,1,0:T(4,128)S(1)}) %tuple.63), branch_computations={%region_22.23_spmd, %region_23.24_spmd} | conditional | bytes 3014448 | solution.py:814
  89.6 1.7 %branch_1_fun.17 = f32[16,60,2,128]{3,2,1,0:T(2,128)} custom-call(s32[10,96]{1,0:T(8,128)S(1)} %get-tuple-element.119.tab_ref, f32[6,5,4,128]{3,2,1,0:T(4,128)S(1)} %get-tuple-element.120.mean_ref), custom_call_target="tpu_custom_call" | custom-call | bytes 65280 | tf_op jit(solution)/shard_map/cond/branch_1_fun/pallas_call | solution.py:627
  91.3 5.1 %all-to-all-start.2 = ((f32[16,60,2,128]{3,2,1,0:T(2,128)}), f32[16,60,2,128]{3,2,1,0:T(2,128)}, u32[]{:S(2)}, u32[]{:S(2)}) async-start(f32[16,60,2,128]{3,2,1,0:T(2,128)} %branch_1_fun.17), calls=%async_computation.2 | async-start | bytes 1966080 | tf_op jit(solution)/shard_map/cond/branch_1_fun/all_to_all | solution.py:654
  96.4 15.0 %all-to-all-done.2 = f32[16,60,2,128]{3,2,1,0:T(2,128)} async-done(((f32[16,60,2,128]{3,2,1,0:T(2,128)}), f32[16,60,2,128]{3,2,1,0:T(2,128)}, u32[]{:S(2)}, u32[]{:S(2)}) %all-to-all-start.2) | async-done | bytes 983072 | tf_op jit(solution)/shard_map/cond/branch_1_fun/all_to_all | solution.py:654
  111.4 1.3 %collective-permute-start.3 = (f32[2,5,16,256]{3,2,1,0:T(8,128)S(1)}, f32[2,5,16,256]{3,2,1,0:T(8,128)S(1)}, u32[]{:S(2)}, u32[]{:S(2)}) collective-permute-start(f32[2,5,16,256]{3,2,1,0:T(8,128)S(1)} %get-tuple-element.152), channel_id=1, source_target_pairs={{16,0},{17,1},{18,2},{19,3},{20,4},{21,5},{22,6},{23,7},{24,8},{25... | collective-permute-start | bytes 491528 | tf_op jit(solution)/shard_map/ppermute | solution.py:650
  112.7 2.0 %collective-permute-done.3 = f32[2,5,16,256]{3,2,1,0:T(8,128)S(1)} collective-permute-done((f32[2,5,16,256]{3,2,1,0:T(8,128)S(1)}, f32[2,5,16,256]{3,2,1,0:T(8,128)S(1)}, u32[]{:S(2)}, u32[]{:S(2)}) %collective-permute-start.3) | collective-permute-done | bytes 163872 | tf_op jit(solution)/shard_map/ppermute | solution.py:650
  114.7 4.8 %conditional.9 = (f32[1,16,5,16,256]{4,3,2,1,0:T(8,128)S(1)}) conditional(s32[]{:T(128)} %convert_element_type.56, f32[16,5,16,256]{3,2,1,0:T(8,128)S(1)} %get-tuple-element.148, (s32[10,96]{1,0:T(8,128)S(1)}, s32[48,128]{1,0:T(8,128)S(1)}, f32[16,5,16,256]{3,2,1,0:T(8,128)}, f32[6,5,32,128]{3,2,1,0:T(8,128)}, f32[16,60,2,128]{3,2,1,0:T(2,128)}, ...), branch_computations={%region_24.25_spmd, %region_25.26_spmd} | conditional | bytes 2977544 | solution.py:826
  114.7 4.8 %branch_1_fun.19 = f32[16,5,16,256]{3,2,1,0:T(8,128)S(1)} custom-call(s32[10,96]{1,0:T(8,128)S(1)} %get-tuple-element.121.tab_ref, s32[48,128]{1,0:T(8,128)S(1)} %get-tuple-element.122.bits_ref, f32[16,5,16,256]{3,2,1,0:T(8,128)} %get-tuple-element.123.new_ref, f32[6,5,32,128]{3,2,1,0:T(8,128)} %get-tuple-element.124.face_ref, ...), custom_call_target="tpu_custom_call" | custom-call | bytes 2977536 | tf_op jit(solution)/shard_map/cond/branch_1_fun/pallas_call | solution.py:627
  (49 shorter events, 7.3 us)
Async XLA Ops:
  0.0 1.8 %copy-start = (s32[256,6]{0,1:T(8,128)S(1)}, s32[256,6]{0,1:T(8,128)}, u32[]{:S(2)}) copy-start(s32[256,6]{0,1:T(8,128)} %param.14) | copy-start | bytes 18436
  7.7 1.3 %copy-start.1 = (f32[16,60,4,128]{3,2,1,0:T(4,128)}, f32[16,60,4,128]{3,2,1,0:T(4,128)S(1)}, u32[]{:S(2)}) copy-start(f32[16,60,4,128]{3,2,1,0:T(4,128)S(1)} %branch_1_fun.12) | copy-start | bytes 5898244 | tf_op jit(solution)/shard_map/cond
  8.9 32.6 %all-to-all-start = ((f32[16,60,4,128]{3,2,1,0:T(4,128)}), f32[16,60,4,128]{3,2,1,0:T(4,128)S(1)}, u32[]{:S(2)}, u32[]{:S(2)}) async-start(f32[16,60,4,128]{3,2,1,0:T(4,128)} %copy-done.1), calls=%async_computation | async-start | bytes 3932160 | tf_op jit(solution)/shard_map/cond/branch_1_fun/all_to_all | solution.py:654
  30.0 1.1 copy-start.2
  41.5 1.3 %copy-start.3 = (f32[16,5,16,256]{3,2,1,0:T(8,128)S(1)}, f32[16,5,16,256]{3,2,1,0:T(8,128)}, u32[]{:S(2)}) copy-start(f32[16,5,16,256]{3,2,1,0:T(8,128)} %copy-done.2) | copy-start | bytes 3932164 | tf_op jit(solution)/shard_map/cond
  52.6 2.4 %collective-permute-start = (f32[6,5,4,128]{3,2,1,0:T(4,128)}, f32[6,5,4,128]{3,2,1,0:T(4,128)S(1)}, u32[]{:S(2)}, u32[]{:S(2)}) collective-permute-start(f32[6,5,4,128]{3,2,1,0:T(4,128)} %get-tuple-element.142), channel_id=1, source_target_pairs={{0,16},{1,17},{2,18},{3,19},{4,20},{5,21},{6,22},{7,23},{8,24},{9,... | collective-permute-start | bytes 184328 | tf_op jit(solution)/shard_map/ppermute | solution.py:650
  55.1 22.1 %all-to-all-start.1 = ((f32[16,60,2,128]{3,2,1,0:T(2,128)}), f32[16,60,2,128]{3,2,1,0:T(2,128)S(1)}, u32[]{:S(2)}, u32[]{:S(2)}) async-start(f32[16,60,2,128]{3,2,1,0:T(2,128)} %get-tuple-element.102), calls=%async_computation.1 | async-start | bytes 1966080 | tf_op jit(solution)/shard_map/cond/branch_1_fun/all_to_all | solution.py:654
  77.9 2.2 %collective-permute-start.1 = (f32[6,5,4,128]{3,2,1,0:T(4,128)S(1)}, f32[6,5,4,128]{3,2,1,0:T(4,128)S(1)}, u32[]{:S(2)}, u32[]{:S(2)}) collective-permute-start(f32[6,5,4,128]{3,2,1,0:T(4,128)S(1)} %get-tuple-element.146), channel_id=1, source_target_pairs={{0,16},{1,17},{2,18},{3,19},{4,20},{5,21},{6,22},{7,23},{8,24},{9,... | collective-permute-start | bytes 184328 | tf_op jit(solution)/shard_map/ppermute | solution.py:650
  80.1 9.5 %collective-permute-start.2 = (f32[6,5,4,128]{3,2,1,0:T(4,128)S(1)}, f32[6,5,4,128]{3,2,1,0:T(4,128)S(1)}, u32[]{:S(2)}, u32[]{:S(2)}) collective-permute-start(f32[6,5,4,128]{3,2,1,0:T(4,128)S(1)} %get-tuple-element.150), channel_id=1, source_target_pairs={{16,0},{17,1},{18,2},{19,3},{20,4},{21,5},{22,6},{23,7},{24,8},{25... | collective-permute-start | bytes 184328 | tf_op jit(solution)/shard_map/ppermute | solution.py:650
  91.3 20.2 %all-to-all-start.2 = ((f32[16,60,2,128]{3,2,1,0:T(2,128)}), f32[16,60,2,128]{3,2,1,0:T(2,128)}, u32[]{:S(2)}, u32[]{:S(2)}) async-start(f32[16,60,2,128]{3,2,1,0:T(2,128)} %branch_1_fun.17), calls=%async_computation.2 | async-start | bytes 1966080 | tf_op jit(solution)/shard_map/cond/branch_1_fun/all_to_all | solution.py:654
  111.4 3.3 %collective-permute-start.3 = (f32[2,5,16,256]{3,2,1,0:T(8,128)S(1)}, f32[2,5,16,256]{3,2,1,0:T(8,128)S(1)}, u32[]{:S(2)}, u32[]{:S(2)}) collective-permute-start(f32[2,5,16,256]{3,2,1,0:T(8,128)S(1)} %get-tuple-element.152), channel_id=1, source_target_pairs={{16,0},{17,1},{18,2},{19,3},{20,4},{21,5},{22,6},{23,7},{24,8},{25... | collective-permute-start | bytes 491528 | tf_op jit(solution)/shard_map/ppermute | solution.py:650
  119.5 1.1 copy-start.4

commit v3 on v2

--- a/solution.py
+++ b/solution.py
@@ -25,10 +25,6 @@
 
 def reciprocal(x):
     return pltpu.reciprocal(x, approx=True)
-
-
-def exact_dot(a, b):
-    return jnp.dot(a, b, precision=lax.Precision.HIGHEST, preferred_element_type=F32)
 
 
 def physical_flux(s, n):
@@ -219,7 +215,7 @@
     lax.fori_loop(0, 5, turn, 0)
 
 
-def expand_add(base_ref, add_ref, out_ref, layers, nb, edge):
+def expand_add(base_ref, add_ref, out_ref, layers, nb, edge, split_ref=None):
     groups = LANES // edge
     lane = lane_of()
     row = row_of()
@@ -307,7 +303,10 @@
                     if layers > 1:
                         deeper = add_ref[rt, c, (2 + h) * nb + b : (2 + h) * nb + b + 1, :]
                         x = jnp.where(row == 1 + (ROWS - 3) * rt, deeper, x)
-                    out_ref[b, c, rows, lanes] = base_ref[b, c, rows, lanes] + (total + x)
+                    value = base_ref[b, c, rows, lanes] + (total + x)
+                    out_ref[b, c, rows, lanes] = value
+                    if split_ref is not None:
+                        split_ref[b, c, h, rows, :] = value
         return carry
 
     lax.fori_loop(0, 5, spread, 0)
@@ -320,7 +319,7 @@
 def pack(tab_ref, valid_row, slot_row, plane_ref, send_ref, count, nb):
     for face in range(6):
         for block in range(nb):
-            item = block * 6 + face
+            item = face * nb + block
 
             def move(item=item, face=face, block=block):
                 target = tab_ref[0, item]
@@ -339,7 +338,7 @@
 def unpack(tab_ref, valid_row, slot_row, recv_ref, plane_ref, count, nb):
     for face in range(6):
         for block in range(nb):
-            item = block * 6 + face
+            item = face * nb + block
 
             def move(item=item, face=face, block=block):
                 target = tab_ref[0, item]
@@ -355,10 +354,46 @@
                 pl.when(tab_ref[valid_row, item] > 0)(move)
 
 
-def take_rims(tab_ref, slot_row, recv_ref, rim_ref, parents_here):
+def pack_wide(tab_ref, slots, plane_ref, send_ref, over_ref, nb):
+    for face in range(6):
+        for block in range(nb):
+            item = face * nb + block
+            slot = tab_ref[1, item]
+
+            def move(ref, first, face=face, block=block):
+                for c in range(5):
+                    ref[first + c] = plane_ref[face, c, block_rows(block, nb, 4), :]
+
+            target_ref = send_ref.at[tab_ref[0, item]]
+            if over_ref is None:
+                move(target_ref, slot * 5)
+            else:
+                pl.when(slot < slots)(functools.partial(move, target_ref, slot * 5))
+                pl.when(slot >= slots)(functools.partial(move, over_ref, (slot - slots) * 5))
+
+
+def unpack_wide(tab_ref, slots, recv_ref, over_ref, plane_ref, nb):
+    for face in range(6):
+        for block in range(nb):
+            item = face * nb + block
+            slot = tab_ref[2, item]
+
+            def move(ref, first, face=face, block=block):
+                for c in range(5):
+                    plane_ref[face, c, block_rows(block, nb, 4), :] = ref[first + c]
+
+            source_ref = recv_ref.at[tab_ref[0, item]]
+            if over_ref is None:
+                move(source_ref, slot * 5)
+            else:
+                pl.when(slot < slots)(functools.partial(move, source_ref, slot * 5))
+                pl.when(slot >= slots)(functools.partial(move, over_ref, (slot - slots) * 5))
+
+
+def take_rims(tab_ref, slot_row, recv_ref, rim_ref, parents_here, nb):
     for face in range(6):
         for p in range(parents_here):
-            item = tab_ref[9, p] * 6 + face
+            item = face * nb + tab_ref[9, p]
             target = tab_ref[0, item]
             first = tab_ref[slot_row, item] * 5
             for c in range(5):
@@ -438,35 +473,108 @@
     interior(nb, edge, u_ref, d_ref)
 
 
-def send_kernel(nb, edge, tab_ref, u_ref, send_ref, plane_ref):
+def coarse_inner_kernel(nb, edge, u_ref, d_ref, plane_ref, near_ref):
+    inner_kernel(nb, edge, u_ref, d_ref, plane_ref)
+    extract(d_ref, near_ref, 1, nb, edge)
+
+
+def send_kernel(nb, edge, slots, tab_ref, u_ref, send_ref, *refs):
+    *over_ref, plane_ref = refs
     extract(u_ref, plane_ref, 2, nb, edge)
-    pack(tab_ref, None, 1, plane_ref, send_ref, 4, nb)
-
-
-def coarse_kernel(
-    nb, edge, parents_here, tab_ref, d_ref, plane_ref, recv_ref, new_ref, face_ref, send_ref,
-    rim_ref, ghost_ref, add_ref, near_ref,
-):
-    take_rims(tab_ref, 2, recv_ref, rim_ref, parents_here)
-    unpack(tab_ref, None, 2, recv_ref, ghost_ref, 4, nb)
+    pack_wide(tab_ref, slots, plane_ref, send_ref, over_ref[0] if over_ref else None, nb)
+
+
+def near_layers(near_ref, add_ref, new_ref, nb, edge):
+    lane = lane_of()
+    group = lane // edge
+    sub = lane % edge
+    views = ((1, 2), (0, 2), (0, 1))
+
+    def rows_at(layer, half, rt):
+        at = (layer * 2 + half) * nb + rt * ROWS
+        return slice(at, at + ROWS)
+
+    def body(c, carry):
+        for face in range(6):
+            axis = face // 2
+            depth = 0 if face % 2 == 0 else edge - 1
+            for half in range(2):
+                tiles = []
+                for rt in range(nb // ROWS):
+                    at = rows_at(0, half, rt)
+                    tiles.append(near_ref[face, c, at, :] + add_ref[face, c, at, :])
+                for other in range(6):
+                    lateral = other // 2
+                    if lateral == axis:
+                        continue
+                    first = views[axis][0] == lateral
+                    along = sub if first else group + half * ROWS
+                    for layer in range(2):
+                        place = layer if other % 2 == 0 else edge - 1 - layer
+                        if first:
+                            if place // ROWS != half:
+                                continue
+                            hit = group == place % ROWS
+                        else:
+                            hit = sub == place
+                        for rt in range(nb // ROWS):
+                            if views[lateral][0] == axis:
+                                index = edge * (depth % ROWS) + along
+                                value = take_lanes(
+                                    add_ref[other, c, rows_at(layer, depth // ROWS, rt), :], index
+                                )
+                            elif first:
+                                index = edge * (along % ROWS) + depth
+                                value = jnp.where(
+                                    along < ROWS,
+                                    take_lanes(add_ref[other, c, rows_at(layer, 0, rt), :], index),
+                                    take_lanes(add_ref[other, c, rows_at(layer, 1, rt), :], index),
+                                )
+                            else:
+                                index = edge * group + depth
+                                value = take_lanes(
+                                    add_ref[other, c, rows_at(layer, half, rt), :], index
+                                )
+                            tiles[rt] = tiles[rt] + jnp.where(hit, value, 0.0)
+                for rt in range(nb // ROWS):
+                    new_ref[face, c, rows_at(0, half, rt), :] = tiles[rt]
+        return carry
+
+    lax.fori_loop(0, 5, body, 0)
+
+
+def coarse_kernel(nb, edge, parents_here, slots, tab_ref, plane_ref, near_ref, recv_ref, *refs):
+    *over_ref, add_ref, face_ref, send_ref, rim_ref, ghost_ref, new_ref = refs
+    unpack_wide(tab_ref, slots, recv_ref, over_ref[0] if over_ref else None, ghost_ref, nb)
+    for face in range(6):
+        for p in range(parents_here):
+            block = tab_ref[9, p]
+            for c in range(5):
+                rim_ref[face, c, 2 * p : 2 * p + 2, :] = ghost_ref[
+                    face, c, block_rows(block, nb, 2), :
+                ]
     face_fluxes(plane_ref, ghost_ref, add_ref, face_ref, nb)
-    expand_add(d_ref, add_ref, new_ref, 2, nb, edge)
-    extract(new_ref, near_ref, 1, nb, edge)
-    pack(tab_ref, 3, 5, near_ref, send_ref, 2, nb)
-
-
-def rims_kernel(parents_here, tab_ref, recv_ref, rim_ref):
-    take_rims(tab_ref, 6, recv_ref, rim_ref, parents_here)
-
-
-def fine_ghosts(nb, edge, fam_ref, bits_ref, plane_ref, rim_ref, rim2_ref, ghost_ref, parents_here):
+    near_layers(near_ref, add_ref, new_ref, nb, edge)
+    pack(tab_ref, 3, 5, new_ref, send_ref, 2, nb)
+
+
+def coarse_cells_kernel(nb, edge, d_ref, add_ref, new_ref, temp_ref):
+    temp_ref[...] = add_ref[...]
+    expand_add(d_ref, temp_ref, new_ref, 2, nb, edge)
+
+
+def rims_kernel(nb, parents_here, tab_ref, recv_ref, rim_ref):
+    take_rims(tab_ref, 6, recv_ref, rim_ref, parents_here, nb)
+
+
+def fine_ghosts(nb, edge, tab_ref, bits_ref, plane_ref, rim_ref, rim2_ref, ghost_ref, parents_here):
     lane = lane_of()
     for face in range(6):
         axis = face // 2
         side = face % 2
         opposite = face + 1 - 2 * side
         for block in range(nb):
-            sibling = fam_ref[2 + axis, block]
+            sibling = tab_ref[12 + axis, block]
             for c in range(5):
                 ghost_ref[face, c, block_rows(block, nb, 4), :] = plane_ref[
                     opposite, c, block_rows(sibling, nb, 4), :
@@ -501,15 +609,18 @@
 
 
 def fine_kernel(
-    nb, edge, parents_here, fam_ref, bits_ref, d_ref, plane_ref, rim_ref, new_ref, face_ref,
-    ghost_ref, add_ref,
+    nb, edge, parents_here, tab_ref, bits_ref, d_ref, plane_ref, rim_ref, new_ref, face_ref,
+    ghost_ref, add_ref, base_ref, sem,
 ):
-    fine_ghosts(nb, edge, fam_ref, bits_ref, plane_ref, rim_ref, None, ghost_ref, parents_here)
+    fetch = pltpu.make_async_copy(d_ref, base_ref, sem)
+    fetch.start()
+    fine_ghosts(nb, edge, tab_ref, bits_ref, plane_ref, rim_ref, None, ghost_ref, parents_here)
     face_fluxes(plane_ref, ghost_ref, add_ref, face_ref, nb)
-    expand_add(d_ref, add_ref, new_ref, 2, nb, edge)
-
-
-def face_means(nb, edge, parents_here, fam_ref, one_ref, two_ref, mean_ref, quarter_ref):
+    fetch.wait()
+    expand_add(base_ref, add_ref, new_ref, 2, nb, edge)
+
+
+def face_means(nb, edge, parents_here, tab_ref, one_ref, two_ref, mean_ref, quarter_ref):
     lane = lane_of()
     group = lane // edge
     sub = lane % edge
@@ -536,8 +647,8 @@
         for p in range(parents_here):
             for half in range(2):
                 octant = (face % 2) * BIT_OF[axis] + half * TANGENT[axis][0]
-                one = fam_ref[5 + p, octant]
-                two = fam_ref[5 + p, octant + TANGENT[axis][1]]
+                one = tab_ref[15 + p, octant]
+                two = tab_ref[15 + p, octant + TANGENT[axis][1]]
                 value = jnp.where(
                     left,
                     quarter_ref[face, pl.ds(one, 5, stride=nb), :],
@@ -547,59 +658,64 @@
                     mean_ref[face, c, 2 * p + half : 2 * p + half + 1, :] = value[c : c + 1, :]
 
 
-def last_fine_kernel(
-    nb, edge, parents_here, fam_ref, bits_ref, d_ref, plane_ref, rim_ref, rim2_ref, one_ref,
-    new_ref, mean_ref, ghost_ref, add_ref, face_ref, quarter_ref,
+def means_kernel(
+    nb, edge, parents_here, tab_ref, bits_ref, plane_ref, rim_ref, rim2_ref, one_ref, send_ref,
+    add_ref, ghost_ref, face_ref, quarter_ref, mean_ref,
 ):
-    fine_ghosts(nb, edge, fam_ref, bits_ref, plane_ref, rim_ref, rim2_ref, ghost_ref, parents_here)
+    fine_ghosts(nb, edge, tab_ref, bits_ref, plane_ref, rim_ref, rim2_ref, ghost_ref, parents_here)
     face_fluxes(plane_ref, ghost_ref, add_ref, face_ref, nb)
-    face_means(nb, edge, parents_here, fam_ref, one_ref, face_ref, mean_ref, quarter_ref)
-    expand_add(d_ref, add_ref, new_ref, 2, nb, edge)
-
-
-def averages_kernel(nb, edge, family_ref, u_ref, out_ref):
-    square = edge * edge
-    half = edge // 2
-    i = iota((square, LANES), 0)
-    pairs = jnp.where(
-        iota((square, LANES), 1) == (i // edge // 2) * edge + (i % edge) // 2, 0.125, 0.0
-    ).astype(F32)
-    i = iota((5 * half, 5 * edge), 0)
-    j = iota((5 * half, 5 * edge), 1)
-    rows = jnp.where(j // 2 == i, 1.0, 0.0).astype(F32)
-    high = (iota((5 * half, LANES), 1) % edge) // half
-    out_ref[...] = jnp.zeros(out_ref.shape, F32)
-
-    def body(b, carry):
-        octant = family_ref[0, b]
-        p = family_ref[1, b]
-        oz = octant % 2
-        u = u_ref[b].reshape(5 * edge, square)
-        v = exact_dot(rows, exact_dot(u, pairs))
-        v = jnp.where(high == oz, pltpu.roll(v, half * oz, 1), 0.0)
-        lanes = pl.ds(pl.multiple_of((octant // 2 % 2) * LANES, LANES), LANES)
-        at = pl.ds(pl.multiple_of((octant // 4) * ROWS, ROWS), ROWS)
-        for c in range(5):
-            out_ref[p, c, at, lanes] = out_ref[p, c, at, lanes] + v[c * half : (c + 1) * half, :]
-        return carry
-
-    lax.fori_loop(0, nb, body, 0)
-
-
-def return_kernel(parents_here, tab_ref, mean_ref, send_ref):
+    face_means(nb, edge, parents_here, tab_ref, one_ref, face_ref, mean_ref, quarter_ref)
     for face in range(6):
         for p in range(parents_here):
-            item = tab_ref[9, p] * 6 + face
+            item = face * nb + tab_ref[9, p]
             target = tab_ref[0, item]
             first = tab_ref[7, item] * 5
             for c in range(5):
                 send_ref[target, first + c] = mean_ref[face, c, 2 * p : 2 * p + 2, :]
 
 
+def finish_kernel(
+    nb, edge, parents_here, tab_ref, d_ref, add_ref, new_ref, average_ref, temp_ref, split_ref,
+    eighth_ref,
+):
+    temp_ref[...] = add_ref[...]
+    expand_add(d_ref, temp_ref, new_ref, 2, nb, edge, split_ref)
+    averages(nb, edge, parents_here, tab_ref, split_ref, average_ref, eighth_ref)
+
+
+def averages(nb, edge, parents_here, tab_ref, split_ref, out_ref, eighth_ref):
+    lane = lane_of()
+    group = lane // edge
+    index = edge * (2 * (group % (ROWS // 2))) + 2 * (lane % (edge // 2))
+    for b in range(nb):
+        tiles = [
+            split_ref[b, c, h, pl.ds(0, ROWS, stride=2), :]
+            + split_ref[b, c, h, pl.ds(1, ROWS, stride=2), :]
+            for c in range(5)
+            for h in range(2)
+        ]
+        tiles = [v + pltpu.roll(v, LANES - 1, 1) for v in tiles]
+        tiles = [v + pltpu.roll(v, LANES - edge, 1) for v in tiles]
+        tiles = [0.125 * take_lanes(v, index) for v in tiles]
+        for c in range(5):
+            eighth_ref[b, c] = jnp.where(group < ROWS // 2, tiles[2 * c], tiles[2 * c + 1])
+    left = lane % edge < edge // 2
+    for p in range(parents_here):
+        for corner in range(4):
+            one = tab_ref[15 + p, 2 * corner]
+            two = tab_ref[15 + p, 2 * corner + 1]
+            rows = slice(corner // 2 * ROWS, (corner // 2 + 1) * ROWS)
+            lanes = slice(corner % 2 * LANES, (corner % 2 + 1) * LANES)
+            for c in range(5):
+                out_ref[p, c, rows, lanes] = jnp.where(left, eighth_ref[one, c], eighth_ref[two, c])
+
+
 def correct_kernel(
     nb, edge, parents_here, tab_ref, bits_ref, new_ref, face_ref, recv_ref, cells_ref, out_ref,
-    mean_ref, add_ref, base_ref,
+    mean_ref, add_ref, base_ref, sem,
 ):
+    fetch = pltpu.make_async_copy(new_ref, base_ref, sem)
+    fetch.start()
     unpack(tab_ref, 3, 8, recv_ref, mean_ref, 2, nb)
     beside = bits_ref[2 * nb : 3 * nb, :]
     for face in range(6):
@@ -611,31 +727,155 @@
                 add_ref[face, c, at, :] = jnp.where(
                     hit, sign * (face_ref[face, c, at, :] - mean_ref[face, c, at, :]), 0.0
                 )
-    base_ref[...] = new_ref[...]
+    fetch.wait()
     for p in range(parents_here):
         base_ref[tab_ref[9, p]] = cells_ref[p]
     expand_add(base_ref, add_ref, out_ref, 1, nb, edge)
 
 
-def run(kernel, outs, operands, scratch=(), scalars=0, flops=0):
-    single = isinstance(outs[0], int)
-    shapes = [outs] if single else list(outs)
-    held = [o.shape for o in operands] + shapes + list(scratch)
+def column(row):
+    return jnp.transpose(jnp.broadcast_to(row.astype(F32), (LANES, LANES)))
+
+
+def count(hits):
+    return jnp.sum(jnp.where(hits, 1.0, 0.0), axis=0, keepdims=True).astype(I32)
+
+
+def tables_kernel(
+    nb, devices, parents_here, blk_ref, all_near_ref, all_parent_ref, tab_ref, bits_ref, near_ref,
+    parent_ref, sems,
+):
+    fetches = [
+        pltpu.make_async_copy(all_near_ref, near_ref, sems.at[0]),
+        pltpu.make_async_copy(all_parent_ref, parent_ref, sems.at[1]),
+    ]
+    for fetch in fetches:
+        fetch.start()
+    for fetch in fetches:
+        fetch.wait()
+    total = near_ref.shape[1]
+    tiles = total // LANES
+    start = blk_ref[0] * nb
+    tile = pl.ds(pl.multiple_of(start // LANES * LANES, LANES), LANES)
+    turn = (LANES - start % LANES) % LANES
+    own = pltpu.roll(near_ref[:, tile], turn, 1)
+    own_parent = pltpu.roll(parent_ref[:, tile], turn, 1)
+    lane = iota((1, LANES), 1)
+    face = lane // nb
+    block = lane % nb
+    row = iota((LANES, LANES), 0)
+    near = jnp.zeros((1, LANES), I32)
+    for f in range(6):
+        near = jnp.where(face == f, pltpu.roll(own[f : f + 1, :], nb * f, 1), near)
+    target = near // nb
+    wanted = (face + 1 - 2 * (face % 2)) * nb + near % nb
+    wanted_f = wanted.astype(F32)
+    parent_columns = [
+        column(parent_ref[0:1, k * LANES : (k + 1) * LANES]) for k in range(tiles)
+    ]
+
+    def any_parent(ids):
+        ids = ids.astype(F32)
+        hits = [jnp.max(jnp.where(x == ids, 1.0, 0.0), axis=0, keepdims=True) for x in parent_columns]
+        return functools.reduce(jnp.maximum, hits)
+
+    beside = any_parent(near)
+    parent = own_parent[0:1, :] - start
+    octant = own_parent[1:2, :]
+    parent_column = column(parent)
+    octant_column = column(octant)
+    mine = row < nb
+    owned = jnp.max(
+        jnp.where(mine & (parent_column == block.astype(F32)), 1.0, 0.0), axis=0, keepdims=True
+    )
+    same = (column(target) == target.astype(F32)) & (row < 6 * nb)
+    by_own = same & (row < lane)
+    by_wanted = same & (column(wanted) < wanted_f)
+    beside_column = column(beside) > 0.0
+    owned_column = column(owned) > 0.0
+    parent_f = parent.astype(F32)
+    slot = count(mine & (parent_column < parent_f)) // 8
+    slot_column = column(slot)
+    row_f = row.astype(F32)
+    lane_f = lane.astype(F32)
+
+    def pick(hits, values):
+        return jnp.sum(jnp.where(mine & hits, values, 0.0), axis=0, keepdims=True).astype(I32)
+
+    rows = [
+        target,
+        count(by_own),
+        count(by_wanted),
+        beside.astype(I32),
+        owned.astype(I32),
+        count(by_own & beside_column),
+        count(by_wanted & owned_column),
+        count(by_own & owned_column),
+        count(by_wanted & beside_column),
+        pick((octant_column == 0.0) & (slot_column == lane_f), parent_column),
+        octant,
+        slot,
+    ]
+    for bit in BIT_OF:
+        partner = (octant + bit - 2 * bit * (octant // bit % 2)).astype(F32)
+        rows.append(pick((parent_column == parent_f) & (octant_column == partner), row_f))
+    for p in range(parents_here):
+        rows.append(pick((slot_column == p) & (octant_column == lane_f), row_f))
+
+    most = jnp.zeros((devices, LANES), F32)
+    most_all = jnp.zeros((devices, LANES), F32)
+    device = iota((devices, LANES), 0)
+    lanes_2d = iota((devices, LANES), 1)
+    for k in range(tiles):
+        lanes = slice(k * LANES, (k + 1) * LANES)
+        hits = jnp.zeros((devices, LANES), F32)
+        for f in range(6):
+            hits = hits + jnp.where(near_ref[f : f + 1, lanes] // nb == device, 1.0, 0.0)
+        sums = [hits * any_parent(k * LANES + lane), hits]
+        width = 1
+        while width < nb:
+            sums = [x + pltpu.roll(x, LANES - width, 1) for x in sums]
+            width *= 2
+        start_lane = lanes_2d % nb == 0
+        opposite = (k * LANES + lanes_2d) // nb + devices // 2
+        opposite = jnp.where(opposite >= devices, opposite - devices, opposite) == device
+        most = jnp.maximum(most, jnp.where(start_lane, sums[0], 0.0))
+        most_all = jnp.maximum(most_all, jnp.where(start_lane & ~opposite, sums[1], 0.0))
+    for values in (most, most_all):
+        values = jnp.max(jnp.max(values, axis=0, keepdims=True), axis=1, keepdims=True)
+        rows.append(jnp.broadcast_to(values, (1, LANES)).astype(I32))
+    for k, values in enumerate(rows):
+        tab_ref[k : k + 1, :] = values
+
+    beside_bits = jnp.zeros((1, LANES), F32)
+    for f in range(6):
+        part = jnp.where(face == f, beside * (1 << f), 0.0)
+        beside_bits = beside_bits + pltpu.roll(part, (LANES - nb * f) % LANES, 1)
+    for k, values in enumerate((octant_column, slot_column, column(beside_bits))):
+        bits_ref[k * nb : (k + 1) * nb, :] = values[0:nb, :].astype(I32)
+
+
+def run(kernel, outs, operands, scratch=(), scalars=0, far=None, flops=0):
+    held = [o.shape for o in operands] + list(outs) + list(scratch)
     limit = sum(4 * max(math.prod(s), 8 * LANES) for s in held) + SPARE
     smem = pl.BlockSpec(memory_space=pltpu.SMEM)
     vmem = pl.BlockSpec(memory_space=pltpu.VMEM)
-    result = pl.pallas_call(
+    specs = [smem if k < scalars else vmem for k in range(len(operands))]
+    scratches = [pltpu.VMEM(s, F32) for s in scratch]
+    if far is not None:
+        specs[far] = pl.BlockSpec(memory_space=pltpu.HBM)
+        scratches.append(pltpu.SemaphoreType.DMA)
+    return pl.pallas_call(
         kernel,
-        out_shape=[jax.ShapeDtypeStruct(s, F32) for s in shapes],
-        in_specs=[smem if k < scalars else vmem for k in range(len(operands))],
-        out_specs=[vmem] * len(shapes),
-        scratch_shapes=[pltpu.VMEM(s, F32) for s in scratch],
+        out_shape=[jax.ShapeDtypeStruct(s, F32) for s in outs],
+        in_specs=specs,
+        out_specs=[vmem] * len(outs),
+        scratch_shapes=scratches,
         compiler_params=pltpu.CompilerParams(vmem_limit_bytes=limit),
         cost_estimate=pl.CostEstimate(
             flops=flops, bytes_accessed=4 * sum(o.size for o in operands), transcendentals=0
         ),
     )(*operands)
-    return result[0] if single else result
 
 
 def blank(*shapes):
@@ -655,178 +895,168 @@
 
 
 def local(fluid_state, neighbours, parents):
-    level_id = lax.axis_index("level")
     blk_index = lax.axis_index("blk")
     devices = lax.axis_size("blk")
     u = fluid_state[0]
+    nb, _, edge, _ = u.shape
+    parents_here = nb // 8
+    capacity = 2 * ((6 * nb + devices - 1) // devices)
+    smem = pl.BlockSpec(memory_space=pltpu.SMEM)
+    vmem = pl.BlockSpec(memory_space=pltpu.VMEM)
+    hbm = pl.BlockSpec(memory_space=pltpu.HBM)
+    table, bits = pl.pallas_call(
+        functools.partial(tables_kernel, nb, devices, parents_here),
+        out_shape=[
+            jax.ShapeDtypeStruct((17 + parents_here, LANES), I32),
+            jax.ShapeDtypeStruct((3 * nb, LANES), I32),
+        ],
+        in_specs=[smem, hbm, hbm],
+        out_specs=[vmem, vmem],
+        scratch_shapes=[
+            pltpu.VMEM(neighbours.shape[::-1], I32),
+            pltpu.VMEM(parents.shape[::-1], I32),
+            pltpu.SemaphoreType.DMA((2,)),
+        ],
+        compiler_params=pltpu.CompilerParams(vmem_limit_bytes=2 * SPARE),
+    )(jnp.reshape(blk_index, (1,)).astype(I32), neighbours.T, parents.T)
+
+    few = max(1, capacity // 3)
+    half = max(1, capacity // 2)
+    counts = table[15 + parents_here : 17 + parents_here, 0]
+    finished = lax.cond(
+        (counts[0] <= few) & (counts[1] <= half) & (devices % 2 == 0),
+        functools.partial(step, capacity, half, few),
+        functools.partial(step, capacity, capacity, capacity),
+        u,
+        table,
+        bits,
+    )
+    return finished[None]
+
+
+def step(capacity, wide, slots, u, table, bits):
+    level_id = lax.axis_index("level")
+    devices = lax.axis_size("blk")
     nb, _, edge, square = u.shape
     parents_here = nb // 8
-    capacity = 2 * ((6 * nb + devices - 1) // devices)
-
-    own_rows = lax.dynamic_slice_in_dim(neighbours, blk_index * nb, nb, 0)
-    parent_rows = lax.dynamic_slice_in_dim(parents, blk_index * nb, nb, 0)
-    parent_of = parent_rows[:, 0] - blk_index * nb
-    octants = parent_rows[:, 1]
-    beside = jnp.any(own_rows[:, :, None] == parents[None, None, :, 0], axis=2)
-    is_parent = jnp.any(jnp.arange(nb)[:, None] == parent_of[None, :], axis=1)
-    flat = own_rows.reshape(-1)
-    items = jnp.arange(6 * nb, dtype=I32)
-    targets = flat // nb
-    faces = items % 6
-    wanted = flat % nb * 6 + faces + 1 - 2 * (faces % 2)
-    beside_item = beside.reshape(-1)
-    parent_item = jnp.repeat(is_parent, 6)
-    same = targets[:, None] == targets[None, :]
-    by_own = same & (items[None, :] < items[:, None])
-    by_wanted = same & (wanted[None, :] < wanted[:, None])
-
-    def rank(order, mask=None):
-        return jnp.sum(order if mask is None else order & mask[None, :], axis=1, dtype=I32)
-
-    slot_of_block = jnp.sum(parent_of[None, :] < parent_of[:, None], axis=1, dtype=I32) // 8
-    parent_list = jnp.sum(
-        jnp.where(
-            (slot_of_block[None, :] == jnp.arange(6 * nb)[:, None]) & (octants[None, :] == 0),
-            parent_of[None, :],
-            0,
-        ),
-        axis=1,
-        dtype=I32,
-    )
-    table = jnp.stack(
-        [
-            targets,
-            rank(by_own),
-            rank(by_wanted),
-            beside_item.astype(I32),
-            parent_item.astype(I32),
-            rank(by_own, beside_item),
-            rank(by_wanted, parent_item),
-            rank(by_own, parent_item),
-            rank(by_wanted, beside_item),
-            parent_list,
-        ]
-    )
-    blocks = jnp.arange(nb, dtype=I32)
-    family = [octants, slot_of_block]
-    for axis in range(3):
-        bit = BIT_OF[axis]
-        partner = octants + bit - 2 * bit * (octants // bit % 2)
-        match = (parent_of[:, None] == parent_of[None, :]) & (octants[None, :] == partner[:, None])
-        family.append(jnp.sum(jnp.where(match, blocks[None, :], 0), axis=1, dtype=I32))
-    for p in range(parents_here):
-        match = (slot_of_block[None, :] == p) & (octants[None, :] == blocks[:, None])
-        family.append(jnp.sum(jnp.where(match, blocks[None, :], 0), axis=1, dtype=I32))
-    family = jnp.stack(family)
-    beside_bits = jnp.sum(
-        beside.astype(I32) * (1 << jnp.arange(6, dtype=I32))[None, :], axis=1, dtype=I32
-    )
-    bits = jnp.broadcast_to(
-        jnp.concatenate([octants, slot_of_block, beside_bits])[:, None], (3 * nb, LANES)
-    )
-
     part = functools.partial
     cell_shape = u.shape
     plane_shape = (6, 5, 6 * nb, LANES)
     ghost_shape = (6, 5, 4 * nb, LANES)
     face_shape = (6, 5, 2 * nb, LANES)
     rim_shape = (6, 5, 2 * parents_here, LANES)
-    wide_send = (devices, capacity * 5, 4, LANES)
-    thin_send = (devices, capacity * 5, 2, LANES)
+    wide_send = (devices, wide * 5, 4, LANES)
+    over_send = [((capacity - wide) * 5, 4, LANES)] if wide < capacity else []
+    thin_send = (devices, slots * 5, 2, LANES)
     average_shape = (parents_here,) + cell_shape[1:]
     work = 220 * 3 * 5 * nb * edge * square
 
     def inner(cells):
         return run(part(inner_kernel, nb, edge), [cell_shape, plane_shape], [cells], flops=work)
 
+    def half_way_round(buffer):
+        turned = [(d, (d + devices // 2) % devices) for d in range(devices)]
+        return lax.ppermute(buffer, ("level", "blk"), turned)
+
     def coarse_first(u):
-        send = run(part(send_kernel, nb, edge), wide_send, [table, u], [ghost_shape], 1)
-        received = route(send)
-        partial_new, planes = inner(u)
-        cells, faces, send, rims = run(
-            part(coarse_kernel, nb, edge, parents_here),
-            [cell_shape, face_shape, thin_send, rim_shape],
-            [table, partial_new, planes, received],
-            [ghost_shape, ghost_shape, face_shape],
+        send, *over = run(
+            part(send_kernel, nb, edge, wide), [wide_send] + over_send, [table, u], [ghost_shape], 1
+        )
+        received = [route(send)] + [half_way_round(buffer) for buffer in over]
+        partial_new, planes, near = run(
+            part(coarse_inner_kernel, nb, edge),
+            [cell_shape, plane_shape, face_shape],
+            [u],
+            flops=work,
+        )
+        adds, faces, send, rims = run(
+            part(coarse_kernel, nb, edge, parents_here, wide),
+            [ghost_shape, face_shape, thin_send, rim_shape],
+            [table, planes, near] + received,
+            [ghost_shape, face_shape],
             1,
         )
-        (unused,) = blank(plane_shape)
-        return cells, faces, send, rims, unused
+        return (partial_new, adds, faces, send, rims, *blank(plane_shape))
 
     def fine_first(u):
         partial_new, planes = inner(u)
-        faces, send, rims = blank(face_shape, thin_send, rim_shape)
-        return partial_new, faces, send, rims, planes
-
-    cells, faces, send, rims, planes = lax.cond(level_id == 0, coarse_first, fine_first, u)
+        return (partial_new, *blank(ghost_shape, face_shape, thin_send, rim_shape), planes)
+
+    partial_new, adds, faces, send, rims, planes = lax.cond(
+        level_id == 0, coarse_first, fine_first, u
+    )
     early_rims = level_shift(rims, 0)
 
-    def coarse_second(cells, send, planes, early_rims):
-        late = run(
-            part(rims_kernel, parents_here), rim_shape, [table, route(send)], (), 1
+    def coarse_second(send, partial_new, adds, planes, early_rims):
+        received = route(send)
+        (cells,) = run(
+            part(coarse_cells_kernel, nb, edge),
+            [cell_shape],
+            [partial_new, adds],
+            [ghost_shape],
+            flops=work // 4,
         )
-        return (late, *blank(cell_shape, plane_shape, face_shape))
-
-    def fine_second(cells, send, planes, early_rims):
+        (late,) = run(part(rims_kernel, nb, parents_here), [rim_shape], [table, received], (), 1)
+        return (late, cells, *blank(plane_shape, face_shape))
+
+    def fine_second(send, partial_new, adds, planes, early_rims):
         half, faces = run(
             part(fine_kernel, nb, edge, parents_here),
             [cell_shape, face_shape],
-            [family, bits, cells, planes, early_rims],
-            [ghost_shape, ghost_shape],
+            [table, bits, partial_new, planes, early_rims],
+            [ghost_shape, ghost_shape, cell_shape],
+            1,
+            far=2,
+        )
+        return (*blank(rim_shape), *inner(half), faces)
+
+    late, cells, half_planes, half_faces = lax.cond(
+        level_id == 0, coarse_second, fine_second, send, partial_new, adds, planes, early_rims
+    )
+    late_rims = level_shift(late, 0)
+
+    def coarse_third(cells, half_planes, half_faces, early_rims, late_rims):
+        return tuple(blank(thin_send, cell_shape, average_shape))
+
+    def fine_third(cells, half_planes, half_faces, early_rims, late_rims):
+        send, adds = run(
+            part(means_kernel, nb, edge, parents_here),
+            [thin_send, ghost_shape],
+            [table, bits, half_planes, early_rims, late_rims, half_faces],
+            [ghost_shape, face_shape, (6, 5 * nb, LANES), rim_shape],
             1,
         )
-        (late,) = blank(rim_shape)
-        return (late, *inner(half), faces)
-
-    late, half_cells, half_planes, half_faces = lax.cond(
-        level_id == 0, coarse_second, fine_second, cells, send, planes, early_rims
+        received = route(send)
+        out, averaged = run(
+            part(finish_kernel, nb, edge, parents_here),
+            [cell_shape, average_shape],
+            [table, cells, adds],
+            [ghost_shape, (nb, 5, 2, edge, LANES), (nb, 5, ROWS, LANES)],
+            1,
+            flops=work,
+        )
+        return received, out, averaged
+
+    returned, out, averaged = lax.cond(
+        level_id == 0, coarse_third, fine_third,
+        cells, half_planes, half_faces, early_rims, late_rims,
     )
-    late_rims = level_shift(late, 0)
-
-    def coarse_third(half_cells, half_planes, half_faces, early_rims, late_rims):
-        return tuple(blank(cell_shape, rim_shape))
-
-    def fine_third(half_cells, half_planes, half_faces, early_rims, late_rims):
-        return tuple(
-            run(
-                part(last_fine_kernel, nb, edge, parents_here),
-                [cell_shape, rim_shape],
-                [family, bits, half_cells, half_planes, early_rims, late_rims, half_faces],
-                [ghost_shape, ghost_shape, face_shape, (6, 5 * nb, LANES)],
-                1,
-            )
-        )
-
-    out, means = lax.cond(
-        level_id == 0, coarse_third, fine_third,
-        half_cells, half_planes, half_faces, early_rims, late_rims,
-    )
-    means = level_shift(means, 1)
-
-    def coarse_fourth(means, out):
-        send = run(part(return_kernel, parents_here), thin_send, [table, means], (), 1)
-        return route(send), blank(average_shape)[0]
-
-    def fine_fourth(means, out):
-        averages = run(part(averages_kernel, nb, edge), average_shape, [family, out], (), 1)
-        return blank(thin_send)[0], averages
-
-    returned, averages = lax.cond(level_id == 0, coarse_fourth, fine_fourth, means, out)
-    averages = level_shift(averages, 1)
-
-    def correct(out, cells, faces, returned, averages):
+    returned = level_shift(returned, 1)
+    averaged = level_shift(averaged, 1)
+
+    def correct(out, cells, faces, returned, averaged):
         return run(
             part(correct_kernel, nb, edge, parents_here),
-            cell_shape,
-            [table, bits, cells, faces, returned, averages],
+            [cell_shape],
+            [table, bits, cells, faces, returned, averaged],
             [face_shape, face_shape, cell_shape],
             1,
-        )
-
-    finished = lax.cond(
-        level_id == 0, correct, lambda out, *rest: out, out, cells, faces, returned, averages
+            far=2,
+        )[0]
+
+    return lax.cond(
+        level_id == 0, correct, lambda out, *rest: out, out, cells, faces, returned, averaged
     )
-    return finished[None]
 
 
 def solution(mesh):

time: 121 us -> 98.3 us (0.81)
  waiting for transfers between devices: 52.2 us -> 25.9 us
  Pallas kernels: 33.7 us -> 40 us
  local copies, waits for them, and re-layouts: 7.33 us -> 1.96 us
  starting transfers between devices: 25.7 us -> 27.2 us
  between operations: 0.14 us -> 1.57 us
  other arithmetic: 1.41 us -> 0 us
    all_to_all x3 -> x2, waiting for transfers between devices: 40.5 us -> 5.09 us  [route(): lax.all_to_all(buffer, 'blk', split_axis=0, concat_axis=0, tiled=True)]
    ppermute x4, waiting for transfers between devices: 11.7 us -> 20.9 us  [level_shift(): return lax.ppermute(array, 'level', [(source, 1 - source)])]
    all_to_all x3 -> x2, starting transfers between devices: 20.6 us -> 13 us  [route(): lax.all_to_all(buffer, 'blk', split_axis=0, concat_axis=0, tiled=True)]
    pallas_call x6 -> x7, Pallas kernels: 33.7 us -> 40 us  [the longest x6 39.4 us: run(): pl.pallas_call(kernel, out_shape=[jax.ShapeDtypeStruct(s, F32) for s in o...]
    ppermute x0 -> x1, starting transfers between devices: none -> 4.72 us  [half_way_round(): return lax.ppermute(buffer, ('level', 'blk'), turned)]
    ppermute x4, starting transfers between devices: 5.13 us -> 9.57 us  [level_shift(): return lax.ppermute(array, 'level', [(source, 1 - source)])]
    cond x6 -> x0, local copies, waits for them, and re-layouts: 3.64 us -> none
  transfers between devices with their start and end apart: 7 -> 7, of which waited for: 7 -> 4; matrix products, arithmetic and copies ran while one was open for 0% -> 0% of each run, Pallas kernels for 11% -> 20%
where the time goes in v3:
time: 98.3 us; the launch traced here: 97.6 us
  Pallas kernels  40 us (41%)
  starting transfers between devices  27.2 us (28%)
  waiting for transfers between devices  25.9 us (26%)
  local copies, waits for them, and re-layouts  1.96 us (2%)
  between operations  1.57 us (2%)
    pallas_call x6, Pallas kernels, run(): pl.pallas_call(kernel, out_shape=[jax.ShapeDtypeStruct(s, F32) for s in o...  39.4 us
    ppermute x4, waiting for transfers between devices, level_shift(): return lax.ppermute(array, 'level', [(source, 1 - source)])  20.9 us
    all_to_all x2, starting transfers between devices, route(): lax.all_to_all(buffer, 'blk', split_axis=0, concat_axis=0, tiled=True)  13 us
    ppermute x4, starting transfers between devices, level_shift(): return lax.ppermute(array, 'level', [(source, 1 - source)])  9.57 us
    all_to_all x2, waiting for transfers between devices, route(): lax.all_to_all(buffer, 'blk', split_axis=0, concat_axis=0, tiled=True)  5.09 us
    ppermute x1, starting transfers between devices, half_way_round(): return lax.ppermute(buffer, ('level', 'blk'), turned)  4.72 us
  transfers between devices with their start and end apart: 7, of which 4 were waited for; matrix products, arithmetic and copies ran while one was open for 0% of the time, Pallas kernels for 20%

profile of v3, /device:TPU:0, one launch (start us, length us, event | category | flops | bytes accessed | tf_op | source)
XLA Modules:
  0.0 97.6 jit_solution(3963823121409158756)
XLA Ops:
  0.0 0.7 copy-done.3
  0.7 0.7 copy-done.4
  2.0 0.6 fusion
  3.9 93.5 %conditional.9 = ((f32[1,16,5,16,256]{4,3,2,1,0:T(8,128)})) conditional(s32[]{:T(128)} %bitcast.7, (f32[16,5,16,256]{3,2,1,0:T(8,128)}, s32[19,128]{1,0:T(8,128)S(1)}, s32[48,128]{1,0:T(8,128)S(1)}) %tuple.103, (f32[16,5,16,256]{3,2,1,0:T(8,128)}, s32[19,128]{1,0:T(8,128)S(1)}, s32[48,128]{1,0:T(8,128)S(1)}) %tuple.104), branch_computations={%region_0.0_spmd, %region_9.0_spmd} | conditional | flops 648806400 | bytes 45942464 | solution.py:926
  4.1 42.7 %conditional.4 = (f32[16,5,16,256]{3,2,1,0:T(8,128)}, f32[6,5,64,128]{3,2,1,0:T(8,128)}, f32[6,5,32,128]{3,2,1,0:T(8,128)}, f32[16,20,2,128]{3,2,1,0:T(2,128)}, ...) conditional(s32[]{:T(128)} %convert_element_type.10, ...), branch_computations={%region_10.0_spmd, %region_11.0_spmd} | conditional | flops 216268800 | bytes 8846456 | solution.py:985
  4.2 6.2 %branch_1_fun.28 = (f32[16,30,4,128]{3,2,1,0:T(4,128)}, f32[30,4,128]{2,1,0:T(4,128)S(1)}) custom-call(s32[19,128]{1,0:T(8,128)S(1)} %get-tuple-element.200.tab_ref, f32[16,5,16,256]{3,2,1,0:T(8,128)} %get-tuple-element.198.u_ref), custom_call_target="tpu_custom_call" | custom-call | bytes 1320448 | tf_op jit(solution)/shard_map/cond/branch_1_fun/cond/branch_1_fun/pallas_call | solution.py:868
  10.4 8.3 %all-to-all-start.3 = ((f32[16,30,4,128]{3,2,1,0:T(4,128)}), f32[16,30,4,128]{3,2,1,0:T(4,128)S(1)}, u32[]{:S(2)}, u32[]{:S(2)}) async-start(f32[16,30,4,128]{3,2,1,0:T(4,128)} %get-tuple-element.203), calls=%async_computation.3 | async-start | bytes 1966080 | tf_op jit(solution)/shard_map/cond/branch_1_fun/cond/branch_1_fun/all_to_all | solution.py:894
  18.7 4.7 %collective-permute-start.4 = (f32[30,4,128]{2,1,0:T(4,128)S(1)}, f32[30,4,128]{2,1,0:T(4,128)S(1)}, u32[]{:S(2)}, u32[]{:S(2)}) collective-permute-start(f32[30,4,128]{2,1,0:T(4,128)S(1)} %get-tuple-element.204), channel_id=1, source_target_pairs={{0,8},{1,9},{2,10},{3,11},{4,12},{5,13},{6,14},{7,15},{8,0},{9,1},... | collective-permute-start | bytes 184328 | tf_op jit(solution)/shard_map/cond/branch_1_fun/cond/branch_1_fun/ppermute | solution.py:959
  23.4 15.5 %branch_1_fun.27 = (f32[16,5,16,256]{3,2,1,0:T(8,128)}, f32[6,5,96,128]{3,2,1,0:T(8,128)S(1)}, f32[6,5,32,128]{3,2,1,0:T(8,128)S(1)}) custom-call(f32[16,5,16,256]{3,2,1,0:T(8,128)} %get-tuple-element.198.u_ref), custom_call_target="tpu_custom_call" | custom-call | flops 216268800 | bytes 1310720 | tf_op jit(solution)/shard_map/cond/branch_1_fun/cond/branch_1_fun/pallas_call | solution.py:868
  39.0 7.8 %branch_1_fun.29 = (f32[6,5,64,128]{3,2,1,0:T(8,128)}, f32[6,5,32,128]{3,2,1,0:T(8,128)}, f32[16,20,2,128]{3,2,1,0:T(2,128)}, f32[6,5,4,128]{3,2,1,0:T(4,128)S(1)}) custom-call(s32[19,128]{1,0:T(8,128)S(1)} %get-tuple-element.200.tab_ref, f32[6,5,96,128]{3,2,1,0:T(8,128)S(1)} %get-tuple-element.201.plane_ref, ...), custom_call_target="tpu_custom_call" | custom-call | bytes 3020288 | tf_op jit(solution)/shard_map/cond/branch_1_fun/cond/branch_1_fun/pallas_call | solution.py:868
  46.8 1.3 %collective-permute-start.5 = (f32[6,5,4,128]{3,2,1,0:T(4,128)S(1)}, f32[6,5,4,128]{3,2,1,0:T(4,128)S(1)}, u32[]{:S(2)}, u32[]{:S(2)}) collective-permute-start(f32[6,5,4,128]{3,2,1,0:T(4,128)S(1)} %get-tuple-element.246), channel_id=1, source_target_pairs={{0,16},{1,17},{2,18},{3,19},{4,20},{5,21},{6,22},{7,23},{8,24},{9,... | collective-permute-start | bytes 184328 | tf_op jit(solution)/shard_map/cond/branch_1_fun/ppermute | solution.py:890
  48.1 0.9 collective-permute-done.5
  49.0 14.7 %conditional.5 = (f32[6,5,4,128]{3,2,1,0:T(4,128)S(1)}, f32[16,5,16,256]{3,2,1,0:T(8,128)S(1)}, f32[6,5,96,128]{3,2,1,0:T(8,128)}, f32[6,5,32,128]{3,2,1,0:T(8,128)S(1)}) conditional(s32[]{:T(128)} %convert_element_type.10, (s32[19,128]{1,0:T(8,128)S(1)}, s32[48,128]{1,0:T(8,128)S(1)}, f32[16,5,16,256]{3,2,1,0:T(8,128)}, ...), branch_computations={%region_12.0_spmd, %region_13.0_spmd} | conditional | flops 216268800 | bytes 4191776 | solution.py:1013
  49.0 4.6 %all-to-all-start.4 = ((f32[16,20,2,128]{3,2,1,0:T(2,128)}), f32[16,20,2,128]{3,2,1,0:T(2,128)S(1)}, u32[]{:S(2)}, u32[]{:S(2)}) async-start(f32[16,20,2,128]{3,2,1,0:T(2,128)} %get-tuple-element.219), calls=%async_computation.4 | async-start | bytes 655360 | tf_op jit(solution)/shard_map/cond/branch_1_fun/cond/branch_1_fun/all_to_all | solution.py:894
  53.6 3.9 %branch_1_fun.32 = f32[16,5,16,256]{3,2,1,0:T(8,128)S(1)} custom-call(f32[16,5,16,256]{3,2,1,0:T(8,128)} %get-tuple-element.220.d_ref, f32[6,5,64,128]{3,2,1,0:T(8,128)} %get-tuple-element.221.add_ref), custom_call_target="tpu_custom_call" | custom-call | flops 54067200 | bytes 2293760 | tf_op jit(solution)/shard_map/cond/branch_1_fun/cond/branch_1_fun/pallas_call | solution.py:868
  57.5 5.1 %all-to-all-done.4.recv_ref = f32[16,20,2,128]{3,2,1,0:T(2,128)S(1)} async-done(((f32[16,20,2,128]{3,2,1,0:T(2,128)}), f32[16,20,2,128]{3,2,1,0:T(2,128)S(1)}, u32[]{:S(2)}, u32[]{:S(2)}) %all-to-all-start.4) | async-done | bytes 327712 | tf_op jit(solution)/shard_map/cond/branch_1_fun/cond/branch_1_fun/all_to_all | solution.py:894
  62.6 0.8 branch_1_fun.31
  63.7 5.7 %collective-permute-start.6 = (f32[6,5,4,128]{3,2,1,0:T(4,128)S(1)}, f32[6,5,4,128]{3,2,1,0:T(4,128)S(1)}, u32[]{:S(2)}, u32[]{:S(2)}) collective-permute-start(f32[6,5,4,128]{3,2,1,0:T(4,128)S(1)} %get-tuple-element.250), channel_id=1, source_target_pairs={{0,16},{1,17},{2,18},{3,19},{4,20},{5,21},{6,22},{7,23},{8,24},{9,... | collective-permute-start | bytes 184328 | tf_op jit(solution)/shard_map/cond/branch_1_fun/ppermute | solution.py:890
  69.4 0.9 collective-permute-done.6
  70.3 1.3 %collective-permute-start.7 = (f32[16,20,2,128]{3,2,1,0:T(2,128)S(1)}, f32[16,20,2,128]{3,2,1,0:T(2,128)S(1)}, u32[]{:S(2)}, u32[]{:S(2)}) collective-permute-start(f32[16,20,2,128]{3,2,1,0:T(2,128)S(1)} %get-tuple-element.255), channel_id=1, source_target_pairs={{16,0},{17,1},{18,2},{19,3},{20,4},{21,5},{22,6},{23,7},{24,8},{25... | collective-permute-start | bytes 983048 | tf_op jit(solution)/shard_map/cond/branch_1_fun/ppermute | solution.py:890
  71.6 1.3 %collective-permute-start.8 = (f32[2,5,16,256]{3,2,1,0:T(8,128)S(1)}, f32[2,5,16,256]{3,2,1,0:T(8,128)S(1)}, u32[]{:S(2)}, u32[]{:S(2)}) collective-permute-start(f32[2,5,16,256]{3,2,1,0:T(8,128)S(1)} %get-tuple-element.256), channel_id=1, source_target_pairs={{16,0},{17,1},{18,2},{19,3},{20,4},{21,5},{22,6},{23,7},{24,8},{25... | collective-permute-start | bytes 491528 | tf_op jit(solution)/shard_map/cond/branch_1_fun/ppermute | solution.py:890
  72.9 19.1 %collective-permute-done.8 = f32[2,5,16,256]{3,2,1,0:T(8,128)S(1)} collective-permute-done((f32[2,5,16,256]{3,2,1,0:T(8,128)S(1)}, f32[2,5,16,256]{3,2,1,0:T(8,128)S(1)}, u32[]{:S(2)}, u32[]{:S(2)}) %collective-permute-start.8) | collective-permute-done | bytes 163872 | tf_op jit(solution)/shard_map/cond/branch_1_fun/ppermute | solution.py:890
  92.0 5.2 %conditional.7 = (f32[1,16,5,16,256]{4,3,2,1,0:T(8,128)}) conditional(s32[]{:T(128)} %convert_element_type.10, f32[16,5,16,256]{3,2,1,0:T(8,128)} %get-tuple-element.253, (s32[19,128]{1,0:T(8,128)S(1)}, s32[48,128]{1,0:T(8,128)S(1)}, f32[16,5,16,256]{3,2,1,0:T(8,128)S(1)}, f32[6,5,32,128]{3,2,1,0:T(8,128)}, f32[16,20,2,128]{3,2,1,0:T(2,128)S(1)}, ...), branch_computations={%region_16.0_spmd, %region_17.0_spmd} | conditional | bytes 2328072 | solution.py:1057
  92.0 5.2 %branch_1_fun.35 = f32[16,5,16,256]{3,2,1,0:T(8,128)} custom-call(s32[19,128]{1,0:T(8,128)S(1)} %get-tuple-element.235.tab_ref, s32[48,128]{1,0:T(8,128)S(1)} %get-tuple-element.236.bits_ref, f32[16,5,16,256]{3,2,1,0:T(8,128)S(1)} %get-tuple-element.237.new_ref, f32[6,5,32,128]{3,2,1,0:T(8,128)} %get-tuple-element.238.face_ref, ...), custom_call_target="tpu_custom_call" | custom-call | bytes 2328064 | tf_op jit(solution)/shard_map/cond/branch_1_fun/cond/branch_1_fun/pallas_call | solution.py:868
  (10 shorter events, 0.6 us)
Async XLA Ops:
  0.0 0.7 copy-start.3
  0.7 0.7 copy-start.4
  10.4 28.6 %all-to-all-start.3 = ((f32[16,30,4,128]{3,2,1,0:T(4,128)}), f32[16,30,4,128]{3,2,1,0:T(4,128)S(1)}, u32[]{:S(2)}, u32[]{:S(2)}) async-start(f32[16,30,4,128]{3,2,1,0:T(4,128)} %get-tuple-element.203), calls=%async_computation.3 | async-start | bytes 1966080 | tf_op jit(solution)/shard_map/cond/branch_1_fun/cond/branch_1_fun/all_to_all | solution.py:894
  18.7 20.3 %collective-permute-start.4 = (f32[30,4,128]{2,1,0:T(4,128)S(1)}, f32[30,4,128]{2,1,0:T(4,128)S(1)}, u32[]{:S(2)}, u32[]{:S(2)}) collective-permute-start(f32[30,4,128]{2,1,0:T(4,128)S(1)} %get-tuple-element.204), channel_id=1, source_target_pairs={{0,8},{1,9},{2,10},{3,11},{4,12},{5,13},{6,14},{7,15},{8,0},{9,1},... | collective-permute-start | bytes 184328 | tf_op jit(solution)/shard_map/cond/branch_1_fun/cond/branch_1_fun/ppermute | solution.py:959
  46.8 2.2 %collective-permute-start.5 = (f32[6,5,4,128]{3,2,1,0:T(4,128)S(1)}, f32[6,5,4,128]{3,2,1,0:T(4,128)S(1)}, u32[]{:S(2)}, u32[]{:S(2)}) collective-permute-start(f32[6,5,4,128]{3,2,1,0:T(4,128)S(1)} %get-tuple-element.246), channel_id=1, source_target_pairs={{0,16},{1,17},{2,18},{3,19},{4,20},{5,21},{6,22},{7,23},{8,24},{9,... | collective-permute-start | bytes 184328 | tf_op jit(solution)/shard_map/cond/branch_1_fun/ppermute | solution.py:890
  49.0 13.7 %all-to-all-start.4 = ((f32[16,20,2,128]{3,2,1,0:T(2,128)}), f32[16,20,2,128]{3,2,1,0:T(2,128)S(1)}, u32[]{:S(2)}, u32[]{:S(2)}) async-start(f32[16,20,2,128]{3,2,1,0:T(2,128)} %get-tuple-element.219), calls=%async_computation.4 | async-start | bytes 655360 | tf_op jit(solution)/shard_map/cond/branch_1_fun/cond/branch_1_fun/all_to_all | solution.py:894
  63.7 6.6 %collective-permute-start.6 = (f32[6,5,4,128]{3,2,1,0:T(4,128)S(1)}, f32[6,5,4,128]{3,2,1,0:T(4,128)S(1)}, u32[]{:S(2)}, u32[]{:S(2)}) collective-permute-start(f32[6,5,4,128]{3,2,1,0:T(4,128)S(1)} %get-tuple-element.250), channel_id=1, source_target_pairs={{0,16},{1,17},{2,18},{3,19},{4,20},{5,21},{6,22},{7,23},{8,24},{9,... | collective-permute-start | bytes 184328 | tf_op jit(solution)/shard_map/cond/branch_1_fun/ppermute | solution.py:890
  70.3 21.7 %collective-permute-start.7 = (f32[16,20,2,128]{3,2,1,0:T(2,128)S(1)}, f32[16,20,2,128]{3,2,1,0:T(2,128)S(1)}, u32[]{:S(2)}, u32[]{:S(2)}) collective-permute-start(f32[16,20,2,128]{3,2,1,0:T(2,128)S(1)} %get-tuple-element.255), channel_id=1, source_target_pairs={{16,0},{17,1},{18,2},{19,3},{20,4},{21,5},{22,6},{23,7},{24,8},{25... | collective-permute-start | bytes 983048 | tf_op jit(solution)/shard_map/cond/branch_1_fun/ppermute | solution.py:890
  71.6 20.4 %collective-permute-start.8 = (f32[2,5,16,256]{3,2,1,0:T(8,128)S(1)}, f32[2,5,16,256]{3,2,1,0:T(8,128)S(1)}, u32[]{:S(2)}, u32[]{:S(2)}) collective-permute-start(f32[2,5,16,256]{3,2,1,0:T(8,128)S(1)} %get-tuple-element.256), channel_id=1, source_target_pairs={{16,0},{17,1},{18,2},{19,3},{20,4},{21,5},{22,6},{23,7},{24,8},{25... | collective-permute-start | bytes 491528 | tf_op jit(solution)/shard_map/cond/branch_1_fun/ppermute | solution.py:890

commit v4 on v3

--- a/solution.py
+++ b/solution.py
@@ -17,6 +17,10 @@
 SPARE = 8 * 1024 * 1024
 LANES = 128
 ROWS = 8
+COUNTS = 15
+OTHERS = 17
+SELF = 18
+CHILDREN = 19
 
 
 def iota(shape, dim):
@@ -124,7 +128,7 @@
     return edge * ((row_of() - lane // edge + ROWS) % ROWS) + lane % edge
 
 
-def extract(u_ref, plane_ref, layers, nb, edge):
+def extract(u_ref, plane_ref, layers, nb, edge, eager):
     groups = LANES // edge
     for side in range(2):
         for layer in range(layers):
@@ -179,7 +183,7 @@
                     plane_ref[5, c, rows_at(layer, rt, h), :] = zacc[edge - 1 - layer]
         return carry
 
-    lax.fori_loop(0, 5, gather, 0)
+    lax.fori_loop(0, 5, gather, 0, unroll=5 if eager else 1)
 
     def turn(c, carry):
         last = swap_back_index(lane, edge)
@@ -212,10 +216,10 @@
             plane_ref[face, c, at, :] = v
         return carry
 
-    lax.fori_loop(0, 5, turn, 0)
-
-
-def expand_add(base_ref, add_ref, out_ref, layers, nb, edge, split_ref=None):
+    lax.fori_loop(0, 5, turn, 0, unroll=5 if eager else 1)
+
+
+def expand_add(base_ref, add_ref, out_ref, layers, nb, edge, eager, split_ref=None, copies=()):
     groups = LANES // edge
     lane = lane_of()
     row = row_of()
@@ -261,7 +265,7 @@
                 add_ref[face, c, rows_at(layer, rt, h), :] = pair[h]
         return carry
 
-    lax.fori_loop(0, 5, turn, 0)
+    lax.fori_loop(0, 5, turn, 0, unroll=5 if eager else 1)
 
     def spread(c, carry):
         for rt in range(2):
@@ -309,85 +313,67 @@
                         split_ref[b, c, h, rows, :] = value
         return carry
 
-    lax.fori_loop(0, 5, spread, 0)
+    if eager:
+        for c in range(5):
+            spread(c, 0)
+            for copy in copies[c : c + 1]:
+                copy.start()
+    else:
+        lax.fori_loop(0, 5, spread, 0)
+        for copy in copies:
+            copy.start()
 
 
 def block_rows(block, nb, count):
     return pl.ds(block, count, stride=nb)
 
 
-def pack(tab_ref, valid_row, slot_row, plane_ref, send_ref, count, nb):
+def pack(tab_ref, valid_row, slot_row, slots, plane_ref, send_ref, count, nb):
     for face in range(6):
         for block in range(nb):
             item = face * nb + block
-
-            def move(item=item, face=face, block=block):
-                target = tab_ref[0, item]
-                first = tab_ref[slot_row, item] * 5
-                for c in range(5):
-                    send_ref[target, first + c] = plane_ref[
-                        face, c, block_rows(block, nb, count), :
-                    ]
-
-            if valid_row is None:
-                move()
-            else:
-                pl.when(tab_ref[valid_row, item] > 0)(move)
-
-
-def unpack(tab_ref, valid_row, slot_row, recv_ref, plane_ref, count, nb):
+            valid = tab_ref[valid_row, item] > 0
+            target = jnp.where(valid, tab_ref[0, item], tab_ref[SELF, 0])
+            first = jnp.where(valid, tab_ref[slot_row, item] * 5, 0)
+            for c in range(5):
+                send_ref[target, first + c] = plane_ref[face, c, block_rows(block, nb, count), :]
+
+
+def unpack(tab_ref, slot_row, slots, recv_ref, plane_ref, count, nb):
     for face in range(6):
         for block in range(nb):
             item = face * nb + block
-
-            def move(item=item, face=face, block=block):
-                target = tab_ref[0, item]
-                first = tab_ref[slot_row, item] * 5
-                for c in range(5):
-                    plane_ref[face, c, block_rows(block, nb, count), :] = recv_ref[
-                        target, first + c
-                    ]
-
-            if valid_row is None:
-                move()
-            else:
-                pl.when(tab_ref[valid_row, item] > 0)(move)
-
-
-def pack_wide(tab_ref, slots, plane_ref, send_ref, over_ref, nb):
+            target = tab_ref[0, item]
+            first = jnp.minimum(tab_ref[slot_row, item], slots - 1) * 5
+            for c in range(5):
+                plane_ref[face, c, block_rows(block, nb, count), :] = recv_ref[target, first + c]
+
+
+def pack_wide(tab_ref, slots, devices, plane_ref, all_ref, nb):
     for face in range(6):
         for block in range(nb):
             item = face * nb + block
             slot = tab_ref[1, item]
-
-            def move(ref, first, face=face, block=block):
-                for c in range(5):
-                    ref[first + c] = plane_ref[face, c, block_rows(block, nb, 4), :]
-
-            target_ref = send_ref.at[tab_ref[0, item]]
-            if over_ref is None:
-                move(target_ref, slot * 5)
-            else:
-                pl.when(slot < slots)(functools.partial(move, target_ref, slot * 5))
-                pl.when(slot >= slots)(functools.partial(move, over_ref, (slot - slots) * 5))
+            first = jnp.where(
+                slot < slots, tab_ref[0, item] * slots + slot, (devices - 1) * slots + slot
+            )
+            for c in range(5):
+                all_ref[first * 5 + c] = plane_ref[face, c, block_rows(block, nb, 4), :]
 
 
 def unpack_wide(tab_ref, slots, recv_ref, over_ref, plane_ref, nb):
     for face in range(6):
         for block in range(nb):
             item = face * nb + block
+            target = tab_ref[0, item]
             slot = tab_ref[2, item]
-
-            def move(ref, first, face=face, block=block):
-                for c in range(5):
-                    plane_ref[face, c, block_rows(block, nb, 4), :] = ref[first + c]
-
-            source_ref = recv_ref.at[tab_ref[0, item]]
-            if over_ref is None:
-                move(source_ref, slot * 5)
-            else:
-                pl.when(slot < slots)(functools.partial(move, source_ref, slot * 5))
-                pl.when(slot >= slots)(functools.partial(move, over_ref, (slot - slots) * 5))
+            first = jnp.minimum(slot, slots - 1) * 5
+            beyond = jnp.maximum(slot - slots, 0) * 5
+            for c in range(5):
+                value = recv_ref[target, first + c]
+                if over_ref is not None:
+                    value = jnp.where(slot < slots, value, over_ref[beyond + c])
+                plane_ref[face, c, block_rows(block, nb, 4), :] = value
 
 
 def take_rims(tab_ref, slot_row, recv_ref, rim_ref, parents_here, nb):
@@ -400,7 +386,7 @@
                 rim_ref[face, c, 2 * p : 2 * p + 2, :] = recv_ref[target, first + c, 0:2, :]
 
 
-def interior(nb, edge, u_ref, d_ref):
+def interior(nb, edge, eager, u_ref, d_ref, tab_ref=None):
     square = edge * edge
 
     def sweep(u, axis, index, size, step, dim):
@@ -413,7 +399,7 @@
         flux = [jnp.where(inside, x, 0.0) for x in hllc(prev, low, n)]
         return [pltpu.roll(x, size - step, dim) - x for x in flux]
 
-    def body(b, carry):
+    def work(b):
         for rt in range(edge // ROWS):
             rows = slice(rt * ROWS, (rt + 1) * ROWS)
             u = [u_ref[b, c, rows, :] for c in range(5)]
@@ -427,12 +413,15 @@
             more = sweep(u, 2, iota((edge, LANES), 1) % edge, LANES, 1, 1)
             for c in range(5):
                 d_ref[b, c, :, lanes] = d_ref[b, c, :, lanes] - STEP_RATIO * (div[c] + more[c])
+
+    def body(k, carry):
+        work(k if tab_ref is None else tab_ref[OTHERS, k])
         return carry
 
-    lax.fori_loop(0, nb, body, 0)
-
-
-def face_fluxes(plane_ref, ghost_ref, add_ref, face_ref, nb):
+    lax.fori_loop(0, nb if tab_ref is None else nb - nb // 8, body, 0, unroll=2 if eager else 1)
+
+
+def face_fluxes(plane_ref, ghost_ref, add_ref, face_ref, nb, eager):
     for face in range(6):
         axis = face // 2
         side = face % 2
@@ -465,23 +454,34 @@
                 add_ref[face, c, rows(1), :] = (sign * STEP_RATIO) * second[c]
             return carry
 
-        lax.fori_loop(0, 2, body, 0)
-
-
-def inner_kernel(nb, edge, u_ref, d_ref, plane_ref):
-    extract(u_ref, plane_ref, 3, nb, edge)
-    interior(nb, edge, u_ref, d_ref)
-
-
-def coarse_inner_kernel(nb, edge, u_ref, d_ref, plane_ref, near_ref):
-    inner_kernel(nb, edge, u_ref, d_ref, plane_ref)
-    extract(d_ref, near_ref, 1, nb, edge)
-
-
-def send_kernel(nb, edge, slots, tab_ref, u_ref, send_ref, *refs):
-    *over_ref, plane_ref = refs
-    extract(u_ref, plane_ref, 2, nb, edge)
-    pack_wide(tab_ref, slots, plane_ref, send_ref, over_ref[0] if over_ref else None, nb)
+        lax.fori_loop(0, 2, body, 0, unroll=2 if eager else 1)
+
+
+def inner_kernel(nb, edge, eager, u_ref, d_ref, plane_ref):
+    extract(u_ref, plane_ref, 3, nb, edge, eager)
+    interior(nb, edge, eager, u_ref, d_ref)
+
+
+def coarse_inner_kernel(nb, edge, eager, tab_ref, u_ref, d_ref, near_ref):
+    interior(nb, edge, eager, u_ref, d_ref, tab_ref)
+    extract(d_ref, near_ref, 1, nb, edge, eager)
+
+
+def send_kernel(nb, edge, eager, slots, devices, tab_ref, u_ref, plane_ref, *refs):
+    *out_refs, all_ref, sems = refs
+    extract(u_ref, plane_ref, 3, nb, edge, eager)
+    pack_wide(tab_ref, slots, devices, plane_ref, all_ref, nb)
+    start = 0
+    copies = []
+    for k, out_ref in enumerate(out_refs):
+        count = out_ref.shape[0]
+        copies.append(
+            pltpu.make_async_copy(all_ref.at[start : start + count], out_ref, sems.at[k])
+        )
+        copies[-1].start()
+        start += count
+    for copy in copies:
+        copy.wait()
 
 
 def near_layers(near_ref, add_ref, new_ref, nb, edge):
@@ -543,7 +543,9 @@
     lax.fori_loop(0, 5, body, 0)
 
 
-def coarse_kernel(nb, edge, parents_here, slots, tab_ref, plane_ref, near_ref, recv_ref, *refs):
+def coarse_kernel(
+    nb, edge, eager, parents_here, slots, thin, tab_ref, plane_ref, near_ref, recv_ref, *refs
+):
     *over_ref, add_ref, face_ref, send_ref, rim_ref, ghost_ref, new_ref = refs
     unpack_wide(tab_ref, slots, recv_ref, over_ref[0] if over_ref else None, ghost_ref, nb)
     for face in range(6):
@@ -553,14 +555,14 @@
                 rim_ref[face, c, 2 * p : 2 * p + 2, :] = ghost_ref[
                     face, c, block_rows(block, nb, 2), :
                 ]
-    face_fluxes(plane_ref, ghost_ref, add_ref, face_ref, nb)
+    face_fluxes(plane_ref, ghost_ref, add_ref, face_ref, nb, eager)
     near_layers(near_ref, add_ref, new_ref, nb, edge)
-    pack(tab_ref, 3, 5, new_ref, send_ref, 2, nb)
-
-
-def coarse_cells_kernel(nb, edge, d_ref, add_ref, new_ref, temp_ref):
+    pack(tab_ref, 3, 5, thin, new_ref, send_ref, 2, nb)
+
+
+def coarse_cells_kernel(nb, edge, eager, d_ref, add_ref, new_ref, temp_ref):
     temp_ref[...] = add_ref[...]
-    expand_add(d_ref, temp_ref, new_ref, 2, nb, edge)
+    expand_add(d_ref, temp_ref, new_ref, 2, nb, edge, eager)
 
 
 def rims_kernel(nb, parents_here, tab_ref, recv_ref, rim_ref):
@@ -609,15 +611,16 @@
 
 
 def fine_kernel(
-    nb, edge, parents_here, tab_ref, bits_ref, d_ref, plane_ref, rim_ref, new_ref, face_ref,
-    ghost_ref, add_ref, base_ref, sem,
+    nb, edge, eager, parents_here, tab_ref, bits_ref, d_ref, plane_ref, rim_ref, new_ref, next_ref,
+    face_ref, ghost_ref, add_ref, half_ref, base_ref, sem,
 ):
     fetch = pltpu.make_async_copy(d_ref, base_ref, sem)
     fetch.start()
     fine_ghosts(nb, edge, tab_ref, bits_ref, plane_ref, rim_ref, None, ghost_ref, parents_here)
-    face_fluxes(plane_ref, ghost_ref, add_ref, face_ref, nb)
+    face_fluxes(plane_ref, ghost_ref, add_ref, face_ref, nb, eager)
     fetch.wait()
-    expand_add(base_ref, add_ref, new_ref, 2, nb, edge)
+    expand_add(base_ref, add_ref, half_ref, 2, nb, edge, eager)
+    inner_kernel(nb, edge, eager, half_ref, new_ref, next_ref)
 
 
 def face_means(nb, edge, parents_here, tab_ref, one_ref, two_ref, mean_ref, quarter_ref):
@@ -647,8 +650,8 @@
         for p in range(parents_here):
             for half in range(2):
                 octant = (face % 2) * BIT_OF[axis] + half * TANGENT[axis][0]
-                one = tab_ref[15 + p, octant]
-                two = tab_ref[15 + p, octant + TANGENT[axis][1]]
+                one = tab_ref[CHILDREN + p, octant]
+                two = tab_ref[CHILDREN + p, octant + TANGENT[axis][1]]
                 value = jnp.where(
                     left,
                     quarter_ref[face, pl.ds(one, 5, stride=nb), :],
@@ -659,11 +662,11 @@
 
 
 def means_kernel(
-    nb, edge, parents_here, tab_ref, bits_ref, plane_ref, rim_ref, rim2_ref, one_ref, send_ref,
+    nb, edge, eager, parents_here, tab_ref, bits_ref, plane_ref, rim_ref, rim2_ref, one_ref, send_ref,
     add_ref, ghost_ref, face_ref, quarter_ref, mean_ref,
 ):
     fine_ghosts(nb, edge, tab_ref, bits_ref, plane_ref, rim_ref, rim2_ref, ghost_ref, parents_here)
-    face_fluxes(plane_ref, ghost_ref, add_ref, face_ref, nb)
+    face_fluxes(plane_ref, ghost_ref, add_ref, face_ref, nb, eager)
     face_means(nb, edge, parents_here, tab_ref, one_ref, face_ref, mean_ref, quarter_ref)
     for face in range(6):
         for p in range(parents_here):
@@ -675,11 +678,11 @@
 
 
 def finish_kernel(
-    nb, edge, parents_here, tab_ref, d_ref, add_ref, new_ref, average_ref, temp_ref, split_ref,
+    nb, edge, eager, parents_here, tab_ref, d_ref, add_ref, new_ref, average_ref, temp_ref, split_ref,
     eighth_ref,
 ):
     temp_ref[...] = add_ref[...]
-    expand_add(d_ref, temp_ref, new_ref, 2, nb, edge, split_ref)
+    expand_add(d_ref, temp_ref, new_ref, 2, nb, edge, eager, split_ref)
     averages(nb, edge, parents_here, tab_ref, split_ref, average_ref, eighth_ref)
 
 
@@ -702,8 +705,8 @@
     left = lane % edge < edge // 2
     for p in range(parents_here):
         for corner in range(4):
-            one = tab_ref[15 + p, 2 * corner]
-            two = tab_ref[15 + p, 2 * corner + 1]
+            one = tab_ref[CHILDREN + p, 2 * corner]
+            two = tab_ref[CHILDREN + p, 2 * corner + 1]
             rows = slice(corner // 2 * ROWS, (corner // 2 + 1) * ROWS)
             lanes = slice(corner % 2 * LANES, (corner % 2 + 1) * LANES)
             for c in range(5):
@@ -711,12 +714,12 @@
 
 
 def correct_kernel(
-    nb, edge, parents_here, tab_ref, bits_ref, new_ref, face_ref, recv_ref, cells_ref, out_ref,
-    mean_ref, add_ref, base_ref, sem,
+    nb, edge, eager, parents_here, slots, tab_ref, bits_ref, new_ref, face_ref, recv_ref, cells_ref,
+    out_ref, mean_ref, add_ref, done_ref, base_ref, sem, sems,
 ):
     fetch = pltpu.make_async_copy(new_ref, base_ref, sem)
     fetch.start()
-    unpack(tab_ref, 3, 8, recv_ref, mean_ref, 2, nb)
+    unpack(tab_ref, 8, slots, recv_ref, mean_ref, 2, nb)
     beside = bits_ref[2 * nb : 3 * nb, :]
     for face in range(6):
         sign = STEP_RATIO if face % 2 else -STEP_RATIO
@@ -730,7 +733,12 @@
     fetch.wait()
     for p in range(parents_here):
         base_ref[tab_ref[9, p]] = cells_ref[p]
-    expand_add(base_ref, add_ref, out_ref, 1, nb, edge)
+    copies = [
+        pltpu.make_async_copy(done_ref.at[:, c], out_ref.at[:, c], sems.at[c]) for c in range(5)
+    ]
+    expand_add(base_ref, add_ref, done_ref, 1, nb, edge, eager, copies=copies)
+    for copy in copies:
+        copy.wait()
 
 
 def column(row):
@@ -819,8 +827,12 @@
     for bit in BIT_OF:
         partner = (octant + bit - 2 * bit * (octant // bit % 2)).astype(F32)
         rows.append(pick((parent_column == parent_f) & (octant_column == partner), row_f))
-    for p in range(parents_here):
-        rows.append(pick((slot_column == p) & (octant_column == lane_f), row_f))
+    children = [
+        pick((slot_column == p) & (octant_column == lane_f), row_f) for p in range(parents_here)
+    ]
+    free = mine & (owned_column == False)
+    place = column(lane - count(mine & owned_column & (row < lane)))
+    others = pick(free & (place == lane_f), row_f)
 
     most = jnp.zeros((devices, LANES), F32)
     most_all = jnp.zeros((devices, LANES), F32)
@@ -844,6 +856,7 @@
     for values in (most, most_all):
         values = jnp.max(jnp.max(values, axis=0, keepdims=True), axis=1, keepdims=True)
         rows.append(jnp.broadcast_to(values, (1, LANES)).astype(I32))
+    rows = rows + [others, jnp.broadcast_to(blk_ref[0], (1, LANES))] + children
     for k, values in enumerate(rows):
         tab_ref[k : k + 1, :] = values
 
@@ -855,21 +868,26 @@
         bits_ref[k * nb : (k + 1) * nb, :] = values[0:nb, :].astype(I32)
 
 
-def run(kernel, outs, operands, scratch=(), scalars=0, far=None, flops=0):
+def run(
+    kernel, outs, operands, scratch=(), scalars=0, far=None, remote=(), copies=None, flops=0
+):
     held = [o.shape for o in operands] + list(outs) + list(scratch)
     limit = sum(4 * max(math.prod(s), 8 * LANES) for s in held) + SPARE
     smem = pl.BlockSpec(memory_space=pltpu.SMEM)
     vmem = pl.BlockSpec(memory_space=pltpu.VMEM)
+    hbm = pl.BlockSpec(memory_space=pltpu.HBM)
     specs = [smem if k < scalars else vmem for k in range(len(operands))]
     scratches = [pltpu.VMEM(s, F32) for s in scratch]
     if far is not None:
-        specs[far] = pl.BlockSpec(memory_space=pltpu.HBM)
+        specs[far] = hbm
         scratches.append(pltpu.SemaphoreType.DMA)
+    if remote:
+        scratches.append(pltpu.SemaphoreType.DMA((copies or len(remote),)))
     return pl.pallas_call(
         kernel,
         out_shape=[jax.ShapeDtypeStruct(s, F32) for s in outs],
         in_specs=specs,
-        out_specs=[vmem] * len(outs),
+        out_specs=[hbm if k in remote else vmem for k in range(len(outs))],
         scratch_shapes=scratches,
         compiler_params=pltpu.CompilerParams(vmem_limit_bytes=limit),
         cost_estimate=pl.CostEstimate(
@@ -907,7 +925,7 @@
     table, bits = pl.pallas_call(
         functools.partial(tables_kernel, nb, devices, parents_here),
         out_shape=[
-            jax.ShapeDtypeStruct((17 + parents_here, LANES), I32),
+            jax.ShapeDtypeStruct((CHILDREN + parents_here, LANES), I32),
             jax.ShapeDtypeStruct((3 * nb, LANES), I32),
         ],
         in_specs=[smem, hbm, hbm],
@@ -917,12 +935,12 @@
             pltpu.VMEM(parents.shape[::-1], I32),
             pltpu.SemaphoreType.DMA((2,)),
         ],
-        compiler_params=pltpu.CompilerParams(vmem_limit_bytes=2 * SPARE),
+        compiler_params=pltpu.CompilerParams(vmem_limit_bytes=7 * SPARE),
     )(jnp.reshape(blk_index, (1,)).astype(I32), neighbours.T, parents.T)
 
     few = max(1, capacity // 3)
     half = max(1, capacity // 2)
-    counts = table[15 + parents_here : 17 + parents_here, 0]
+    counts = table[COUNTS : COUNTS + 2, 0]
     finished = lax.cond(
         (counts[0] <= few) & (counts[1] <= half) & (devices % 2 == 0),
         functools.partial(step, capacity, half, few),
@@ -935,6 +953,7 @@
 
 
 def step(capacity, wide, slots, u, table, bits):
+    eager = wide < capacity
     level_id = lax.axis_index("level")
     devices = lax.axis_size("blk")
     nb, _, edge, square = u.shape
@@ -945,32 +964,37 @@
     ghost_shape = (6, 5, 4 * nb, LANES)
     face_shape = (6, 5, 2 * nb, LANES)
     rim_shape = (6, 5, 2 * parents_here, LANES)
-    wide_send = (devices, wide * 5, 4, LANES)
-    over_send = [((capacity - wide) * 5, 4, LANES)] if wide < capacity else []
+    wide_sends = [(devices * wide * 5, 4, LANES)]
+    if wide < capacity:
+        wide_sends.append(((capacity - wide) * 5, 4, LANES))
     thin_send = (devices, slots * 5, 2, LANES)
     average_shape = (parents_here,) + cell_shape[1:]
     work = 220 * 3 * 5 * nb * edge * square
 
     def inner(cells):
-        return run(part(inner_kernel, nb, edge), [cell_shape, plane_shape], [cells], flops=work)
+        return run(part(inner_kernel, nb, edge, False), [cell_shape, plane_shape], [cells], flops=work)
 
     def half_way_round(buffer):
         turned = [(d, (d + devices // 2) % devices) for d in range(devices)]
         return lax.ppermute(buffer, ("level", "blk"), turned)
 
     def coarse_first(u):
-        send, *over = run(
-            part(send_kernel, nb, edge, wide), [wide_send] + over_send, [table, u], [ghost_shape], 1
+        planes, *sends = run(
+            part(send_kernel, nb, edge, eager, wide, devices),
+            [plane_shape] + wide_sends,
+            [table, u],
+            [(sum(x[0] for x in wide_sends), 4, LANES)],
+            1,
+            remote=range(1, 1 + len(wide_sends)),
         )
-        received = [route(send)] + [half_way_round(buffer) for buffer in over]
-        partial_new, planes, near = run(
-            part(coarse_inner_kernel, nb, edge),
-            [cell_shape, plane_shape, face_shape],
-            [u],
+        received = [route(sends[0].reshape(devices, wide * 5, 4, LANES))]
+        received += [half_way_round(buffer) for buffer in sends[1:]]
+        partial_new, near = run(
+            part(coarse_inner_kernel, nb, edge, False), [cell_shape, face_shape], [table, u], (), 1,
             flops=work,
         )
         adds, faces, send, rims = run(
-            part(coarse_kernel, nb, edge, parents_here, wide),
+            part(coarse_kernel, nb, edge, eager, parents_here, wide, slots),
             [ghost_shape, face_shape, thin_send, rim_shape],
             [table, planes, near] + received,
             [ghost_shape, face_shape],
@@ -990,7 +1014,7 @@
     def coarse_second(send, partial_new, adds, planes, early_rims):
         received = route(send)
         (cells,) = run(
-            part(coarse_cells_kernel, nb, edge),
+            part(coarse_cells_kernel, nb, edge, False),
             [cell_shape],
             [partial_new, adds],
             [ghost_shape],
@@ -1000,15 +1024,16 @@
         return (late, cells, *blank(plane_shape, face_shape))
 
     def fine_second(send, partial_new, adds, planes, early_rims):
-        half, faces = run(
-            part(fine_kernel, nb, edge, parents_here),
-            [cell_shape, face_shape],
+        results = run(
+            part(fine_kernel, nb, edge, eager, parents_here),
+            [cell_shape, plane_shape, face_shape],
             [table, bits, partial_new, planes, early_rims],
-            [ghost_shape, ghost_shape, cell_shape],
+            [ghost_shape, ghost_shape, cell_shape, cell_shape],
             1,
             far=2,
+            flops=work,
         )
-        return (*blank(rim_shape), *inner(half), faces)
+        return (*blank(rim_shape), *results)
 
     late, cells, half_planes, half_faces = lax.cond(
         level_id == 0, coarse_second, fine_second, send, partial_new, adds, planes, early_rims
@@ -1020,7 +1045,7 @@
 
     def fine_third(cells, half_planes, half_faces, early_rims, late_rims):
         send, adds = run(
-            part(means_kernel, nb, edge, parents_here),
+            part(means_kernel, nb, edge, eager, parents_here),
             [thin_send, ghost_shape],
             [table, bits, half_planes, early_rims, late_rims, half_faces],
             [ghost_shape, face_shape, (6, 5 * nb, LANES), rim_shape],
@@ -1028,7 +1053,7 @@
         )
         received = route(send)
         out, averaged = run(
-            part(finish_kernel, nb, edge, parents_here),
+            part(finish_kernel, nb, edge, False, parents_here),
             [cell_shape, average_shape],
             [table, cells, adds],
             [ghost_shape, (nb, 5, 2, edge, LANES), (nb, 5, ROWS, LANES)],
@@ -1046,12 +1071,14 @@
 
     def correct(out, cells, faces, returned, averaged):
         return run(
-            part(correct_kernel, nb, edge, parents_here),
+            part(correct_kernel, nb, edge, eager, parents_here, slots),
             [cell_shape],
             [table, bits, cells, faces, returned, averaged],
-            [face_shape, face_shape, cell_shape],
+            [face_shape, face_shape, cell_shape, cell_shape],
             1,
             far=2,
+            remote=range(1),
+            copies=5,
         )[0]
 
     return lax.cond(

time: 98.3 us -> 86.3 us (0.88)
  Pallas kernels: 40 us -> 32.5 us
  starting transfers between devices: 27.2 us -> 25.4 us
  local copies, waits for them, and re-layouts: 1.96 us -> 0.54 us
    pallas_call x6, Pallas kernels: 39.4 us -> 31.1 us  [run(): pl.pallas_call(kernel, out_shape=[jax.ShapeDtypeStruct(s, F32) for s in o...]
    ppermute x4, starting transfers between devices: 9.57 us -> 7.73 us  [level_shift(): return lax.ppermute(array, 'level', [(source, 1 - source)])]
    unnamed x4 -> x0, local copies, waits for them, and re-layouts: 1.38 us -> none
  transfers between devices with their start and end apart: 7 -> 7, of which waited for: 4 -> 5; matrix products, arithmetic and copies ran while one was open for 0% -> 0% of each run, Pallas kernels for 20% -> 18%
where the time goes in v4:
time: 86.3 us; the launch traced here: 85.7 us
  Pallas kernels  32.5 us (38%)
  starting transfers between devices  25.4 us (29%)
  waiting for transfers between devices  25.1 us (29%)
  between operations  1.52 us (2%)
    pallas_call x6, Pallas kernels, run(): pl.pallas_call(kernel, out_shape=[jax.ShapeDtypeStruct(s, F32) for s in o...  31.1 us
    ppermute x4, waiting for transfers between devices, level_shift(): return lax.ppermute(array, 'level', [(source, 1 - source)])  19.9 us
    all_to_all x2, starting transfers between devices, route(): lax.all_to_all(buffer, 'blk', split_axis=0, concat_axis=0, tiled=True)  13 us
    ppermute x4, starting transfers between devices, level_shift(): return lax.ppermute(array, 'level', [(source, 1 - source)])  7.73 us
    all_to_all x2, waiting for transfers between devices, route(): lax.all_to_all(buffer, 'blk', split_axis=0, concat_axis=0, tiled=True)  5.09 us
    ppermute x1, starting transfers between devices, half_way_round(): return lax.ppermute(buffer, ('level', 'blk'), turned)  4.72 us
  transfers between devices with their start and end apart: 7, of which 5 were waited for; matrix products, arithmetic and copies ran while one was open for 0% of the time, Pallas kernels for 18%

profile of v4, /device:TPU:0, one launch (start us, length us, event | category | flops | bytes accessed | tf_op | source)
XLA Modules:
  0.0 85.7 jit_solution(9300508438352906949)
XLA Ops:
  0.0 1.4 %shard_map.39 = (s32[21,128]{1,0:T(8,128)S(1)}, s32[48,128]{1,0:T(8,128)S(1)}) custom-call(s32[1]{0:T(128)} %bitcast.6.blk_ref, s32[6,256]{1,0:T(8,128)} %bitcast.14, s32[2,256]{1,0:T(2,128)} %bitcast.15), custom_call_target="tpu_custom_call" | custom-call | tf_op jit(solution)/shard_map/pallas_call | solution.py:925
  1.4 0.5 fusion
  3.2 82.3 %conditional.9 = ((f32[1,16,5,16,256]{4,3,2,1,0:T(8,128)})) conditional(s32[]{:T(128)} %bitcast.9, (f32[16,5,16,256]{3,2,1,0:T(8,128)}, s32[21,128]{1,0:T(8,128)S(1)}, s32[48,128]{1,0:T(8,128)S(1)}) %tuple.103, (f32[16,5,16,256]{3,2,1,0:T(8,128)}, s32[21,128]{1,0:T(8,128)S(1)}, s32[48,128]{1,0:T(8,128)S(1)}) %tuple.104), branch_computations={%region_0.0_spmd, %region_9.0_spmd} | conditional | flops 648806400 | bytes 45959360 | solution.py:944
  3.5 36.0 %conditional.4 = (f32[16,5,16,256]{3,2,1,0:T(8,128)}, f32[6,5,64,128]{3,2,1,0:T(8,128)}, f32[6,5,32,128]{3,2,1,0:T(8,128)}, f32[16,20,2,128]{3,2,1,0:T(2,128)}, ...) conditional(s32[]{:T(128)} %convert_element_type.10, ...), branch_computations={%region_10.0_spmd, %region_11.0_spmd} | conditional | flops 216268800 | bytes 8859256 | solution.py:1009
  3.5 4.9 %branch_1_fun.28 = (f32[6,5,96,128]{3,2,1,0:T(8,128)S(1)}, f32[480,4,128]{2,1,0:T(4,128)}, f32[30,4,128]{2,1,0:T(4,128)S(1)}) custom-call(s32[21,128]{1,0:T(8,128)S(1)} %get-tuple-element.198.tab_ref, f32[16,5,16,256]{3,2,1,0:T(8,128)} %get-tuple-element.199.u_ref), custom_call_target="tpu_custom_call" | custom-call | bytes 1321472 | tf_op jit(solution)/shard_map/cond/branch_1_fun/cond/branch_1_fun/pallas_call | solution.py:886
  8.4 8.3 %all-to-all-start.3 = ((f32[16,30,4,128]{3,2,1,0:T(4,128)}), f32[16,30,4,128]{3,2,1,0:T(4,128)S(1)}, u32[]{:S(2)}, u32[]{:S(2)}) async-start(f32[16,30,4,128]{3,2,1,0:T(4,128)} %bitcast.3), calls=%async_computation.3 | async-start | bytes 1966080 | tf_op jit(solution)/shard_map/cond/branch_1_fun/cond/branch_1_fun/all_to_all | solution.py:912
  16.8 4.7 %collective-permute-start.4 = (f32[30,4,128]{2,1,0:T(4,128)S(1)}, f32[30,4,128]{2,1,0:T(4,128)S(1)}, u32[]{:S(2)}, u32[]{:S(2)}) collective-permute-start(f32[30,4,128]{2,1,0:T(4,128)S(1)} %get-tuple-element.204), channel_id=1, source_target_pairs={{0,8},{1,9},{2,10},{3,11},{4,12},{5,13},{6,14},{7,15},{8,0},{9,1},... | collective-permute-start | bytes 184328 | tf_op jit(solution)/shard_map/cond/branch_1_fun/cond/branch_1_fun/ppermute | solution.py:979
  21.5 11.7 %branch_1_fun.27 = (f32[16,5,16,256]{3,2,1,0:T(8,128)}, f32[6,5,32,128]{3,2,1,0:T(8,128)S(1)}) custom-call(s32[21,128]{1,0:T(8,128)S(1)} %get-tuple-element.198.tab_ref, f32[16,5,16,256]{3,2,1,0:T(8,128)} %get-tuple-element.199.u_ref), custom_call_target="tpu_custom_call" | custom-call | flops 216268800 | bytes 1321472 | tf_op jit(solution)/shard_map/cond/branch_1_fun/cond/branch_1_fun/pallas_call | solution.py:886
  33.2 0.1 collective-permute-done.4.refs_0_
  33.2 6.3 %branch_1_fun.29 = (f32[6,5,64,128]{3,2,1,0:T(8,128)}, f32[6,5,32,128]{3,2,1,0:T(8,128)}, f32[16,20,2,128]{3,2,1,0:T(2,128)}, f32[6,5,4,128]{3,2,1,0:T(4,128)S(1)}) custom-call(s32[21,128]{1,0:T(8,128)S(1)} %get-tuple-element.198.tab_ref, f32[6,5,96,128]{3,2,1,0:T(8,128)S(1)} %get-tuple-element.201.plane_ref, ...), custom_call_target="tpu_custom_call" | custom-call | bytes 3021312 | tf_op jit(solution)/shard_map/cond/branch_1_fun/cond/branch_1_fun/pallas_call | solution.py:886
  39.5 1.3 %collective-permute-start.5 = (f32[6,5,4,128]{3,2,1,0:T(4,128)S(1)}, f32[6,5,4,128]{3,2,1,0:T(4,128)S(1)}, u32[]{:S(2)}, u32[]{:S(2)}) collective-permute-start(f32[6,5,4,128]{3,2,1,0:T(4,128)S(1)} %get-tuple-element.245), channel_id=1, source_target_pairs={{0,16},{1,17},{2,18},{3,19},{4,20},{5,21},{6,22},{7,23},{8,24},{9,... | collective-permute-start | bytes 184328 | tf_op jit(solution)/shard_map/cond/branch_1_fun/ppermute | solution.py:908
  40.8 0.9 %collective-permute-done.5 = f32[6,5,4,128]{3,2,1,0:T(4,128)S(1)} collective-permute-done((f32[6,5,4,128]{3,2,1,0:T(4,128)S(1)}, f32[6,5,4,128]{3,2,1,0:T(4,128)S(1)}, u32[]{:S(2)}, u32[]{:S(2)}) %collective-permute-start.5) | collective-permute-done | bytes 61472 | tf_op jit(solution)/shard_map/cond/branch_1_fun/ppermute | solution.py:908
  41.7 14.4 %conditional.5 = (f32[6,5,4,128]{3,2,1,0:T(4,128)S(1)}, f32[16,5,16,256]{3,2,1,0:T(8,128)S(1)}, f32[6,5,96,128]{3,2,1,0:T(8,128)}, f32[6,5,32,128]{3,2,1,0:T(8,128)S(1)}) conditional(s32[]{:T(128)} %convert_element_type.10, (s32[21,128]{1,0:T(8,128)S(1)}, s32[48,128]{1,0:T(8,128)S(1)}, f32[16,5,16,256]{3,2,1,0:T(8,128)}, ...), branch_computations={%region_12.0_spmd, %region_13.0_spmd} | conditional | flops 216268800 | bytes 3615296 | solution.py:1038
  41.7 4.6 %all-to-all-start.4 = ((f32[16,20,2,128]{3,2,1,0:T(2,128)}), f32[16,20,2,128]{3,2,1,0:T(2,128)S(1)}, u32[]{:S(2)}, u32[]{:S(2)}) async-start(f32[16,20,2,128]{3,2,1,0:T(2,128)} %get-tuple-element.218), calls=%async_computation.4 | async-start | bytes 655360 | tf_op jit(solution)/shard_map/cond/branch_1_fun/cond/branch_1_fun/all_to_all | solution.py:912
  46.3 3.9 %branch_1_fun.32 = f32[16,5,16,256]{3,2,1,0:T(8,128)S(1)} custom-call(f32[16,5,16,256]{3,2,1,0:T(8,128)} %get-tuple-element.219.d_ref, f32[6,5,64,128]{3,2,1,0:T(8,128)} %get-tuple-element.220.add_ref), custom_call_target="tpu_custom_call" | custom-call | flops 54067200 | bytes 2293760 | tf_op jit(solution)/shard_map/cond/branch_1_fun/cond/branch_1_fun/pallas_call | solution.py:886
  50.2 5.1 %all-to-all-done.4.recv_ref = f32[16,20,2,128]{3,2,1,0:T(2,128)S(1)} async-done(((f32[16,20,2,128]{3,2,1,0:T(2,128)}), f32[16,20,2,128]{3,2,1,0:T(2,128)S(1)}, u32[]{:S(2)}, u32[]{:S(2)}) %all-to-all-start.4) | async-done | bytes 327712 | tf_op jit(solution)/shard_map/cond/branch_1_fun/cond/branch_1_fun/all_to_all | solution.py:912
  55.3 0.8 branch_1_fun.31
  56.1 3.9 %collective-permute-start.6 = (f32[6,5,4,128]{3,2,1,0:T(4,128)S(1)}, f32[6,5,4,128]{3,2,1,0:T(4,128)S(1)}, u32[]{:S(2)}, u32[]{:S(2)}) collective-permute-start(f32[6,5,4,128]{3,2,1,0:T(4,128)S(1)} %get-tuple-element.249), channel_id=1, source_target_pairs={{0,16},{1,17},{2,18},{3,19},{4,20},{5,21},{6,22},{7,23},{8,24},{9,... | collective-permute-start | bytes 184328 | tf_op jit(solution)/shard_map/cond/branch_1_fun/ppermute | solution.py:908
  60.0 0.9 %collective-permute-done.6 = f32[6,5,4,128]{3,2,1,0:T(4,128)S(1)} collective-permute-done((f32[6,5,4,128]{3,2,1,0:T(4,128)S(1)}, f32[6,5,4,128]{3,2,1,0:T(4,128)S(1)}, u32[]{:S(2)}, u32[]{:S(2)}) %collective-permute-start.6) | collective-permute-done | bytes 61472 | tf_op jit(solution)/shard_map/cond/branch_1_fun/ppermute | solution.py:908
  60.9 1.3 %collective-permute-start.7 = (f32[16,20,2,128]{3,2,1,0:T(2,128)S(1)}, f32[16,20,2,128]{3,2,1,0:T(2,128)S(1)}, u32[]{:S(2)}, u32[]{:S(2)}) collective-permute-start(f32[16,20,2,128]{3,2,1,0:T(2,128)S(1)} %get-tuple-element.254), channel_id=1, source_target_pairs={{16,0},{17,1},{18,2},{19,3},{20,4},{21,5},{22,6},{23,7},{24,8},{25... | collective-permute-start | bytes 983048 | tf_op jit(solution)/shard_map/cond/branch_1_fun/ppermute | solution.py:908
  62.2 1.3 %collective-permute-start.8 = (f32[2,5,16,256]{3,2,1,0:T(8,128)S(1)}, f32[2,5,16,256]{3,2,1,0:T(8,128)S(1)}, u32[]{:S(2)}, u32[]{:S(2)}) collective-permute-start(f32[2,5,16,256]{3,2,1,0:T(8,128)S(1)} %get-tuple-element.255), channel_id=1, source_target_pairs={{16,0},{17,1},{18,2},{19,3},{20,4},{21,5},{22,6},{23,7},{24,8},{25... | collective-permute-start | bytes 491528 | tf_op jit(solution)/shard_map/cond/branch_1_fun/ppermute | solution.py:908
  63.5 18.2 %collective-permute-done.8 = f32[2,5,16,256]{3,2,1,0:T(8,128)S(1)} collective-permute-done((f32[2,5,16,256]{3,2,1,0:T(8,128)S(1)}, f32[2,5,16,256]{3,2,1,0:T(8,128)S(1)}, u32[]{:S(2)}, u32[]{:S(2)}) %collective-permute-start.8) | collective-permute-done | bytes 163872 | tf_op jit(solution)/shard_map/cond/branch_1_fun/ppermute | solution.py:908
  81.6 3.6 %conditional.7 = (f32[1,16,5,16,256]{4,3,2,1,0:T(8,128)}) conditional(s32[]{:T(128)} %convert_element_type.10, f32[16,5,16,256]{3,2,1,0:T(8,128)} %get-tuple-element.252, (s32[21,128]{1,0:T(8,128)S(1)}, s32[48,128]{1,0:T(8,128)S(1)}, f32[16,5,16,256]{3,2,1,0:T(8,128)S(1)}, f32[6,5,32,128]{3,2,1,0:T(8,128)}, f32[16,20,2,128]{3,2,1,0:T(2,128)S(1)}, ...), branch_computations={%region_16.0_spmd, %region_17.0_spmd} | conditional | bytes 2329096 | solution.py:1084
  81.6 3.6 %branch_1_fun.35 = f32[16,5,16,256]{3,2,1,0:T(8,128)} custom-call(s32[21,128]{1,0:T(8,128)S(1)} %get-tuple-element.234.tab_ref, s32[48,128]{1,0:T(8,128)S(1)} %get-tuple-element.235.bits_ref, f32[16,5,16,256]{3,2,1,0:T(8,128)S(1)} %get-tuple-element.236.new_ref, f32[6,5,32,128]{3,2,1,0:T(8,128)} %get-tuple-element.237.face_ref, ...), custom_call_target="tpu_custom_call" | custom-call | bytes 2329088 | tf_op jit(solution)/shard_map/cond/branch_1_fun/cond/branch_1_fun/pallas_call | solution.py:886
  (6 shorter events, 0.0 us)
Async XLA Ops:
  8.4 24.8 %all-to-all-start.3 = ((f32[16,30,4,128]{3,2,1,0:T(4,128)}), f32[16,30,4,128]{3,2,1,0:T(4,128)S(1)}, u32[]{:S(2)}, u32[]{:S(2)}) async-start(f32[16,30,4,128]{3,2,1,0:T(4,128)} %bitcast.3), calls=%async_computation.3 | async-start | bytes 1966080 | tf_op jit(solution)/shard_map/cond/branch_1_fun/cond/branch_1_fun/all_to_all | solution.py:912
  16.8 16.5 %collective-permute-start.4 = (f32[30,4,128]{2,1,0:T(4,128)S(1)}, f32[30,4,128]{2,1,0:T(4,128)S(1)}, u32[]{:S(2)}, u32[]{:S(2)}) collective-permute-start(f32[30,4,128]{2,1,0:T(4,128)S(1)} %get-tuple-element.204), channel_id=1, source_target_pairs={{0,8},{1,9},{2,10},{3,11},{4,12},{5,13},{6,14},{7,15},{8,0},{9,1},... | collective-permute-start | bytes 184328 | tf_op jit(solution)/shard_map/cond/branch_1_fun/cond/branch_1_fun/ppermute | solution.py:979
  39.5 2.2 %collective-permute-start.5 = (f32[6,5,4,128]{3,2,1,0:T(4,128)S(1)}, f32[6,5,4,128]{3,2,1,0:T(4,128)S(1)}, u32[]{:S(2)}, u32[]{:S(2)}) collective-permute-start(f32[6,5,4,128]{3,2,1,0:T(4,128)S(1)} %get-tuple-element.245), channel_id=1, source_target_pairs={{0,16},{1,17},{2,18},{3,19},{4,20},{5,21},{6,22},{7,23},{8,24},{9,... | collective-permute-start | bytes 184328 | tf_op jit(solution)/shard_map/cond/branch_1_fun/ppermute | solution.py:908
  41.7 13.6 %all-to-all-start.4 = ((f32[16,20,2,128]{3,2,1,0:T(2,128)}), f32[16,20,2,128]{3,2,1,0:T(2,128)S(1)}, u32[]{:S(2)}, u32[]{:S(2)}) async-start(f32[16,20,2,128]{3,2,1,0:T(2,128)} %get-tuple-element.218), calls=%async_computation.4 | async-start | bytes 655360 | tf_op jit(solution)/shard_map/cond/branch_1_fun/cond/branch_1_fun/all_to_all | solution.py:912
  56.1 4.8 %collective-permute-start.6 = (f32[6,5,4,128]{3,2,1,0:T(4,128)S(1)}, f32[6,5,4,128]{3,2,1,0:T(4,128)S(1)}, u32[]{:S(2)}, u32[]{:S(2)}) collective-permute-start(f32[6,5,4,128]{3,2,1,0:T(4,128)S(1)} %get-tuple-element.249), channel_id=1, source_target_pairs={{0,16},{1,17},{2,18},{3,19},{4,20},{5,21},{6,22},{7,23},{8,24},{9,... | collective-permute-start | bytes 184328 | tf_op jit(solution)/shard_map/cond/branch_1_fun/ppermute | solution.py:908
  60.9 20.8 %collective-permute-start.7 = (f32[16,20,2,128]{3,2,1,0:T(2,128)S(1)}, f32[16,20,2,128]{3,2,1,0:T(2,128)S(1)}, u32[]{:S(2)}, u32[]{:S(2)}) collective-permute-start(f32[16,20,2,128]{3,2,1,0:T(2,128)S(1)} %get-tuple-element.254), channel_id=1, source_target_pairs={{16,0},{17,1},{18,2},{19,3},{20,4},{21,5},{22,6},{23,7},{24,8},{25... | collective-permute-start | bytes 983048 | tf_op jit(solution)/shard_map/cond/branch_1_fun/ppermute | solution.py:908
  62.2 19.5 %collective-permute-start.8 = (f32[2,5,16,256]{3,2,1,0:T(8,128)S(1)}, f32[2,5,16,256]{3,2,1,0:T(8,128)S(1)}, u32[]{:S(2)}, u32[]{:S(2)}) collective-permute-start(f32[2,5,16,256]{3,2,1,0:T(8,128)S(1)} %get-tuple-element.255), channel_id=1, source_target_pairs={{16,0},{17,1},{18,2},{19,3},{20,4},{21,5},{22,6},{23,7},{24,8},{25... | collective-permute-start | bytes 491528 | tf_op jit(solution)/shard_map/cond/branch_1_fun/ppermute | solution.py:908

commit v5 on v4

--- a/solution.py
+++ b/solution.py
@@ -386,7 +386,7 @@
                 rim_ref[face, c, 2 * p : 2 * p + 2, :] = recv_ref[target, first + c, 0:2, :]
 
 
-def interior(nb, edge, eager, u_ref, d_ref, tab_ref=None):
+def interior(nb, edge, eager, u_ref, d_ref, tab_ref=None, axes=(0, 1, 2), from_ref=None):
     square = edge * edge
 
     def sweep(u, axis, index, size, step, dim):
@@ -399,8 +399,11 @@
         flux = [jnp.where(inside, x, 0.0) for x in hllc(prev, low, n)]
         return [pltpu.roll(x, size - step, dim) - x for x in flux]
 
+    columns = {0: (iota((edge, LANES), 0), edge, 1, 0), 2: (iota((edge, LANES), 1) % edge, LANES, 1, 1)}
+    from_ref = d_ref if from_ref is None else from_ref
+
     def work(b):
-        for rt in range(edge // ROWS):
+        for rt in range(edge // ROWS if 1 in axes else 0):
             rows = slice(rt * ROWS, (rt + 1) * ROWS)
             u = [u_ref[b, c, rows, :] for c in range(5)]
             div = sweep(u, 1, iota((ROWS, square), 1) // edge, square, edge, 1)
@@ -409,10 +412,10 @@
         for half in range(square // LANES):
             lanes = slice(half * LANES, (half + 1) * LANES)
             u = [u_ref[b, c, :, lanes] for c in range(5)]
-            div = sweep(u, 0, iota((edge, LANES), 0), edge, 1, 0)
-            more = sweep(u, 2, iota((edge, LANES), 1) % edge, LANES, 1, 1)
-            for c in range(5):
-                d_ref[b, c, :, lanes] = d_ref[b, c, :, lanes] - STEP_RATIO * (div[c] + more[c])
+            parts = [sweep(u, axis, *columns[axis]) for axis in (0, 2) if axis in axes]
+            for c in range(5):
+                total = sum(part[c] for part in parts)
+                d_ref[b, c, :, lanes] = from_ref[b, c, :, lanes] - STEP_RATIO * total
 
     def body(k, carry):
         work(k if tab_ref is None else tab_ref[OTHERS, k])
@@ -612,7 +615,7 @@
 
 def fine_kernel(
     nb, edge, eager, parents_here, tab_ref, bits_ref, d_ref, plane_ref, rim_ref, new_ref, next_ref,
-    face_ref, ghost_ref, add_ref, half_ref, base_ref, sem,
+    face_ref, half_ref, ghost_ref, add_ref, base_ref, sem,
 ):
     fetch = pltpu.make_async_copy(d_ref, base_ref, sem)
     fetch.start()
@@ -620,7 +623,8 @@
     face_fluxes(plane_ref, ghost_ref, add_ref, face_ref, nb, eager)
     fetch.wait()
     expand_add(base_ref, add_ref, half_ref, 2, nb, edge, eager)
-    inner_kernel(nb, edge, eager, half_ref, new_ref, next_ref)
+    extract(half_ref, next_ref, 3, nb, edge, eager)
+    interior(nb, edge, eager, half_ref, new_ref, axes=(1, 2))
 
 
 def face_means(nb, edge, parents_here, tab_ref, one_ref, two_ref, mean_ref, quarter_ref):
@@ -678,11 +682,12 @@
 
 
 def finish_kernel(
-    nb, edge, eager, parents_here, tab_ref, d_ref, add_ref, new_ref, average_ref, temp_ref, split_ref,
-    eighth_ref,
+    nb, edge, eager, parents_here, tab_ref, d_ref, add_ref, half_ref, new_ref, average_ref,
+    temp_ref, split_ref, eighth_ref, base_ref,
 ):
     temp_ref[...] = add_ref[...]
-    expand_add(d_ref, temp_ref, new_ref, 2, nb, edge, eager, split_ref)
+    interior(nb, edge, eager, half_ref, base_ref, axes=(0,), from_ref=d_ref)
+    expand_add(base_ref, temp_ref, new_ref, 2, nb, edge, eager, split_ref)
     averages(nb, edge, parents_here, tab_ref, split_ref, average_ref, eighth_ref)
 
 
@@ -1021,29 +1026,29 @@
             flops=work // 4,
         )
         (late,) = run(part(rims_kernel, nb, parents_here), [rim_shape], [table, received], (), 1)
-        return (late, cells, *blank(plane_shape, face_shape))
+        return (late, cells, *blank(plane_shape, face_shape, cell_shape))
 
     def fine_second(send, partial_new, adds, planes, early_rims):
         results = run(
             part(fine_kernel, nb, edge, eager, parents_here),
-            [cell_shape, plane_shape, face_shape],
+            [cell_shape, plane_shape, face_shape, cell_shape],
             [table, bits, partial_new, planes, early_rims],
-            [ghost_shape, ghost_shape, cell_shape, cell_shape],
+            [ghost_shape, ghost_shape, cell_shape],
             1,
             far=2,
             flops=work,
         )
         return (*blank(rim_shape), *results)
 
-    late, cells, half_planes, half_faces = lax.cond(
+    late, cells, half_planes, half_faces, half = lax.cond(
         level_id == 0, coarse_second, fine_second, send, partial_new, adds, planes, early_rims
     )
     late_rims = level_shift(late, 0)
 
-    def coarse_third(cells, half_planes, half_faces, early_rims, late_rims):
+    def coarse_third(cells, half_planes, half_faces, half, early_rims, late_rims):
         return tuple(blank(thin_send, cell_shape, average_shape))
 
-    def fine_third(cells, half_planes, half_faces, early_rims, late_rims):
+    def fine_third(cells, half_planes, half_faces, half, early_rims, late_rims):
         send, adds = run(
             part(means_kernel, nb, edge, eager, parents_here),
             [thin_send, ghost_shape],
@@ -1055,8 +1060,8 @@
         out, averaged = run(
             part(finish_kernel, nb, edge, False, parents_here),
             [cell_shape, average_shape],
-            [table, cells, adds],
-            [ghost_shape, (nb, 5, 2, edge, LANES), (nb, 5, ROWS, LANES)],
+            [table, cells, adds, half],
+            [ghost_shape, (nb, 5, 2, edge, LANES), (nb, 5, ROWS, LANES), cell_shape],
             1,
             flops=work,
         )
@@ -1064,7 +1069,7 @@
 
     returned, out, averaged = lax.cond(
         level_id == 0, coarse_third, fine_third,
-        cells, half_planes, half_faces, early_rims, late_rims,
+        cells, half_planes, half_faces, half, early_rims, late_rims,
     )
     returned = level_shift(returned, 1)
     averaged = level_shift(averaged, 1)

time: 86.3 us -> 85.7 us (level)
  no operation moved by 1% of the time
where the time goes in v5:
time: 85.7 us; the launch traced here: 85.1 us
  Pallas kernels  32.5 us (38%)
  waiting for transfers between devices  25.3 us (30%)
  starting transfers between devices  24.7 us (29%)
  between operations  1.5 us (2%)
    pallas_call x6, Pallas kernels, run(): pl.pallas_call(kernel, out_shape=[jax.ShapeDtypeStruct(s, F32) for s in o...  31.1 us
    ppermute x4, waiting for transfers between devices, level_shift(): return lax.ppermute(array, 'level', [(source, 1 - source)])  20.1 us
    all_to_all x2, starting transfers between devices, route(): lax.all_to_all(buffer, 'blk', split_axis=0, concat_axis=0, tiled=True)  13 us
    ppermute x4, starting transfers between devices, level_shift(): return lax.ppermute(array, 'level', [(source, 1 - source)])  6.96 us
    all_to_all x2, waiting for transfers between devices, route(): lax.all_to_all(buffer, 'blk', split_axis=0, concat_axis=0, tiled=True)  5.09 us
    ppermute x1, starting transfers between devices, half_way_round(): return lax.ppermute(buffer, ('level', 'blk'), turned)  4.72 us
  transfers between devices with their start and end apart: 7, of which 5 were waited for; matrix products, arithmetic and copies ran while one was open for 0% of the time, Pallas kernels for 18%

profile of v5, /device:TPU:0, one launch (start us, length us, event | category | flops | bytes accessed | tf_op | source)
XLA Modules:
  0.0 85.1 jit_solution(17585607452400616327)
XLA Ops:
  0.0 1.4 %shard_map.39 = (s32[21,128]{1,0:T(8,128)S(1)}, s32[48,128]{1,0:T(8,128)S(1)}) custom-call(s32[1]{0:T(128)} %bitcast.6.blk_ref, s32[6,256]{1,0:T(8,128)} %bitcast.14, s32[2,256]{1,0:T(2,128)} %bitcast.15), custom_call_target="tpu_custom_call" | custom-call | tf_op jit(solution)/shard_map/pallas_call | solution.py:930
  1.4 0.5 fusion
  3.2 81.7 %conditional.9 = ((f32[1,16,5,16,256]{4,3,2,1,0:T(8,128)})) conditional(s32[]{:T(128)} %bitcast.9, (f32[16,5,16,256]{3,2,1,0:T(8,128)}, s32[21,128]{1,0:T(8,128)S(1)}, s32[48,128]{1,0:T(8,128)S(1)}) %tuple.103, (f32[16,5,16,256]{3,2,1,0:T(8,128)}, s32[21,128]{1,0:T(8,128)S(1)}, s32[48,128]{1,0:T(8,128)S(1)}) %tuple.104), branch_computations={%region_0.0_spmd, %region_9.0_spmd} | conditional | flops 648806400 | bytes 47270096 | solution.py:949
  3.4 36.0 %conditional.4 = (f32[16,5,16,256]{3,2,1,0:T(8,128)}, f32[6,5,64,128]{3,2,1,0:T(8,128)}, f32[6,5,32,128]{3,2,1,0:T(8,128)}, f32[16,20,2,128]{3,2,1,0:T(2,128)}, ...) conditional(s32[]{:T(128)} %convert_element_type.10, ...), branch_computations={%region_10.0_spmd, %region_11.0_spmd} | conditional | flops 216268800 | bytes 8859256 | solution.py:1014
  3.5 4.9 %branch_1_fun.28 = (f32[6,5,96,128]{3,2,1,0:T(8,128)S(1)}, f32[480,4,128]{2,1,0:T(4,128)}, f32[30,4,128]{2,1,0:T(4,128)S(1)}) custom-call(s32[21,128]{1,0:T(8,128)S(1)} %get-tuple-element.206.tab_ref, f32[16,5,16,256]{3,2,1,0:T(8,128)} %get-tuple-element.207.u_ref), custom_call_target="tpu_custom_call" | custom-call | bytes 1321472 | tf_op jit(solution)/shard_map/cond/branch_1_fun/cond/branch_1_fun/pallas_call | solution.py:891
  8.4 8.3 %all-to-all-start.3 = ((f32[16,30,4,128]{3,2,1,0:T(4,128)}), f32[16,30,4,128]{3,2,1,0:T(4,128)S(1)}, u32[]{:S(2)}, u32[]{:S(2)}) async-start(f32[16,30,4,128]{3,2,1,0:T(4,128)} %bitcast.3), calls=%async_computation.3 | async-start | bytes 1966080 | tf_op jit(solution)/shard_map/cond/branch_1_fun/cond/branch_1_fun/all_to_all | solution.py:917
  16.7 4.7 %collective-permute-start.4 = (f32[30,4,128]{2,1,0:T(4,128)S(1)}, f32[30,4,128]{2,1,0:T(4,128)S(1)}, u32[]{:S(2)}, u32[]{:S(2)}) collective-permute-start(f32[30,4,128]{2,1,0:T(4,128)S(1)} %get-tuple-element.212), channel_id=1, source_target_pairs={{0,8},{1,9},{2,10},{3,11},{4,12},{5,13},{6,14},{7,15},{8,0},{9,1},... | collective-permute-start | bytes 184328 | tf_op jit(solution)/shard_map/cond/branch_1_fun/cond/branch_1_fun/ppermute | solution.py:984
  21.5 11.7 %branch_1_fun.27 = (f32[16,5,16,256]{3,2,1,0:T(8,128)}, f32[6,5,32,128]{3,2,1,0:T(8,128)S(1)}) custom-call(s32[21,128]{1,0:T(8,128)S(1)} %get-tuple-element.206.tab_ref, f32[16,5,16,256]{3,2,1,0:T(8,128)} %get-tuple-element.207.u_ref), custom_call_target="tpu_custom_call" | custom-call | flops 216268800 | bytes 1321472 | tf_op jit(solution)/shard_map/cond/branch_1_fun/cond/branch_1_fun/pallas_call | solution.py:891
  33.1 0.1 collective-permute-done.4.refs_0_
  33.2 6.3 %branch_1_fun.29 = (f32[6,5,64,128]{3,2,1,0:T(8,128)}, f32[6,5,32,128]{3,2,1,0:T(8,128)}, f32[16,20,2,128]{3,2,1,0:T(2,128)}, f32[6,5,4,128]{3,2,1,0:T(4,128)S(1)}) custom-call(s32[21,128]{1,0:T(8,128)S(1)} %get-tuple-element.206.tab_ref, f32[6,5,96,128]{3,2,1,0:T(8,128)S(1)} %get-tuple-element.209.plane_ref, ...), custom_call_target="tpu_custom_call" | custom-call | bytes 3021312 | tf_op jit(solution)/shard_map/cond/branch_1_fun/cond/branch_1_fun/pallas_call | solution.py:891
  39.5 1.3 %collective-permute-start.5 = (f32[6,5,4,128]{3,2,1,0:T(4,128)S(1)}, f32[6,5,4,128]{3,2,1,0:T(4,128)S(1)}, u32[]{:S(2)}, u32[]{:S(2)}) collective-permute-start(f32[6,5,4,128]{3,2,1,0:T(4,128)S(1)} %get-tuple-element.256), channel_id=1, source_target_pairs={{0,16},{1,17},{2,18},{3,19},{4,20},{5,21},{6,22},{7,23},{8,24},{9,... | collective-permute-start | bytes 184328 | tf_op jit(solution)/shard_map/cond/branch_1_fun/ppermute | solution.py:913
  40.8 0.9 %collective-permute-done.5 = f32[6,5,4,128]{3,2,1,0:T(4,128)S(1)} collective-permute-done((f32[6,5,4,128]{3,2,1,0:T(4,128)S(1)}, f32[6,5,4,128]{3,2,1,0:T(4,128)S(1)}, u32[]{:S(2)}, u32[]{:S(2)}) %collective-permute-start.5) | collective-permute-done | bytes 61472 | tf_op jit(solution)/shard_map/cond/branch_1_fun/ppermute | solution.py:913
  41.6 14.4 %conditional.5 = (f32[6,5,4,128]{3,2,1,0:T(4,128)S(1)}, f32[16,5,16,256]{3,2,1,0:T(8,128)S(1)}, f32[6,5,96,128]{3,2,1,0:T(8,128)}, f32[6,5,32,128]{3,2,1,0:T(8,128)S(1)}, f32[16,5,16,256]{3,2,1,0:T(8,128)}) conditional(s32[]{:T(128)} %convert_element_type.10, (s32[21,128]{1,0:T(8,128)S(1)}, s32[48,128]{1,0:T(8,128)S(1)}, ...), branch_computations={%region_12.0_spmd, %region_13.0_spmd} | conditional | flops 216268800 | bytes 3615304 | solution.py:1043
  41.6 4.6 %all-to-all-start.4 = ((f32[16,20,2,128]{3,2,1,0:T(2,128)}), f32[16,20,2,128]{3,2,1,0:T(2,128)S(1)}, u32[]{:S(2)}, u32[]{:S(2)}) async-start(f32[16,20,2,128]{3,2,1,0:T(2,128)} %get-tuple-element.227), calls=%async_computation.4 | async-start | bytes 655360 | tf_op jit(solution)/shard_map/cond/branch_1_fun/cond/branch_1_fun/all_to_all | solution.py:917
  46.3 3.9 %branch_1_fun.32 = f32[16,5,16,256]{3,2,1,0:T(8,128)S(1)} custom-call(f32[16,5,16,256]{3,2,1,0:T(8,128)} %get-tuple-element.228.d_ref, f32[6,5,64,128]{3,2,1,0:T(8,128)} %get-tuple-element.229.add_ref), custom_call_target="tpu_custom_call" | custom-call | flops 54067200 | bytes 2293760 | tf_op jit(solution)/shard_map/cond/branch_1_fun/cond/branch_1_fun/pallas_call | solution.py:891
  50.2 5.1 %all-to-all-done.4.recv_ref = f32[16,20,2,128]{3,2,1,0:T(2,128)S(1)} async-done(((f32[16,20,2,128]{3,2,1,0:T(2,128)}), f32[16,20,2,128]{3,2,1,0:T(2,128)S(1)}, u32[]{:S(2)}, u32[]{:S(2)}) %all-to-all-start.4) | async-done | bytes 327712 | tf_op jit(solution)/shard_map/cond/branch_1_fun/cond/branch_1_fun/all_to_all | solution.py:917
  55.3 0.8 branch_1_fun.31
  56.1 3.1 %collective-permute-start.6 = (f32[6,5,4,128]{3,2,1,0:T(4,128)S(1)}, f32[6,5,4,128]{3,2,1,0:T(4,128)S(1)}, u32[]{:S(2)}, u32[]{:S(2)}) collective-permute-start(f32[6,5,4,128]{3,2,1,0:T(4,128)S(1)} %get-tuple-element.260), channel_id=1, source_target_pairs={{0,16},{1,17},{2,18},{3,19},{4,20},{5,21},{6,22},{7,23},{8,24},{9,... | collective-permute-start | bytes 184328 | tf_op jit(solution)/shard_map/cond/branch_1_fun/ppermute | solution.py:913
  59.2 0.9 %collective-permute-done.6 = f32[6,5,4,128]{3,2,1,0:T(4,128)S(1)} collective-permute-done((f32[6,5,4,128]{3,2,1,0:T(4,128)S(1)}, f32[6,5,4,128]{3,2,1,0:T(4,128)S(1)}, u32[]{:S(2)}, u32[]{:S(2)}) %collective-permute-start.6) | collective-permute-done | bytes 61472 | tf_op jit(solution)/shard_map/cond/branch_1_fun/ppermute | solution.py:913
  60.1 1.3 %collective-permute-start.7 = (f32[16,20,2,128]{3,2,1,0:T(2,128)S(1)}, f32[16,20,2,128]{3,2,1,0:T(2,128)S(1)}, u32[]{:S(2)}, u32[]{:S(2)}) collective-permute-start(f32[16,20,2,128]{3,2,1,0:T(2,128)S(1)} %get-tuple-element.266), channel_id=1, source_target_pairs={{16,0},{17,1},{18,2},{19,3},{20,4},{21,5},{22,6},{23,7},{24,8},{25... | collective-permute-start | bytes 983048 | tf_op jit(solution)/shard_map/cond/branch_1_fun/ppermute | solution.py:913
  61.4 1.3 %collective-permute-start.8 = (f32[2,5,16,256]{3,2,1,0:T(8,128)S(1)}, f32[2,5,16,256]{3,2,1,0:T(8,128)S(1)}, u32[]{:S(2)}, u32[]{:S(2)}) collective-permute-start(f32[2,5,16,256]{3,2,1,0:T(8,128)S(1)} %get-tuple-element.267), channel_id=1, source_target_pairs={{16,0},{17,1},{18,2},{19,3},{20,4},{21,5},{22,6},{23,7},{24,8},{25... | collective-permute-start | bytes 491528 | tf_op jit(solution)/shard_map/cond/branch_1_fun/ppermute | solution.py:913
  62.7 18.4 %collective-permute-done.8 = f32[2,5,16,256]{3,2,1,0:T(8,128)S(1)} collective-permute-done((f32[2,5,16,256]{3,2,1,0:T(8,128)S(1)}, f32[2,5,16,256]{3,2,1,0:T(8,128)S(1)}, u32[]{:S(2)}, u32[]{:S(2)}) %collective-permute-start.8) | collective-permute-done | bytes 163872 | tf_op jit(solution)/shard_map/cond/branch_1_fun/ppermute | solution.py:913
  81.1 3.6 %conditional.7 = (f32[1,16,5,16,256]{4,3,2,1,0:T(8,128)}) conditional(s32[]{:T(128)} %convert_element_type.10, f32[16,5,16,256]{3,2,1,0:T(8,128)} %get-tuple-element.264, (s32[21,128]{1,0:T(8,128)S(1)}, s32[48,128]{1,0:T(8,128)S(1)}, f32[16,5,16,256]{3,2,1,0:T(8,128)S(1)}, f32[6,5,32,128]{3,2,1,0:T(8,128)}, f32[16,20,2,128]{3,2,1,0:T(2,128)S(1)}, ...), branch_computations={%region_16.0_spmd, %region_17.0_spmd} | conditional | bytes 2329096 | solution.py:1089
  81.1 3.6 %branch_1_fun.35 = f32[16,5,16,256]{3,2,1,0:T(8,128)} custom-call(s32[21,128]{1,0:T(8,128)S(1)} %get-tuple-element.245.tab_ref, s32[48,128]{1,0:T(8,128)S(1)} %get-tuple-element.246.bits_ref, f32[16,5,16,256]{3,2,1,0:T(8,128)S(1)} %get-tuple-element.247.new_ref, f32[6,5,32,128]{3,2,1,0:T(8,128)} %get-tuple-element.248.face_ref, ...), custom_call_target="tpu_custom_call" | custom-call | bytes 2329088 | tf_op jit(solution)/shard_map/cond/branch_1_fun/cond/branch_1_fun/pallas_call | solution.py:891
  (6 shorter events, 0.0 us)
Async XLA Ops:
  8.4 24.8 %all-to-all-start.3 = ((f32[16,30,4,128]{3,2,1,0:T(4,128)}), f32[16,30,4,128]{3,2,1,0:T(4,128)S(1)}, u32[]{:S(2)}, u32[]{:S(2)}) async-start(f32[16,30,4,128]{3,2,1,0:T(4,128)} %bitcast.3), calls=%async_computation.3 | async-start | bytes 1966080 | tf_op jit(solution)/shard_map/cond/branch_1_fun/cond/branch_1_fun/all_to_all | solution.py:917
  16.7 16.5 %collective-permute-start.4 = (f32[30,4,128]{2,1,0:T(4,128)S(1)}, f32[30,4,128]{2,1,0:T(4,128)S(1)}, u32[]{:S(2)}, u32[]{:S(2)}) collective-permute-start(f32[30,4,128]{2,1,0:T(4,128)S(1)} %get-tuple-element.212), channel_id=1, source_target_pairs={{0,8},{1,9},{2,10},{3,11},{4,12},{5,13},{6,14},{7,15},{8,0},{9,1},... | collective-permute-start | bytes 184328 | tf_op jit(solution)/shard_map/cond/branch_1_fun/cond/branch_1_fun/ppermute | solution.py:984
  39.5 2.2 %collective-permute-start.5 = (f32[6,5,4,128]{3,2,1,0:T(4,128)S(1)}, f32[6,5,4,128]{3,2,1,0:T(4,128)S(1)}, u32[]{:S(2)}, u32[]{:S(2)}) collective-permute-start(f32[6,5,4,128]{3,2,1,0:T(4,128)S(1)} %get-tuple-element.256), channel_id=1, source_target_pairs={{0,16},{1,17},{2,18},{3,19},{4,20},{5,21},{6,22},{7,23},{8,24},{9,... | collective-permute-start | bytes 184328 | tf_op jit(solution)/shard_map/cond/branch_1_fun/ppermute | solution.py:913
  41.6 13.6 %all-to-all-start.4 = ((f32[16,20,2,128]{3,2,1,0:T(2,128)}), f32[16,20,2,128]{3,2,1,0:T(2,128)S(1)}, u32[]{:S(2)}, u32[]{:S(2)}) async-start(f32[16,20,2,128]{3,2,1,0:T(2,128)} %get-tuple-element.227), calls=%async_computation.4 | async-start | bytes 655360 | tf_op jit(solution)/shard_map/cond/branch_1_fun/cond/branch_1_fun/all_to_all | solution.py:917
  56.1 4.0 %collective-permute-start.6 = (f32[6,5,4,128]{3,2,1,0:T(4,128)S(1)}, f32[6,5,4,128]{3,2,1,0:T(4,128)S(1)}, u32[]{:S(2)}, u32[]{:S(2)}) collective-permute-start(f32[6,5,4,128]{3,2,1,0:T(4,128)S(1)} %get-tuple-element.260), channel_id=1, source_target_pairs={{0,16},{1,17},{2,18},{3,19},{4,20},{5,21},{6,22},{7,23},{8,24},{9,... | collective-permute-start | bytes 184328 | tf_op jit(solution)/shard_map/cond/branch_1_fun/ppermute | solution.py:913
  60.1 21.0 %collective-permute-start.7 = (f32[16,20,2,128]{3,2,1,0:T(2,128)S(1)}, f32[16,20,2,128]{3,2,1,0:T(2,128)S(1)}, u32[]{:S(2)}, u32[]{:S(2)}) collective-permute-start(f32[16,20,2,128]{3,2,1,0:T(2,128)S(1)} %get-tuple-element.266), channel_id=1, source_target_pairs={{16,0},{17,1},{18,2},{19,3},{20,4},{21,5},{22,6},{23,7},{24,8},{25... | collective-permute-start | bytes 983048 | tf_op jit(solution)/shard_map/cond/branch_1_fun/ppermute | solution.py:913
  61.4 19.7 %collective-permute-start.8 = (f32[2,5,16,256]{3,2,1,0:T(8,128)S(1)}, f32[2,5,16,256]{3,2,1,0:T(8,128)S(1)}, u32[]{:S(2)}, u32[]{:S(2)}) collective-permute-start(f32[2,5,16,256]{3,2,1,0:T(8,128)S(1)} %get-tuple-element.267), channel_id=1, source_target_pairs={{16,0},{17,1},{18,2},{19,3},{20,4},{21,5},{22,6},{23,7},{24,8},{25... | collective-permute-start | bytes 491528 | tf_op jit(solution)/shard_map/cond/branch_1_fun/ppermute | solution.py:913
